TPU v7x, 128 devices: a whole 4x4x4 slice. The times are simulated.
128 devices in a mesh: rep: 4 (over z), gx: 8 (over y, core), gy: 4 (over x).
Axes of the slice: x: 4, y: 4, z: 4, core: 2. Of those that a mesh axis runs over, the one named last changes fastest.
Arguments:
- micro_fields: bfloat16 [4, 4, 32, 64, 128], P('rep', None, 'gx', 'gy'), may hold values from -6 to 6
- lift_w: bfloat16 [4, 32], replicated, may hold values from -3 to 3
- conv_w: bfloat16 [1, 32, 864], replicated, may hold values from -0.21875 to 0.21875
- mix_w: bfloat16 [1, 32, 32], replicated, may hold values from -1 to 1
- phi: bfloat16 [256, 32, 64, 128], P(None, 'gx', 'gy'), may hold values from -6 to 6
- psi: bfloat16 [256, 32, 64, 128], P(None, 'gx', 'gy'), may hold values from -6 to 6
- cotangent: bfloat16 [4, 32, 32, 64, 128], P('rep', None, 'gx', 'gy'), may hold values from -6 to 6
Outputs:
- out_field: float32 [4, 32, 32, 64, 128], P('rep', None, 'gx', 'gy')
- conv_grad: float32 [1, 32, 864], P(None, 'rep')
- mix_grad: float32 [1, 32, 32], P(None, 'rep')
- lift_grad: float32 [4, 32], P(None, 'rep')
All inputs are finite; a program needn't handle non-finite values.
Results may differ from a plain program's by a relative error of at most 0.0065.
Values may be sent and summed in bfloat16 or wider, within the bound.
No kernel may reach another device: no remote copies, remote signals or barrier semaphores. Data moves between devices by JAX's collectives and lax.ppermute only.
A program may use at most 128 MiB of HBM per device.

v0:
```python
import math

import jax
import jax.numpy as jnp
from jax import lax
from jax.sharding import PartitionSpec as P

TAP_OFFSETS = [(a - 1, b - 1, c - 1) for a in range(3) for b in range(3) for c in range(3)]


def with_halo(block, sides, width):
    for axis, dim in sides:
        count = lax.axis_size(axis)
        forward = [(i, i + 1) for i in range(count - 1)]
        backward = [(target, source) for source, target in forward]
        low = lax.ppermute(
            lax.slice_in_dim(block, block.shape[dim] - width, None, axis=dim), axis, forward
        )
        high = lax.ppermute(lax.slice_in_dim(block, 0, width, axis=dim), axis, backward)
        block = jnp.concatenate([low, block, high], axis=dim)
    return block


def gelu_value(values):
    return 0.5 * values * (1.0 + jax.scipy.special.erf(values / math.sqrt(2.0)))


def gelu_slope(values):
    cumulative = 0.5 * (1.0 + jax.scipy.special.erf(values / math.sqrt(2.0)))
    return cumulative + values * jnp.exp(-0.5 * values * values) / math.sqrt(2.0 * math.pi)


def tap_stack(padded, rows_x, rows_y, depth):
    padded_z = jnp.pad(padded, ((0, 0), (0, 0), (0, 0), (1, 1)))
    channels = padded.shape[0]
    pieces = [
        padded_z[
            :,
            1 + shift_x : 1 + shift_x + rows_x,
            1 + shift_y : 1 + shift_y + rows_y,
            1 + shift_z : 1 + shift_z + depth,
        ].reshape(channels, rows_x * rows_y * depth)
        for shift_x, shift_y, shift_z in TAP_OFFSETS
    ]
    return jnp.concatenate(pieces, axis=0)


def on_device(micro_fields, lift_w, conv_w, mix_w, phi, psi, cotangent):
    inputs_block = micro_fields[0]
    in_width, rows_x, rows_y, depth = inputs_block.shape
    channels = lift_w.shape[1]
    basis_count = phi.shape[0]
    cell_count = rows_x * rows_y * depth
    total_cells = cell_count * lax.axis_size("gx") * lax.axis_size("gy")
    inv_cells = 1.0 / math.sqrt(total_cells)
    inv_rank = 1.0 / math.sqrt(basis_count)
    lift_t = lift_w.T
    inputs_flat = inputs_block.reshape(in_width, cell_count)
    shape_rest = inputs_block.shape[1:]
    flat = inputs_block.reshape(in_width, -1)
    lifted = jnp.dot(lift_t, flat, preferred_element_type=jnp.float32).astype(jnp.bfloat16)
    current = lifted.reshape((channels,) + shape_rest)
    first_pad = with_halo(current, (("gx", 1), ("gy", 2)), 1)
    phi_flat = phi.reshape(basis_count, cell_count)
    psi_flat = psi.reshape(basis_count, cell_count)
    stacked = tap_stack(first_pad, rows_x, rows_y, depth)
    conv_sum = jnp.dot(conv_w[0], stacked, preferred_element_type=jnp.float32)
    partial_value = lax.dot_general(
        phi_flat,
        current.reshape(channels, cell_count),
        (((1,), (1,)), ((), ())),
        preferred_element_type=jnp.float32,
    )
    coefficients = lax.psum(partial_value, ("gx", "gy")) * inv_cells
    mixed_coef = jnp.dot(
        coefficients, mix_w[0].astype(jnp.float32), precision=lax.Precision.HIGHEST
    ).astype(jnp.bfloat16)
    kernel_term = (
        lax.dot_general(
            mixed_coef, psi_flat, (((0,), (0,)), ((), ())), preferred_element_type=jnp.float32
        )
        * inv_rank
    )
    preact = conv_sum + kernel_term
    out_block = gelu_value(preact).reshape(channels, rows_x, rows_y, depth)[None]
    grad_field = cotangent[0].reshape(channels, cell_count)
    grad_pre = (grad_field.astype(jnp.float32) * gelu_slope(preact)).astype(jnp.bfloat16)
    conv_local = lax.dot_general(
        grad_pre, stacked, (((1,), (1,)), ((), ())), preferred_element_type=jnp.float32
    )
    mixed_part = (
        lax.dot_general(
            psi_flat, grad_pre, (((1,), (1,)), ((), ())), preferred_element_type=jnp.float32
        )
        * inv_rank
    )
    mix_local = jnp.dot(coefficients.T, mixed_part, precision=lax.Precision.HIGHEST)
    grad_mixed = lax.psum(mixed_part, ("gx", "gy"))
    grad_coef = jnp.dot(
        grad_mixed, mix_w[0].astype(jnp.float32).T, precision=lax.Precision.HIGHEST
    ).astype(jnp.bfloat16)
    grid_grad = grad_pre.reshape(channels, rows_x, rows_y, depth)
    grad_padded = with_halo(grid_grad, (("gx", 1), ("gy", 2)), 1)
    back_stack = tap_stack(grad_padded, rows_x, rows_y, depth)
    flipped = (
        conv_w[0]
        .reshape(channels, 27, channels)[:, ::-1, :]
        .transpose(2, 1, 0)
        .reshape(channels, 27 * channels)
    )
    kernel_back = (
        lax.dot_general(
            grad_coef, phi_flat, (((0,), (0,)), ((), ())), preferred_element_type=jnp.float32
        )
        * inv_cells
    )
    first_grad = jnp.dot(flipped, back_stack, preferred_element_type=jnp.float32) + kernel_back
    lift_part = lax.dot_general(
        inputs_flat.astype(jnp.float32),
        first_grad,
        (((1,), (1,)), ((), ())),
        precision=lax.Precision.HIGHEST,
    )
    grad_terms = (conv_local[None], mix_local[None], lift_part)
    summed = lax.psum((grad_terms[0], grad_terms[1], grad_terms[2]), ("gx", "gy"))
    owned_sums = (
        lax.psum_scatter(summed[0], "rep", scatter_dimension=1, tiled=True),
        lax.psum_scatter(summed[1], "rep", scatter_dimension=1, tiled=True),
        lax.psum_scatter(summed[2], "rep", scatter_dimension=1, tiled=True),
    )
    grad_scale = 1.0 / math.sqrt(total_cells * lax.axis_size("rep"))
    return (
        out_block,
        owned_sums[0] * grad_scale,
        owned_sums[1] * grad_scale,
        owned_sums[2] * grad_scale,
    )


def solution(mesh):
    return jax.shard_map(
        on_device,
        mesh=mesh,
        in_specs=(
            P("rep", None, "gx", "gy", None),
            P(),
            P(),
            P(),
            P(None, "gx", "gy", None),
            P(None, "gx", "gy", None),
            P("rep", None, "gx", "gy", None),
        ),
        out_specs=(
            P("rep", None, "gx", "gy", None),
            P(None, "rep", None),
            P(None, "rep", None),
            P(None, "rep"),
        ),
        check_vma=False,
    )
```

profile of v0, /device:TPU:1, one launch (start us, length us, event | category | flops | bytes accessed | tf_op | source)
XLA Modules:
  0.0 544.4 jit_solution(13477298538471707748)
XLA Ops:
  7.2 0.9 reshape_squeeze.8
  8.1 1.0 convolution_convert_fusion
  9.3 3.3 collective-permute-start.1
  12.6 3.2 collective-permute-start
  15.8 4.6 fusion.14
  20.4 122.3 %psum.35 = f32[256,32]{0,1:T(8,128)S(1)} all-reduce(f32[256,32]{0,1:T(8,128)S(1)} %fusion.14), channel_id=1, replica_groups=mesh['rep'=4,'gx'=8,'gy'=4] {'gx','gy'}, use_global_device_ids=true, to_apply=%region_0.1 | all-reduce | flops 8192 | bytes 65536 | tf_op jit(solution)/shard_map/psum | solution.py:74
  143.0 0.8 fusion.46
  143.9 1.9 collective-permute-start.2
  145.8 1.3 collective-permute-start.3
  147.3 1.0 reshape_squeeze.9
  148.6 0.6 copy.12
  149.4 1.3 reshape.242
  150.6 1.2 dynamic-slice
  152.5 3.1 select_maximum_fusion.2
  155.6 3.7 fusion.44
  159.6 2.5 pad_maximum_fusion.4
  162.1 0.3 bitcast_dynamic-update-slice_fusion.50
  162.5 0.3 bitcast_dynamic-update-slice_fusion.49
  162.8 0.3 bitcast_dynamic-update-slice_fusion.48
  163.1 0.3 bitcast_dynamic-update-slice_fusion.47
  163.4 0.3 bitcast_dynamic-update-slice_fusion.46
  163.7 0.3 bitcast_dynamic-update-slice_fusion.45
  164.1 0.3 bitcast_dynamic-update-slice_fusion.44
  164.4 0.3 bitcast_dynamic-update-slice_fusion.43
  164.7 0.3 bitcast_dynamic-update-slice_fusion.42
  165.0 0.3 bitcast_dynamic-update-slice_fusion.41
  165.3 0.3 bitcast_dynamic-update-slice_fusion.40
  165.6 0.3 bitcast_dynamic-update-slice_fusion.39
  166.0 0.3 bitcast_dynamic-update-slice_fusion.38
  166.3 0.3 bitcast_dynamic-update-slice_fusion.37
  166.6 0.3 bitcast_dynamic-update-slice_fusion.36
  167.0 0.3 bitcast_dynamic-update-slice_fusion.35
  167.3 0.3 bitcast_dynamic-update-slice_fusion.34
  167.9 0.3 bitcast_dynamic-update-slice_fusion.32
  168.2 0.3 bitcast_dynamic-update-slice_fusion.31
  168.6 0.3 bitcast_dynamic-update-slice_fusion.30
  168.9 0.3 bitcast_dynamic-update-slice_fusion.29
  169.2 0.3 bitcast_dynamic-update-slice_fusion.28
  169.5 0.3 bitcast_dynamic-update-slice_fusion.27
  169.8 0.3 bitcast_dynamic-update-slice_fusion.26
  170.2 5.0 copy-done.1
  175.2 2.9 convolution_bitcast_fusion.1
  178.2 9.2 %fusion.25 = (bf16[32,8192]{1,0:T(8,128)(2,1)S(1)}, f32[4,8,64,128]{3,1,2,0:T(8,128)S(1)}) fusion(f32[32,8192]{1,0:T(8,128)S(1)} %reshape.242, f32[32,8192]{1,0:T(8,128)S(1)} %convolution_bitcast_fusion.1, bf16[256,32]{0,1:T(8,128)(2,1)S(1)} %convolution_convert_fusion.2, bf16[32,8,64,128]{3,2,1,0:T(8,128)(2,1)S(1)} %bitcast.291), kind=kOutput, calls=%fused_computation.54 | convolution fusion | flops 137887744 | bytes 7880704 | tf_op jit(solution)/shard_map/dot_general | solution.py:79
  187.4 9.8 %convolution_bitcast_fusion.2 = f32[1,32,864]{2,1,0:T(8,128)} fusion(bf16[32,8192]{1,0:T(8,128)(2,1)S(1)} %get-tuple-element.45, bf16[864,8192]{1,0:T(8,128)(2,1)} %copy-done.1), kind=kOutput, calls=%fused_computation.42 | convolution fusion | flops 452984832 | bytes 14790656 | tf_op jit(solution)/shard_map/dot_general | solution.py:88
  197.2 4.6 fusion.17
  201.8 126.4 %psum.38 = f32[256,32]{0,1:T(8,128)S(1)} all-reduce(f32[256,32]{0,1:T(8,128)S(1)} %bitcast.350), channel_id=1, replica_groups=mesh['rep'=4,'gx'=8,'gy'=4] {'gx','gy'}, use_global_device_ids=true, to_apply=%region_5.6 | all-reduce | flops 8192 | bytes 65536 | tf_op jit(solution)/shard_map/psum | solution.py:98
  328.4 1.9 collective-permute-start.4
  330.4 6.3 %collective-permute-start.5 = (bf16[32,1,16,128]{3,2,1,0:T(8,128)(2,1)S(1)}, bf16[32,1,16,128]{3,2,1,0:T(8,128)(2,1)S(1)}, u32[]{:S(2)}, u32[]{:S(2)}) collective-permute-start(bf16[32,1,16,128]{3,2,1,0:T(8,128)(2,1)S(1)} %get-tuple-element.72), channel_id=1, source_target_pairs={{4,0},{8,4},{12,8},{16,12},{20,16},{24,20},{28,24},{5,1},{9,5},{13... | collective-permute-start | bytes 393224 | tf_op jit(solution)/shard_map/ppermute | solution.py:19
  336.9 1.2 copy.48
  338.6 1.3 collective-permute-start.6
  339.9 1.3 collective-permute-start.7
  341.2 32.5 %all-reduce.9.cloned.1.call-done = f32[1,32,864]{2,1,0:T(8,128)} async-done(((f32[1,32,864]{2,1,0:T(8,128)}), f32[1,32,864]{2,1,0:T(8,128)}) %all-reduce.9.cloned.1.call-update) | async-done | bytes 110608
  373.6 0.8 constant_dynamic-slice_fusion.2
  374.4 2.3 select_maximum_fusion
  376.7 3.7 fusion.43
  380.7 1.5 pad_maximum_fusion
  390.2 2.7 convolution_bitcast_fusion
  392.9 2.5 fusion
  395.4 0.6 convolution_bitcast_fusion.4
  396.0 12.8 %all-reduce.6 = (f32[1,32,32]{2,1,0:T(8,128)S(1)}, f32[4,32]{1,0:T(4,128)S(1)}) all-reduce(f32[1,32,32]{2,1,0:T(8,128)S(1)} %convolution_bitcast_fusion.3, f32[4,32]{1,0:T(4,128)S(1)} %convolution_bitcast_fusion.4), channel_id=3, replica_groups=mesh['rep'=4,'gx'=8,'gy'=4] {'rep'}, use_global_device_ids=true, to_apply=%region_4.5.clone | all-reduce | flops 1152 | bytes 9216
  408.9 126.6 %all-reduce.5 = (f32[1,8,864]{2,1,0:T(8,128)S(1)}, f32[1,8,32]{2,1,0:T(8,128)S(1)}, f32[4,8]{1,0:T(4,128)S(1)}) all-reduce(f32[1,8,864]{2,1,0:T(8,128)S(1)} %constant_dynamic-slice_fusion.2, f32[1,8,32]{2,1,0:T(8,128)S(1)} %constant_dynamic-slice_fusion.1, ...), channel_id=1, replica_groups=mesh['rep'=4,'gx'=8,'gy'=4] {'gx','gy'}, use_global_device_ids=true, to_apply=%region_1.2 | all-reduce | flops 7200 | bytes 57600 | tf_op jit(solution)/shard_map/psum | solution.py:125
  535.5 0.6 broadcast_multiply_fusion
  536.1 0.6 broadcast_multiply_fusion.2
  536.7 0.6 broadcast_multiply_fusion.1
  (71 shorter events, 10.9 us)
Async XLA Ops:
  7.2 139.9 %copy-start = (bf16[1,32,32]{2,1,0:T(8,128)(2,1)S(1)}, bf16[1,32,32]{2,1,0:T(8,128)(2,1)}, u32[]{:S(2)}) copy-start(bf16[1,32,32]{2,1,0:T(8,128)(2,1)} %param.10) | copy-start | bytes 6148
  7.2 366.5 %all-reduce.9.cloned.1.call-start = ((), (), s32[]{:S(2)}) async-start(), calls=%async_computation | async-start | bytes 229376
  9.3 133.5 %collective-permute-start.1 = (bf16[32,1,16,128]{3,2,1,0:T(8,128)(2,1)S(1)}, bf16[32,1,16,128]{3,2,1,0:T(8,128)(2,1)S(1)}, u32[]{:S(2)}, u32[]{:S(2)}) collective-permute-start(bf16[32,1,16,128]{3,2,1,0:T(8,128)(2,1)S(1)} %get-tuple-element.77), channel_id=1, source_target_pairs={{4,0},{8,4},{12,8},{16,12},{20,16},{24,20},{28,24},{5,1},{9,5},{13... | collective-permute-start | bytes 393224 | tf_op jit(solution)/shard_map/ppermute | solution.py:19
  12.6 130.1 %collective-permute-start = (bf16[32,1,16,128]{3,2,1,0:T(8,128)(2,1)S(1)}, bf16[32,1,16,128]{3,2,1,0:T(8,128)(2,1)S(1)}, u32[]{:S(2)}, u32[]{:S(2)}) collective-permute-start(bf16[32,1,16,128]{3,2,1,0:T(8,128)(2,1)S(1)} %get-tuple-element.78), channel_id=1, source_target_pairs={{0,4},{4,8},{8,12},{12,16},{16,20},{20,24},{24,28},{1,5},{5,9},{9,... | collective-permute-start | bytes 393224 | tf_op jit(solution)/shard_map/ppermute | solution.py:16
  142.7 6.4 %copy-start.5 = (f32[256,32]{0,1:T(8,128)}, f32[256,32]{0,1:T(8,128)S(1)}, u32[]{:S(2)}) copy-start(f32[256,32]{0,1:T(8,128)S(1)} %psum.35) | copy-start | bytes 98308
  143.9 8.7 %collective-permute-start.2 = (bf16[32,6,1,128]{3,2,1,0:T(2,128)(2,1)}, bf16[32,6,1,128]{3,2,1,0:T(2,128)(2,1)}, u32[]{:S(2)}, u32[]{:S(2)}) collective-permute-start(bf16[32,6,1,128]{3,2,1,0:T(2,128)(2,1)} %get-tuple-element.67), channel_id=1, source_target_pairs={{0,1},{1,2},{2,3},{4,5},{5,6},{6,7},{8,9},{9,10},{10,11},{12,13},{... | collective-permute-start | bytes 147464 | tf_op jit(solution)/shard_map/ppermute | solution.py:16
  145.8 6.7 %collective-permute-start.3 = (bf16[32,6,1,128]{3,2,1,0:T(2,128)(2,1)}, bf16[32,6,1,128]{3,2,1,0:T(2,128)(2,1)}, u32[]{:S(2)}, u32[]{:S(2)}) collective-permute-start(bf16[32,6,1,128]{3,2,1,0:T(2,128)(2,1)} %get-tuple-element.68), channel_id=1, source_target_pairs={{1,0},{2,1},{3,2},{5,4},{6,5},{7,6},{9,8},{10,9},{11,10},{13,12},{... | collective-permute-start | bytes 147464 | tf_op jit(solution)/shard_map/ppermute | solution.py:19
  162.1 13.1 %copy-start.4 = (bf16[1,32,864]{2,1,0:T(8,128)(2,1)S(1)}, bf16[1,32,864]{2,1,0:T(8,128)(2,1)}, u32[]{:S(2)}) copy-start(bf16[1,32,864]{2,1,0:T(8,128)(2,1)} %param.9) | copy-start | bytes 165892
  167.0 11.2 %copy-start.3 = (bf16[256,4,16,128]{3,2,1,0:T(8,128)(2,1)S(1)}, bf16[256,4,16,128]{3,2,1,0:T(8,128)(2,1)}, u32[]{:S(2)}) copy-start(bf16[256,4,16,128]{3,2,1,0:T(8,128)(2,1)} %param.12) | copy-start | bytes 12582916
  170.2 5.1 copy-start.1
  178.1 158.6 %copy-start.6 = (f32[256,32]{0,1:T(8,128)S(1)}, f32[256,32]{0,1:T(8,128)}, u32[]{:S(2)}) copy-start(f32[256,32]{0,1:T(8,128)} %copy-done.5) | copy-start | bytes 98308
  328.4 9.7 %collective-permute-start.4 = (bf16[32,1,16,128]{3,2,1,0:T(8,128)(2,1)S(1)}, bf16[32,1,16,128]{3,2,1,0:T(8,128)(2,1)S(1)}, u32[]{:S(2)}, u32[]{:S(2)}) collective-permute-start(bf16[32,1,16,128]{3,2,1,0:T(8,128)(2,1)S(1)} %get-tuple-element.73), channel_id=1, source_target_pairs={{0,4},{4,8},{8,12},{12,16},{16,20},{20,24},{24,28},{1,5},{5,9},{9,... | collective-permute-start | bytes 393224 | tf_op jit(solution)/shard_map/ppermute | solution.py:16
  330.4 7.7 %collective-permute-start.5 = (bf16[32,1,16,128]{3,2,1,0:T(8,128)(2,1)S(1)}, bf16[32,1,16,128]{3,2,1,0:T(8,128)(2,1)S(1)}, u32[]{:S(2)}, u32[]{:S(2)}) collective-permute-start(bf16[32,1,16,128]{3,2,1,0:T(8,128)(2,1)S(1)} %get-tuple-element.72), channel_id=1, source_target_pairs={{4,0},{8,4},{12,8},{16,12},{20,16},{24,20},{28,24},{5,1},{9,5},{13... | collective-permute-start | bytes 393224 | tf_op jit(solution)/shard_map/ppermute | solution.py:19
  338.6 35.8 %collective-permute-start.6 = (bf16[32,6,1,128]{3,2,1,0:T(2,128)(2,1)S(1)}, bf16[32,6,1,128]{3,2,1,0:T(2,128)(2,1)S(1)}, u32[]{:S(2)}, u32[]{:S(2)}) collective-permute-start(bf16[32,6,1,128]{3,2,1,0:T(2,128)(2,1)S(1)} %get-tuple-element.62), channel_id=1, source_target_pairs={{0,1},{1,2},{2,3},{4,5},{5,6},{6,7},{8,9},{9,10},{10,11},{12,13},{... | collective-permute-start | bytes 147464 | tf_op jit(solution)/shard_map/ppermute | solution.py:16
  339.9 34.5 %collective-permute-start.7 = (bf16[32,6,1,128]{3,2,1,0:T(2,128)(2,1)S(1)}, bf16[32,6,1,128]{3,2,1,0:T(2,128)(2,1)S(1)}, u32[]{:S(2)}, u32[]{:S(2)}) collective-permute-start(bf16[32,6,1,128]{3,2,1,0:T(2,128)(2,1)S(1)} %get-tuple-element.63), channel_id=1, source_target_pairs={{1,0},{2,1},{3,2},{5,4},{6,5},{7,6},{9,8},{10,9},{11,10},{13,12},{... | collective-permute-start | bytes 147464 | tf_op jit(solution)/shard_map/ppermute | solution.py:19
  387.0 5.9 %copy-start.2 = (bf16[256,4,16,128]{3,2,1,0:T(8,128)(2,1)S(1)}, bf16[256,4,16,128]{3,2,1,0:T(8,128)(2,1)}, u32[]{:S(2)}) copy-start(bf16[256,4,16,128]{3,2,1,0:T(8,128)(2,1)} %param.11) | copy-start | bytes 12582916
Sparse Core Ops, SparseCore 0:
  338.2 35.3 all-reduce.8
where the time goes:
time: 555 us; the launch traced here: 544 us
  blocking collectives  388 us (70%)
  matrix products  38.5 us (7%)
  local copies, waits for them, and re-layouts  37.4 us (7%)
  waiting for transfers between devices  32.5 us (6%)
  starting transfers between devices  20.5 us (4%)
  between operations  15.7 us (3%)
  other arithmetic  11.6 us (2%)
    psum x1, blocking collectives, on_device(): lax.psum((grad_terms[0], grad_terms[1], grad_terms[2]), ('gx', 'gy'))  127 us
    psum x1, blocking collectives, on_device(): grad_mixed = lax.psum(mixed_part, ('gx', 'gy'))  126 us
    psum x1, blocking collectives, on_device(): coefficients = lax.psum(partial_value, ('gx', 'gy')) * inv_cells  122 us
    unnamed x2, waiting for transfers between devices  32.5 us
    unnamed x75, local copies, waits for them, and re-layouts  24.2 us
    unnamed x1, blocking collectives  12.8 us
    ppermute x4, starting transfers between devices, with_halo(): lax.ppermute(lax.slice_in_dim(block, 0, width, axis=dim), axis, backward)  12.2 us
  transfers between devices with their start and end apart: 9, of which 1 were waited for; matrix products, arithmetic and copies ran while one was open for 2% of the time, Pallas kernels for 0%

commit v1 on v0

v1 whole, which is shorter than its diff:
```python
import functools
import math

import jax
import jax.numpy as jnp
import numpy as np
from jax import lax
from jax.experimental import pallas as pl
from jax.experimental.pallas import tpu as pltpu
from jax.sharding import PartitionSpec as P

F32 = jnp.float32
BF16 = jnp.bfloat16
NN = (((1,), (0,)), ((), ()))
NT = (((1,), (1,)), ((), ()))
TN = (((0,), (0,)), ((), ()))

STACK = 768
HALO_AT = 576
U_AT = 704
TAPROWS = 112


def stack_codes():
    codes = np.full((8, STACK), -1, np.int32)
    codes[3] = -100
    for lane in range(STACK):
        if lane < HALO_AT:
            group, row = divmod(lane, 16)
            dx, dz, j = group // 12, group // 4 % 3, group % 4
        elif lane < HALO_AT + 72:
            at = lane - HALO_AT
            dx, dz, side, j = at // 24, at // 8 % 3, at // 4 % 2, at % 4
            row = 16 if side else -1
        elif lane >= U_AT:
            j, row = divmod(lane - U_AT, 16)
            codes[1, lane] = 108 + j
            codes[3, lane] = row
            continue
        else:
            continue
        for dy in range(3):
            codes[dy, lane] = (9 * dx + 3 * dy + dz) * 4 + j
        codes[3, lane] = row
    return codes


def dot(a, b, dims=NN):
    return lax.dot_general(a, b, dims, preferred_element_type=F32)


def split(values):
    high = values.astype(BF16)
    return high, (values - high.astype(F32)).astype(BF16)


def dot_split(a, b, dims=NN):
    high, low = split(a)
    return dot(high, b, dims) + dot(low, b, dims)


def iota(shape, dim):
    return lax.broadcasted_iota(jnp.int32, shape, dim)


def ones_where(condition):
    return jnp.where(condition, 1.0, 0.0).astype(BF16)


def selector(codes, dy):
    return ones_where(iota((TAPROWS, STACK), 0) == codes[dy : dy + 1, :])


def band(codes, dy):
    return (codes[3:4, :] - iota((16, STACK), 0)) == dy - 1


def lift_columns(lift, first):
    rows = iota((4, 128), 0)
    lanes = iota((4, 128), 1)
    if first is None:
        pick = ((lanes & 3) == rows) & (lanes < 108)
    else:
        pick = (lanes - first) == rows
    return dot(lift, ones_where(pick), TN)


def lift_blocks(lift):
    columns = lift_columns(lift, None)
    own = iota((27, 1, 128), 0) == (iota((27, 1, 128), 2) >> 2)
    return jnp.where(own, columns[None], 0.0).reshape(864, 128).astype(BF16)


def weights_kernel(inv, lift_ref, conv_ref, mix_ref, codes_ref, table_ref):
    lift = lift_ref[...]
    codes = codes_ref[...]
    taps = dot(conv_ref[0], lift_blocks(lift))
    mixed = dot(mix_ref[0], lift_columns(lift, 108).astype(BF16), TN) * inv
    weights = (taps + mixed).astype(BF16)[:, :TAPROWS]
    table = jnp.zeros((32, 16, STACK), F32)
    for dy in range(3):
        spread = dot(weights, selector(codes, dy))
        table = jnp.where(band(codes, dy)[None], spread[:, None, :], table)
    table_ref[...] = table.reshape(512, STACK).astype(BF16)


def project_kernel(steps, micro_ref, phi_ref, out_ref, sums):
    step = pl.program_id(0)
    rows = phi_ref.shape[0]
    wide = rows * 16
    fields = jnp.concatenate([micro_ref[:, x].reshape(64, 128) for x in range(4)], axis=1)
    basis = jnp.concatenate([phi_ref[:, x].reshape(wide, 128) for x in range(4)], axis=1)
    product = dot(fields, basis, NT)
    same = iota((16, wide), 0) == (iota((16, wide), 1) & 15)
    chunks = rows // 8
    for j in range(4):
        line = jnp.sum(jnp.where(same, product[16 * j : 16 * j + 16], 0.0), axis=0, keepdims=True)
        for chunk in range(chunks):
            sums[j, pl.ds(step * chunks + chunk, 1), :] = line[:, 128 * chunk : 128 * chunk + 128]

    @pl.when(step == steps - 1)
    def _():
        groups = jnp.where(iota((8, 128), 0) == (iota((8, 128), 1) >> 4), 1.0, 0.0)
        total = lax.dot_general(
            groups,
            sums[...].reshape(128, 128),
            NT,
            preferred_element_type=F32,
            precision=lax.Precision.HIGHEST,
        )
        out_ref[...] = jnp.broadcast_to(total[None], out_ref.shape)


def shift_z(values, dz):
    if dz == 0:
        return values
    lanes = iota(values.shape, 1) & 127
    width = values.shape[1]
    pieces = [
        pltpu.roll(values[:, at : at + 128], (-dz) % 128, 1) for at in range(0, width, 128)
    ]
    rolled = jnp.concatenate(pieces, axis=1)
    return jnp.where(lanes == (127 if dz > 0 else 0), 0.0, rolled)


def edge_kernel(micro_ref, low_ref, high_ref, first_ref, last_ref):
    for x in range(6):
        block = (low_ref[...] if x == 0 else high_ref[...] if x == 5 else micro_ref[:, x - 1]).astype(F32)
        first_ref[:, 128 * x : 128 * x + 128] = block[:, 0, :]
        last_ref[:, 128 * x : 128 * x + 128] = block[:, 15, :]


def main_kernel(
    inv,
    parts_ref,
    micro_ref,
    xlow_ref,
    xhigh_ref,
    ylow_ref,
    yhigh_ref,
    table_ref,
    psi_ref,
    cot_ref,
    lift_ref,
    conv_ref,
    mix_ref,
    codes_ref,
    out_ref,
    send_ref,
    stack,
    spread,
    pre,
    grad,
    corr,
):
    codes = codes_ref[...]
    planes = [xlow_ref[...]] + [micro_ref[:, x] for x in range(4)] + [xhigh_ref[...]]
    fields = jnp.concatenate([plane.reshape(64, 128) for plane in planes], axis=1).astype(F32)
    rims = jnp.concatenate([ylow_ref[...], yhigh_ref[...]], axis=0)
    rim_rows = {}
    for dz in range(3):
        moved = shift_z(fields, dz - 1).astype(BF16)
        moved_rim = shift_z(rims, dz - 1)
        for dx in range(3):
            at = (dx * 3 + dz) * 64
            stack[at : at + 64, :] = moved[:, 128 * dx : 128 * dx + 512]
            rim_rows[dx, dz] = moved_rim[:, 128 * dx : 128 * dx + 512]
    rim_block = jnp.concatenate([rim_rows[dx, dz] for dx in range(3) for dz in range(3)], axis=0)
    stack[HALO_AT:U_AT, :] = jnp.concatenate(
        [rim_block, jnp.zeros((U_AT - HALO_AT - 72, 512), F32)], axis=0
    ).astype(BF16)
    total = jnp.sum(parts_ref[...], axis=0)
    high, low = split(total)
    groups = ones_where(iota((8, 128), 0) == (iota((8, 128), 1) >> 4))
    same = iota((16, 128), 0) == (iota((16, 128), 1) & 15)
    for part, values in enumerate((high, low)):
        expanded = dot(values, groups, TN)
        for j in range(4):
            for chunk in range(32):
                row = expanded[32 * j + chunk : 32 * j + chunk + 1, :]
                at = 64 * part + 16 * j
                spread[at : at + 16, 128 * chunk : 128 * chunk + 128] = jnp.where(
                    same, row, 0.0
                ).astype(BF16)
    for x in range(0, 4, 2):
        field = jnp.zeros((128, 256), F32)
        for at in range(0, 256, 16):
            basis = jnp.concatenate(
                [psi_ref[at : at + 16, x + k].reshape(256, 128) for k in range(2)], axis=1
            )
            field = field + dot(spread[:, 16 * at : 16 * at + 256], basis)
        stack[U_AT:STACK, 128 * x : 128 * x + 256] = (field[:64] + field[64:]).astype(BF16)
    pre[...] = dot(table_ref[...], stack[...])

    def activate(o, carry):
        rows = pl.ds(pl.multiple_of(o * 16, 16), 16)
        for x in range(4):
            lanes = slice(128 * x, 128 * x + 128)
            values = pre[rows, lanes]
            cumulative = 0.5 * (1.0 + lax.erf(values * (1.0 / math.sqrt(2.0))))
            density = jnp.exp(-0.5 * values * values) * (1.0 / math.sqrt(2.0 * math.pi))
            out_ref[0, o, x] = values * cumulative
            slope = cumulative + values * density
            grad[rows, lanes] = (cot_ref[0, o, x].astype(F32) * slope).astype(BF16)
        return carry

    lax.fori_loop(0, 32, activate, 0, unroll=2)
    corr[...] = dot(grad[...], stack[...], NT)
    bands = [band(codes, dy) for dy in range(3)]
    moments = jnp.zeros((32, TAPROWS), F32)
    reduced = [[], [], []]
    for o in range(32):
        block = corr[16 * o : 16 * o + 16, :]
        for dy in range(3):
            reduced[dy].append(jnp.sum(jnp.where(bands[dy], block, 0.0), axis=0, keepdims=True))
    for dy in range(3):
        moments = moments + dot_split(jnp.concatenate(reduced[dy], axis=0), selector(codes, dy), NT)
    lift = lift_ref[...]
    high, low = split(moments)
    lanes112 = iota((112, 128), 1)
    rows112 = iota((112, 128), 0)
    conv = conv_ref[0]
    products = dot(conv, high, TN) + dot(conv, low, TN)
    products = products.reshape(27, 32, TAPROWS)
    own = iota((27, 1, TAPROWS), 0) == (iota((27, 1, TAPROWS), 2) >> 2)
    summed = jnp.sum(jnp.where(own, products, 0.0), axis=0)
    to_lane = ones_where(((rows112 & 3) == lanes112 - 124) & (rows112 < 108))
    lift_term = dot_split(summed, to_lane)
    last = ones_where((rows112 - 108 == lanes112 - 124) & (rows112 >= 108))
    coupled = dot_split(moments, last)
    chigh, clow = split(coupled)
    lift_term = lift_term + inv * (dot(mix_ref[0], chigh) + dot(mix_ref[0], clow))
    keep = ones_where((rows112 == lanes112) & (rows112 < 108))
    kept = dot_split(moments, keep)
    block = kept + lift_term
    shared = jnp.zeros((8, 128), F32)
    for b in range(4):
        pick = ones_where((rows112 - 108 == lanes112 - 108 - 4 * b) & (rows112 >= 108))
        shared = shared + dot_split(moments[8 * b : 8 * b + 8], pick)
    for k in range(4):
        message = (block[8 * k : 8 * k + 8] + shared).astype(send_ref.dtype)
        send_ref[k] = jnp.broadcast_to(message[None], send_ref.shape[1:])


def finish_kernel(scale, inv, recv_ref, lift_ref, conv_out, mix_out, lift_out):
    lift = lift_ref[...]
    rep = lax.axis_index("rep")
    flat = recv_ref[...].reshape(1024, 128)
    total = dot(ones_where(iota((8, 1024), 0) == (iota((8, 1024), 1) & 7)), flat)
    conv_out[0] = dot_split(total, lift_blocks(lift), NT) * scale
    owned = ones_where(iota((8, 32), 1) == iota((8, 32), 0) + 8 * rep)
    for b in range(4):
        left = dot(owned, lift_columns(lift, 108 + 4 * b).astype(BF16)).astype(BF16)
        high, low = split(total)
        mix_out[0, :, 8 * b : 8 * b + 8] = (dot(left, high, NT) + dot(left, low, NT)) * (scale * inv)
    pick = ones_where(iota((4, 128), 1) - 124 == iota((4, 128), 0))
    high, low = split(total)
    lift_out[...] = (dot(pick, high, NT) + dot(pick, low, NT)) * scale


VMEM = pl.BlockSpec(memory_space=pltpu.VMEM)
LIMIT = pltpu.CompilerParams(vmem_limit_bytes=40 * 1024 * 1024)


def on_device(micro_fields, lift_w, conv_w, mix_w, phi, psi, cotangent):
    micro = micro_fields[0]
    rank = phi.shape[0]
    cells = micro.shape[1] * micro.shape[2] * micro.shape[3]
    gx, gy, reps = lax.axis_size("gx"), lax.axis_size("gy"), lax.axis_size("rep")
    total_cells = cells * gx * gy
    inv = 1.0 / math.sqrt(total_cells) / math.sqrt(rank)
    scale = 1.0 / math.sqrt(total_cells * reps)
    codes = jnp.asarray(stack_codes())

    up = lambda count: [(i, i + 1) for i in range(count - 1)]
    down = lambda count: [(i + 1, i) for i in range(count - 1)]
    xlow = lax.ppermute(micro[:, -1], "gx", up(gx))
    xhigh = lax.ppermute(micro[:, 0], "gx", down(gx))

    steps = 8
    parts = pl.pallas_call(
        functools.partial(project_kernel, steps),
        grid=(steps,),
        in_specs=[
            pl.BlockSpec((4, 4, 16, 128), lambda s: (0, 0, 0, 0)),
            pl.BlockSpec((rank // steps, 4, 16, 128), lambda s: (s, 0, 0, 0)),
        ],
        out_specs=pl.BlockSpec((gx * gy, 8, 128), lambda s: (0, 0, 0)),
        out_shape=jax.ShapeDtypeStruct((gx * gy, 8, 128), F32),
        scratch_shapes=[pltpu.VMEM((4, 32, 128), F32)],
        name="project",
    )(micro, phi)

    first, last = pl.pallas_call(
        edge_kernel,
        in_specs=[VMEM] * 3,
        out_specs=[VMEM] * 2,
        out_shape=[jax.ShapeDtypeStruct((4, 768), F32)] * 2,
        name="edges",
    )(micro, xlow, xhigh)
    ylow = lax.ppermute(last, "gy", up(gy))
    yhigh = lax.ppermute(first, "gy", down(gy))

    table = pl.pallas_call(
        functools.partial(weights_kernel, inv),
        in_specs=[VMEM] * 4,
        out_specs=VMEM,
        out_shape=jax.ShapeDtypeStruct((512, STACK), BF16),
        compiler_params=LIMIT,
        name="weights",
    )(lift_w, conv_w, mix_w, codes)

    gathered = lax.all_to_all(parts, ("gx", "gy"), 0, 0)

    out_field, send = pl.pallas_call(
        functools.partial(main_kernel, inv),
        in_specs=[VMEM] * 13,
        out_specs=[VMEM] * 2,
        out_shape=[
            jax.ShapeDtypeStruct((1, 32, 4, 16, 128), F32),
            jax.ShapeDtypeStruct((reps, gx * gy, 8, 128), BF16),
        ],
        scratch_shapes=[
            pltpu.VMEM((STACK, 512), BF16),
            pltpu.VMEM((128, 4096), BF16),
            pltpu.VMEM((512, 512), F32),
            pltpu.VMEM((512, 512), BF16),
            pltpu.VMEM((512, STACK), F32),
        ],
        compiler_params=LIMIT,
        name="layer",
    )(gathered, micro, xlow, xhigh, ylow, yhigh, table, psi, cotangent, lift_w, conv_w, mix_w, codes)

    received = lax.all_to_all(send.reshape(reps * gx * gy, 8, 128), ("rep", "gx", "gy"), 0, 0)

    grads = pl.pallas_call(
        functools.partial(finish_kernel, scale, inv),
        in_specs=[VMEM] * 2,
        out_specs=[VMEM] * 3,
        out_shape=[
            jax.ShapeDtypeStruct((1, 8, 864), F32),
            jax.ShapeDtypeStruct((1, 8, 32), F32),
            jax.ShapeDtypeStruct((4, 8), F32),
        ],
        compiler_params=LIMIT,
        name="finish",
    )(received, lift_w)
    return (out_field, *grads)


def solution(mesh):
    return jax.shard_map(
        on_device,
        mesh=mesh,
        in_specs=(
            P("rep", None, "gx", "gy", None),
            P(),
            P(),
            P(),
            P(None, "gx", "gy", None),
            P(None, "gx", "gy", None),
            P("rep", None, "gx", "gy", None),
        ),
        out_specs=(
            P("rep", None, "gx", "gy", None),
            P(None, "rep", None),
            P(None, "rep", None),
            P(None, "rep"),
        ),
        check_vma=False,
    )
```

time: 555 us -> 66.9 us (0.12); the launches traced: 544 us -> 66.3 us
  blocking collectives: 388 us -> 23.1 us
  matrix products: 38.5 us -> 0 us
  local copies, waits for them, and re-layouts: 37.4 us -> 4.27 us
  waiting for transfers between devices: 32.5 us -> 3.27 us
  Pallas kernels: 0 us -> 16.1 us
  between operations: 15.7 us -> 0.83 us
  other arithmetic: 11.6 us -> 0 us
    psum x3 -> x0, blocking collectives: 375 us -> none  [the longest x1 127 us: on_device(): lax.psum((grad_terms[0], grad_terms[1], grad_terms[2]), ('gx', 'gy'))]
    dot_general x12 -> x0, matrix products: 38.5 us -> none  [the longest x1 9.83 us: on_device(): lax.dot_general(grad_pre, stacked, (((1,), (1,)), ((), ())), preferred_el...]
    unnamed x2 -> x0, waiting for transfers between devices: 32.5 us -> none
    all_to_all x0 -> x1, blocking collectives: none -> 23.1 us  [on_device(): lax.all_to_all(send.reshape(reps * gx * gy, 8, 128), ('rep', 'gx', 'gy'),...]
    unnamed x75 -> x25, local copies, waits for them, and re-layouts: 24.2 us -> 4.27 us
    pallas_call x0 -> x5, Pallas kernels: none -> 16.1 us  [the longest x1 6.78 us: on_device(): pl.pallas_call(functools.partial(project_kernel, steps), grid=(steps,), i...]
    unnamed x1 -> x0, blocking collectives: 12.8 us -> none
    ppermute x8 -> x4, starting transfers between devices: 20.5 us -> 10.1 us  [the longest x1 3.42 us: on_device(): xlow = lax.ppermute(micro[:, -1], 'gx', up(gx))]
  transfers between devices with their start and end apart: 9 -> 5, of which waited for: 1 -> 2; matrix products, arithmetic and copies ran while one was open for 2% -> 0% of each run, Pallas kernels for 0% -> 4%
where the time goes in v1:
time: 66.9 us; the launch traced here: 66.3 us
  blocking collectives  23.1 us (35%)
  starting transfers between devices  18.7 us (28%)
  Pallas kernels  16.1 us (24%)
  local copies, waits for them, and re-layouts  4.27 us (6%)
  waiting for transfers between devices  3.27 us (5%)
  between operations  0.83 us (1%)
    all_to_all x1, blocking collectives, on_device(): lax.all_to_all(send.reshape(reps * gx * gy, 8, 128), ('rep', 'gx', 'gy'),...  23.1 us
    all_to_all x1, starting transfers between devices, on_device(): gathered = lax.all_to_all(parts, ('gx', 'gy'), 0, 0)  8.59 us
    pallas_call x1, Pallas kernels, on_device(): pl.pallas_call(functools.partial(project_kernel, steps), grid=(steps,), i...  6.78 us
    pallas_call x1, Pallas kernels, on_device(): pl.pallas_call(functools.partial(main_kernel, inv), in_specs=[VMEM] * 13,...  5.21 us
    unnamed x25, local copies, waits for them, and re-layouts  4.27 us
    ppermute x1, starting transfers between devices, on_device(): xlow = lax.ppermute(micro[:, -1], 'gx', up(gx))  3.42 us
    ppermute x1, starting transfers between devices, on_device(): ylow = lax.ppermute(last, 'gy', up(gy))  3.28 us
    ppermute x1, waiting for transfers between devices, on_device(): yhigh = lax.ppermute(first, 'gy', down(gy))  2.43 us
  transfers between devices with their start and end apart: 5, of which 2 were waited for; matrix products, arithmetic and copies ran while one was open for 0% of the time, Pallas kernels for 4%

profile of v1, /device:TPU:1, one launch (start us, length us, event | category | flops | bytes accessed | tf_op | source)
XLA Modules:
  0.0 66.3 jit_solution(10458022658288222118)
XLA Ops:
  0.6 0.0 copy-start.5
  0.6 0.0 copy-start.1
  0.7 0.0 copy-start.2
  0.7 0.0 copy-start.11
  0.7 0.0 copy-start.10
  0.7 0.0 copy-start.4
  0.7 0.0 copy-start.3
  0.7 6.8 %project.1 = f32[32,8,128]{2,1,0:T(8,128)} custom-call(bf16[4,4,16,128]{3,2,1,0:T(8,128)(2,1)} %bitcast.9, bf16[256,4,16,128]{3,2,1,0:T(8,128)(2,1)} %phi_ref.1), custom_call_target="tpu_custom_call" | custom-call | tf_op jit(solution)/shard_map/project/pallas_call | solution.py:301
  7.5 8.6 %all-to-all-start = ((f32[32,8,128]{2,1,0:T(8,128)}), f32[32,8,128]{2,1,0:T(8,128)S(1)}, u32[]{:S(2)}, u32[]{:S(2)}) async-start(f32[32,8,128]{2,1,0:T(8,128)} %project.1), calls=%async_computation | async-start | bytes 262144 | tf_op jit(solution)/shard_map/all_to_all | solution.py:333
  16.1 0.0 copy-done.1
  16.1 2.1 %collective-permute-start.1 = (bf16[4,16,128]{2,1,0:T(8,128)(2,1)S(1)}, bf16[4,16,128]{2,1,0:T(8,128)(2,1)S(1)}, u32[]{:S(2)}, u32[]{:S(2)}) collective-permute-start(bf16[4,16,128]{2,1,0:T(8,128)(2,1)S(1)} %get-tuple-element.18), channel_id=1, source_target_pairs={{4,0},{8,4},{12,8},{16,12},{20,16},{24,20},{28,24},{5,1},{9,5},{13... | collective-permute-start | bytes 49160 | tf_op jit(solution)/shard_map/ppermute | solution.py:298
  18.3 3.4 %collective-permute-start = (bf16[4,16,128]{2,1,0:T(8,128)(2,1)S(1)}, bf16[4,16,128]{2,1,0:T(8,128)(2,1)S(1)}, u32[]{:S(2)}, u32[]{:S(2)}) collective-permute-start(bf16[4,16,128]{2,1,0:T(8,128)(2,1)S(1)} %get-tuple-element.19), channel_id=1, source_target_pairs={{0,4},{4,8},{8,12},{12,16},{16,20},{20,24},{24,28},{1,5},{5,9},{9,... | collective-permute-start | bytes 49160 | tf_op jit(solution)/shard_map/ppermute | solution.py:297
  21.7 0.0 collective-permute-done.1.high_ref.xhigh_ref
  21.7 0.0 copy-start.6
  21.7 0.8 %collective-permute-done.low_ref.xlow_ref = bf16[4,16,128]{2,1,0:T(8,128)(2,1)S(1)} collective-permute-done((bf16[4,16,128]{2,1,0:T(8,128)(2,1)S(1)}, bf16[4,16,128]{2,1,0:T(8,128)(2,1)S(1)}, u32[]{:S(2)}, u32[]{:S(2)}) %collective-permute-start) | collective-permute-done | bytes 16416 | tf_op jit(solution)/shard_map/ppermute | solution.py:297
  22.5 0.0 copy-done.6
  22.5 0.0 copy-start.8
  22.5 0.6 copy-done.8
  23.2 1.5 %edges.1 = (f32[4,768]{1,0:T(4,128)}, f32[4,768]{1,0:T(4,128)}) custom-call(bf16[4,4,16,128]{3,2,1,0:T(8,128)(2,1)} %bitcast.10, bf16[4,16,128]{2,1,0:T(8,128)(2,1)} %copy-done.8, bf16[4,16,128]{2,1,0:T(8,128)(2,1)} %copy-done.6), custom_call_target="tpu_custom_call" | custom-call | tf_op jit(solution)/shard_map/edges/pallas_call | solution.py:314
  24.6 3.3 %collective-permute-start.2 = (f32[4,768]{1,0:T(4,128)}, f32[4,768]{1,0:T(4,128)S(1)}, u32[]{:S(2)}, u32[]{:S(2)}) collective-permute-start(f32[4,768]{1,0:T(4,128)} %get-tuple-element.11), channel_id=1, source_target_pairs={{0,1},{1,2},{2,3},{4,5},{5,6},{6,7},{8,9},{9,10},{10,11},{12,13},{... | collective-permute-start | bytes 36872 | tf_op jit(solution)/shard_map/ppermute | solution.py:321
  27.9 1.3 %collective-permute-start.3 = (f32[4,768]{1,0:T(4,128)}, f32[4,768]{1,0:T(4,128)S(1)}, u32[]{:S(2)}, u32[]{:S(2)}) collective-permute-start(f32[4,768]{1,0:T(4,128)} %get-tuple-element.12), channel_id=1, source_target_pairs={{1,0},{2,1},{3,2},{5,4},{6,5},{7,6},{9,8},{10,9},{11,10},{13,12},{... | collective-permute-start | bytes 36872 | tf_op jit(solution)/shard_map/ppermute | solution.py:322
  29.2 0.0 copy-done.5
  29.2 0.0 copy-done.11
  29.2 0.0 copy-done.10
  29.2 0.0 copy-done.4
  29.3 1.0 %weights.1.table_ref = bf16[512,768]{1,0:T(8,128)(2,1)S(1)} custom-call(bf16[4,32]{1,0:T(4,128)(2,1)S(1)} %copy-done.11, bf16[1,32,864]{2,1,0:T(8,128)(2,1)S(1)} %copy-done.4, bf16[1,32,32]{2,1,0:T(8,128)(2,1)S(1)} %copy-done.10, s32[8,768]{1,0:T(8,128)S(1)} %copy-done.5), custom_call_target="tpu_custom_call" | custom-call | tf_op jit(solution)/shard_map/weights/pallas_call | solution.py:324
  30.2 0.0 collective-permute-done.2.ylow_ref
  30.3 2.4 %collective-permute-done.3.yhigh_ref = f32[4,768]{1,0:T(4,128)S(1)} collective-permute-done((f32[4,768]{1,0:T(4,128)}, f32[4,768]{1,0:T(4,128)S(1)}, u32[]{:S(2)}, u32[]{:S(2)}) %collective-permute-start.3) | collective-permute-done | bytes 12320 | tf_op jit(solution)/shard_map/ppermute | solution.py:322
  32.7 0.0 all-to-all-done.parts_ref
  32.7 0.0 copy-done.2
  32.7 0.0 copy-done.3
  32.7 0.0 copy-start
  32.7 2.2 %copy-done = bf16[256,4,16,128]{3,2,1,0:T(8,128)(2,1)S(1)} copy-done((bf16[256,4,16,128]{3,2,1,0:T(8,128)(2,1)S(1)}, bf16[256,4,16,128]{3,2,1,0:T(8,128)(2,1)}, u32[]{:S(2)}) %copy-start) | copy-done | bytes 4194328
  34.9 0.0 copy-start.7
  34.9 0.7 %copy-done.7 = bf16[4,16,128]{2,1,0:T(8,128)(2,1)S(1)} copy-done((bf16[4,16,128]{2,1,0:T(8,128)(2,1)S(1)}, bf16[4,16,128]{2,1,0:T(8,128)(2,1)}, u32[]{:S(2)}) %copy-start.7) | copy-done | bytes 16408
  35.6 0.0 copy-start.9
  35.6 0.7 %copy-done.9 = bf16[4,16,128]{2,1,0:T(8,128)(2,1)S(1)} copy-done((bf16[4,16,128]{2,1,0:T(8,128)(2,1)S(1)}, bf16[4,16,128]{2,1,0:T(8,128)(2,1)}, u32[]{:S(2)}) %copy-start.9) | copy-done | bytes 16408
  36.3 5.2 %layer.1 = (f32[1,32,4,16,128]{4,3,2,1,0:T(8,128)}, bf16[4,32,8,128]{3,2,1,0:T(8,128)(2,1)S(1)}) custom-call(f32[32,8,128]{2,1,0:T(8,128)S(1)} %all-to-all-done.parts_ref, bf16[4,4,16,128]{3,2,1,0:T(8,128)(2,1)S(1)} %bitcast.11, bf16[4,16,128]{2,1,0:T(8,128)(2,1)S(1)} %copy-done.9, bf16[4,16,128]{2,1,0:T(8,128)(2,1)S(1)} %copy-done.7, ...), custom_call_target="tpu_custom_call" | custom-call | tf_op jit(solution)/shard_map/layer/pallas_call | solution.py:335
  41.5 23.1 %all_to_all.10.recv_ref = bf16[128,8,128]{2,1,0:T(8,128)(2,1)S(1)} all-to-all(bf16[128,8,128]{2,1,0:T(8,128)(2,1)S(1)} %bitcast.12), channel_id=1, replica_groups=mesh['rep'=4,'gx'=8,'gy'=4] {'rep','gx','gy'}, dimensions={0} | all-to-all | bytes 524288 | tf_op jit(solution)/shard_map/all_to_all | solution.py:354
  64.7 1.7 %finish.1 = (f32[1,8,864]{2,1,0:T(8,128)}, f32[1,8,32]{2,1,0:T(8,128)}, f32[4,8]{1,0:T(4,128)}) custom-call(bf16[128,8,128]{2,1,0:T(8,128)(2,1)S(1)} %all_to_all.10.recv_ref, bf16[4,32]{1,0:T(4,128)(2,1)S(1)} %copy-done.11), custom_call_target="tpu_custom_call" | custom-call | tf_op jit(solution)/shard_map/finish/pallas_call | solution.py:356
  (2 shorter events, 0.0 us)
Async XLA Ops:
  0.6 28.6 %copy-start.5 = (s32[8,768]{1,0:T(8,128)S(1)}, s32[8,768]{1,0:T(8,128)}, u32[]{:S(2)}) copy-start(s32[8,768]{1,0:T(8,128)} %constant.2.clone.codes_ref) | copy-start | bytes 73732
  0.6 15.4 %copy-start.1 = (bf16[1,4,4,16,128]{4,3,2,1,0:T(8,128)(2,1)S(1)}, bf16[1,4,4,16,128]{4,3,2,1,0:T(8,128)(2,1)}, u32[]{:S(2)}) copy-start(bf16[1,4,4,16,128]{4,3,2,1,0:T(8,128)(2,1)} %param.8) | copy-start | bytes 196612
  0.7 32.0 %copy-start.2 = (bf16[1,4,4,16,128]{4,3,2,1,0:T(8,128)(2,1)S(1)}, bf16[1,4,4,16,128]{4,3,2,1,0:T(8,128)(2,1)}, u32[]{:S(2)}) copy-start(bf16[1,4,4,16,128]{4,3,2,1,0:T(8,128)(2,1)} %param.8) | copy-start | bytes 196612
  0.7 28.6 %copy-start.11 = (bf16[4,32]{1,0:T(4,128)(2,1)S(1)}, bf16[4,32]{1,0:T(4,128)(2,1)}, u32[]{:S(2)}) copy-start(bf16[4,32]{1,0:T(4,128)(2,1)} %lift_ref.5) | copy-start | bytes 772
  0.7 28.6 %copy-start.10 = (bf16[1,32,32]{2,1,0:T(8,128)(2,1)S(1)}, bf16[1,32,32]{2,1,0:T(8,128)(2,1)}, u32[]{:S(2)}) copy-start(bf16[1,32,32]{2,1,0:T(8,128)(2,1)} %mix_ref.3) | copy-start | bytes 6148
  0.7 28.6 %copy-start.4 = (bf16[1,32,864]{2,1,0:T(8,128)(2,1)S(1)}, bf16[1,32,864]{2,1,0:T(8,128)(2,1)}, u32[]{:S(2)}) copy-start(bf16[1,32,864]{2,1,0:T(8,128)(2,1)} %conv_ref.3) | copy-start | bytes 165892
  0.7 32.0 %copy-start.3 = (bf16[1,32,4,16,128]{4,3,2,1,0:T(8,128)(2,1)S(1)}, bf16[1,32,4,16,128]{4,3,2,1,0:T(8,128)(2,1)}, u32[]{:S(2)}) copy-start(bf16[1,32,4,16,128]{4,3,2,1,0:T(8,128)(2,1)} %cot_ref.1) | copy-start | bytes 1572868
  7.5 25.2 %all-to-all-start = ((f32[32,8,128]{2,1,0:T(8,128)}), f32[32,8,128]{2,1,0:T(8,128)S(1)}, u32[]{:S(2)}, u32[]{:S(2)}) async-start(f32[32,8,128]{2,1,0:T(8,128)} %project.1), calls=%async_computation | async-start | bytes 262144 | tf_op jit(solution)/shard_map/all_to_all | solution.py:333
  16.1 5.6 %collective-permute-start.1 = (bf16[4,16,128]{2,1,0:T(8,128)(2,1)S(1)}, bf16[4,16,128]{2,1,0:T(8,128)(2,1)S(1)}, u32[]{:S(2)}, u32[]{:S(2)}) collective-permute-start(bf16[4,16,128]{2,1,0:T(8,128)(2,1)S(1)} %get-tuple-element.18), channel_id=1, source_target_pairs={{4,0},{8,4},{12,8},{16,12},{20,16},{24,20},{28,24},{5,1},{9,5},{13... | collective-permute-start | bytes 49160 | tf_op jit(solution)/shard_map/ppermute | solution.py:298
  18.3 4.3 %collective-permute-start = (bf16[4,16,128]{2,1,0:T(8,128)(2,1)S(1)}, bf16[4,16,128]{2,1,0:T(8,128)(2,1)S(1)}, u32[]{:S(2)}, u32[]{:S(2)}) collective-permute-start(bf16[4,16,128]{2,1,0:T(8,128)(2,1)S(1)} %get-tuple-element.19), channel_id=1, source_target_pairs={{0,4},{4,8},{8,12},{12,16},{16,20},{20,24},{24,28},{1,5},{5,9},{9,... | collective-permute-start | bytes 49160 | tf_op jit(solution)/shard_map/ppermute | solution.py:297
  21.7 0.8 %copy-start.6 = (bf16[4,16,128]{2,1,0:T(8,128)(2,1)}, bf16[4,16,128]{2,1,0:T(8,128)(2,1)S(1)}, u32[]{:S(2)}) copy-start(bf16[4,16,128]{2,1,0:T(8,128)(2,1)S(1)} %collective-permute-done.1.high_ref.xhigh_ref) | copy-start | bytes 49156
  22.5 0.6 copy-start.8
  24.6 5.6 %collective-permute-start.2 = (f32[4,768]{1,0:T(4,128)}, f32[4,768]{1,0:T(4,128)S(1)}, u32[]{:S(2)}, u32[]{:S(2)}) collective-permute-start(f32[4,768]{1,0:T(4,128)} %get-tuple-element.11), channel_id=1, source_target_pairs={{0,1},{1,2},{2,3},{4,5},{5,6},{6,7},{8,9},{9,10},{10,11},{12,13},{... | collective-permute-start | bytes 36872 | tf_op jit(solution)/shard_map/ppermute | solution.py:321
  27.9 4.8 %collective-permute-start.3 = (f32[4,768]{1,0:T(4,128)}, f32[4,768]{1,0:T(4,128)S(1)}, u32[]{:S(2)}, u32[]{:S(2)}) collective-permute-start(f32[4,768]{1,0:T(4,128)} %get-tuple-element.12), channel_id=1, source_target_pairs={{1,0},{2,1},{3,2},{5,4},{6,5},{7,6},{9,8},{10,9},{11,10},{13,12},{... | collective-permute-start | bytes 36872 | tf_op jit(solution)/shard_map/ppermute | solution.py:322
  32.7 2.2 %copy-start = (bf16[256,4,16,128]{3,2,1,0:T(8,128)(2,1)S(1)}, bf16[256,4,16,128]{3,2,1,0:T(8,128)(2,1)}, u32[]{:S(2)}) copy-start(bf16[256,4,16,128]{3,2,1,0:T(8,128)(2,1)} %psi_ref.1) | copy-start | bytes 12582916
  34.9 0.7 %copy-start.7 = (bf16[4,16,128]{2,1,0:T(8,128)(2,1)S(1)}, bf16[4,16,128]{2,1,0:T(8,128)(2,1)}, u32[]{:S(2)}) copy-start(bf16[4,16,128]{2,1,0:T(8,128)(2,1)} %copy-done.6) | copy-start | bytes 49156
  35.6 0.7 %copy-start.9 = (bf16[4,16,128]{2,1,0:T(8,128)(2,1)S(1)}, bf16[4,16,128]{2,1,0:T(8,128)(2,1)}, u32[]{:S(2)}) copy-start(bf16[4,16,128]{2,1,0:T(8,128)(2,1)} %copy-done.8) | copy-start | bytes 49156

commit v2 on v1

--- a/solution.py
+++ b/solution.py
@@ -128,7 +128,24 @@
             preferred_element_type=F32,
             precision=lax.Precision.HIGHEST,
         )
-        out_ref[...] = jnp.broadcast_to(total[None], out_ref.shape)
+        high = total.astype(BF16).astype(F32)
+        me = lax.axis_index("gy")
+        edges = []
+        for row in (0, 15):
+            pick = ones_where(iota((8, 64), 1) == (iota((8, 64), 0) & 3) * 16 + row)
+            edge = dot(pick, fields)
+            upper = iota((8, 128), 0) < 4
+            edges.append(
+                [
+                    jnp.where(upper, edge[:, at : at + 128], edge[:, at + 128 : at + 256])
+                    for at in (0, 256)
+                ]
+            )
+        for target in range(4):
+            rim = [jnp.where(target > me, last, first) for first, last in zip(*edges)]
+            message = jnp.concatenate([high, total - high] + rim, axis=0).astype(BF16)
+            for plane in range(out_ref.shape[0] // 4):
+                out_ref[4 * plane + target] = message
 
 
 def shift_z(values, dz):
@@ -143,11 +160,28 @@
     return jnp.where(lanes == (127 if dz > 0 else 0), 0.0, rolled)
 
 
-def edge_kernel(micro_ref, low_ref, high_ref, first_ref, last_ref):
+def received_rims(parts_ref):
+    gx, gy = lax.axis_index("gx"), lax.axis_index("gy")
+    planes = parts_ref.shape[0] // 4
+
+    def tile(plane, row, at):
+        valid = (plane >= 0) & (plane < planes) & (row >= 0) & (row < 4)
+        peer = jnp.clip(plane, 0, planes - 1) * 4 + jnp.clip(row, 0, 3)
+        both = parts_ref[peer, 16:32, :].astype(F32)
+        return jnp.where(valid, both[at : at + 8], 0.0)
+
+    pieces = []
+    lower = iota((8, 128), 0) < 4
     for x in range(6):
-        block = (low_ref[...] if x == 0 else high_ref[...] if x == 5 else micro_ref[:, x - 1]).astype(F32)
-        first_ref[:, 128 * x : 128 * x + 128] = block[:, 0, :]
-        last_ref[:, 128 * x : 128 * x + 128] = block[:, 15, :]
+        plane = gx - 1 if x == 0 else gx + 1 if x == 5 else gx
+        own = (x - 1) % 4
+        below, above = [tile(plane, gy + step, 8 * (own // 2)) for step in (-1, 1)]
+        if own % 2:
+            below = pltpu.roll(below, 4, 0)
+        else:
+            above = pltpu.roll(above, 4, 0)
+        pieces.append(jnp.where(lower, below, above))
+    return jnp.concatenate(pieces, axis=1)
 
 
 def main_kernel(
@@ -156,8 +190,6 @@
     micro_ref,
     xlow_ref,
     xhigh_ref,
-    ylow_ref,
-    yhigh_ref,
     table_ref,
     psi_ref,
     cot_ref,
@@ -176,7 +208,7 @@
     codes = codes_ref[...]
     planes = [xlow_ref[...]] + [micro_ref[:, x] for x in range(4)] + [xhigh_ref[...]]
     fields = jnp.concatenate([plane.reshape(64, 128) for plane in planes], axis=1).astype(F32)
-    rims = jnp.concatenate([ylow_ref[...], yhigh_ref[...]], axis=0)
+    rims = received_rims(parts_ref)
     rim_rows = {}
     for dz in range(3):
         moved = shift_z(fields, dz - 1).astype(BF16)
@@ -189,8 +221,8 @@
     stack[HALO_AT:U_AT, :] = jnp.concatenate(
         [rim_block, jnp.zeros((U_AT - HALO_AT - 72, 512), F32)], axis=0
     ).astype(BF16)
-    total = jnp.sum(parts_ref[...], axis=0)
-    high, low = split(total)
+    both = jnp.sum(parts_ref[:, 0:16, :].astype(F32), axis=0)
+    high, low = split(both[:8] + both[8:])
     groups = ones_where(iota((8, 128), 0) == (iota((8, 128), 1) >> 4))
     same = iota((16, 128), 0) == (iota((16, 128), 1) & 15)
     for part, values in enumerate((high, low)):
@@ -279,7 +311,7 @@
 
 
 VMEM = pl.BlockSpec(memory_space=pltpu.VMEM)
-LIMIT = pltpu.CompilerParams(vmem_limit_bytes=40 * 1024 * 1024)
+LIMIT = pltpu.CompilerParams(vmem_limit_bytes=20 * 1024 * 1024)
 
 
 def on_device(micro_fields, lift_w, conv_w, mix_w, phi, psi, cotangent):
@@ -305,21 +337,11 @@
             pl.BlockSpec((4, 4, 16, 128), lambda s: (0, 0, 0, 0)),
             pl.BlockSpec((rank // steps, 4, 16, 128), lambda s: (s, 0, 0, 0)),
         ],
-        out_specs=pl.BlockSpec((gx * gy, 8, 128), lambda s: (0, 0, 0)),
-        out_shape=jax.ShapeDtypeStruct((gx * gy, 8, 128), F32),
+        out_specs=pl.BlockSpec((gx * gy, 32, 128), lambda s: (0, 0, 0)),
+        out_shape=jax.ShapeDtypeStruct((gx * gy, 32, 128), BF16),
         scratch_shapes=[pltpu.VMEM((4, 32, 128), F32)],
         name="project",
     )(micro, phi)
-
-    first, last = pl.pallas_call(
-        edge_kernel,
-        in_specs=[VMEM] * 3,
-        out_specs=[VMEM] * 2,
-        out_shape=[jax.ShapeDtypeStruct((4, 768), F32)] * 2,
-        name="edges",
-    )(micro, xlow, xhigh)
-    ylow = lax.ppermute(last, "gy", up(gy))
-    yhigh = lax.ppermute(first, "gy", down(gy))
 
     table = pl.pallas_call(
         functools.partial(weights_kernel, inv),
@@ -334,7 +356,7 @@
 
     out_field, send = pl.pallas_call(
         functools.partial(main_kernel, inv),
-        in_specs=[VMEM] * 13,
+        in_specs=[VMEM] * 11,
         out_specs=[VMEM] * 2,
         out_shape=[
             jax.ShapeDtypeStruct((1, 32, 4, 16, 128), F32),
@@ -349,7 +371,7 @@
         ],
         compiler_params=LIMIT,
         name="layer",
-    )(gathered, micro, xlow, xhigh, ylow, yhigh, table, psi, cotangent, lift_w, conv_w, mix_w, codes)
+    )(gathered, micro, xlow, xhigh, table, psi, cotangent, lift_w, conv_w, mix_w, codes)
 
     received = lax.all_to_all(send.reshape(reps * gx * gy, 8, 128), ("rep", "gx", "gy"), 0, 0)
 

time: 66.9 us -> 54.4 us (0.81)
  starting transfers between devices: 18.7 us -> 14.2 us
  blocking collectives: 23.1 us -> 19.9 us
  local copies, waits for them, and re-layouts: 4.27 us -> 2.23 us
  Pallas kernels: 16.1 us -> 14.8 us
  waiting for transfers between devices: 3.27 us -> 2.23 us
    ppermute x2 -> x0, starting transfers between devices: 4.57 us -> none  [the longest x1 3.28 us: on_device(): ylow = lax.ppermute(last, 'gy', up(gy))]
    all_to_all x1, blocking collectives: 23.1 us -> 19.9 us  [on_device(): lax.all_to_all(send.reshape(reps * gx * gy, 8, 128), ('rep', 'gx', 'gy'),...]
    ppermute x2 -> x0, waiting for transfers between devices: 2.44 us -> none  [the longest x1 2.43 us: on_device(): yhigh = lax.ppermute(first, 'gy', down(gy))]
    all_to_all x1, waiting for transfers between devices: 0.01 us -> 2.22 us  [on_device(): gathered = lax.all_to_all(parts, ('gx', 'gy'), 0, 0)]
    unnamed x25 -> x15, local copies, waits for them, and re-layouts: 4.27 us -> 2.22 us
    pallas_call x2 -> x1, Pallas kernels: 6.69 us -> 5.2 us  [on_device(): pl.pallas_call(functools.partial(main_kernel, inv), in_specs=[VMEM] * 11,...]
    ppermute x1, waiting for transfers between devices: 0.83 us -> 0.01 us  [on_device(): xlow = lax.ppermute(micro[:, -1], 'gx', up(gx))]
  transfers between devices with their start and end apart: 5 -> 3, of which waited for: 2 -> 1; matrix products, arithmetic and copies ran while one was open for 0% -> 0% of each run, Pallas kernels for 4% -> 2%
where the time goes in v2:
time: 54.4 us; the launch traced here: 54.1 us
  blocking collectives  19.9 us (37%)
  Pallas kernels  14.8 us (27%)
  starting transfers between devices  14.2 us (26%)
  local copies, waits for them, and re-layouts  2.23 us (4%)
  waiting for transfers between devices  2.23 us (4%)
  between operations  0.79 us (1%)
    all_to_all x1, blocking collectives, on_device(): lax.all_to_all(send.reshape(reps * gx * gy, 8, 128), ('rep', 'gx', 'gy'),...  19.9 us
    all_to_all x1, starting transfers between devices, on_device(): gathered = lax.all_to_all(parts, ('gx', 'gy'), 0, 0)  8.59 us
    pallas_call x1, Pallas kernels, on_device(): pl.pallas_call(functools.partial(project_kernel, steps), grid=(steps,), i...  6.92 us
    pallas_call x1, Pallas kernels, on_device(): pl.pallas_call(functools.partial(main_kernel, inv), in_specs=[VMEM] * 11,...  5.2 us
    ppermute x1, starting transfers between devices, on_device(): xlow = lax.ppermute(micro[:, -1], 'gx', up(gx))  3.42 us
    all_to_all x1, waiting for transfers between devices, on_device(): gathered = lax.all_to_all(parts, ('gx', 'gy'), 0, 0)  2.22 us
    unnamed x15, local copies, waits for them, and re-layouts  2.22 us
    ppermute x1, starting transfers between devices, on_device(): xhigh = lax.ppermute(micro[:, 0], 'gx', down(gx))  2.14 us
  transfers between devices with their start and end apart: 3, of which 1 were waited for; matrix products, arithmetic and copies ran while one was open for 0% of the time, Pallas kernels for 2%

profile of v2, /device:TPU:1, one launch (start us, length us, event | category | flops | bytes accessed | tf_op | source)
XLA Modules:
  0.0 54.1 jit_solution(9908149686245581882)
XLA Ops:
  0.6 0.0 copy-start.4
  0.6 0.0 copy-start.1
  0.7 0.0 copy-start.6
  0.7 0.0 copy-start.5
  0.7 0.0 copy-start.3
  0.7 0.0 copy-start.2
  0.7 6.9 %project.1 = bf16[32,32,128]{2,1,0:T(8,128)(2,1)} custom-call(bf16[4,4,16,128]{3,2,1,0:T(8,128)(2,1)} %bitcast.9, bf16[256,4,16,128]{3,2,1,0:T(8,128)(2,1)} %phi_ref.1), custom_call_target="tpu_custom_call" | custom-call | tf_op jit(solution)/shard_map/project/pallas_call | solution.py:333
  7.6 8.6 %all-to-all-start = ((bf16[32,32,128]{2,1,0:T(8,128)(2,1)}), bf16[32,32,128]{2,1,0:T(8,128)(2,1)S(1)}, u32[]{:S(2)}, u32[]{:S(2)}) async-start(bf16[32,32,128]{2,1,0:T(8,128)(2,1)} %project.1), calls=%async_computation | async-start | bytes 524288 | tf_op jit(solution)/shard_map/all_to_all | solution.py:355
  16.2 0.0 copy-done.1
  16.3 2.1 %collective-permute-start.1 = (bf16[4,16,128]{2,1,0:T(8,128)(2,1)S(1)}, bf16[4,16,128]{2,1,0:T(8,128)(2,1)S(1)}, u32[]{:S(2)}, u32[]{:S(2)}) collective-permute-start(bf16[4,16,128]{2,1,0:T(8,128)(2,1)S(1)} %get-tuple-element.14), channel_id=1, source_target_pairs={{4,0},{8,4},{12,8},{16,12},{20,16},{24,20},{28,24},{5,1},{9,5},{13... | collective-permute-start | bytes 49160 | tf_op jit(solution)/shard_map/ppermute | solution.py:330
  18.4 3.4 %collective-permute-start = (bf16[4,16,128]{2,1,0:T(8,128)(2,1)S(1)}, bf16[4,16,128]{2,1,0:T(8,128)(2,1)S(1)}, u32[]{:S(2)}, u32[]{:S(2)}) collective-permute-start(bf16[4,16,128]{2,1,0:T(8,128)(2,1)S(1)} %get-tuple-element.15), channel_id=1, source_target_pairs={{0,4},{4,8},{8,12},{12,16},{16,20},{20,24},{24,28},{1,5},{5,9},{9,... | collective-permute-start | bytes 49160 | tf_op jit(solution)/shard_map/ppermute | solution.py:329
  21.8 0.0 copy-done.4
  21.8 0.0 copy-done.6
  21.8 0.0 copy-done.5
  21.9 0.0 copy-done.3
  21.9 1.0 %weights.1.table_ref = bf16[512,768]{1,0:T(8,128)(2,1)S(1)} custom-call(bf16[4,32]{1,0:T(4,128)(2,1)S(1)} %copy-done.6, bf16[1,32,864]{2,1,0:T(8,128)(2,1)S(1)} %copy-done.3, bf16[1,32,32]{2,1,0:T(8,128)(2,1)S(1)} %copy-done.5, s32[8,768]{1,0:T(8,128)S(1)} %copy-done.4), custom_call_target="tpu_custom_call" | custom-call | tf_op jit(solution)/shard_map/weights/pallas_call | solution.py:346
  22.9 0.0 collective-permute-done.1.xhigh_ref
  22.9 0.0 collective-permute-done.xlow_ref
  22.9 2.2 %all-to-all-done.parts_ref = bf16[32,32,128]{2,1,0:T(8,128)(2,1)S(1)} async-done(((bf16[32,32,128]{2,1,0:T(8,128)(2,1)}), bf16[32,32,128]{2,1,0:T(8,128)(2,1)S(1)}, u32[]{:S(2)}, u32[]{:S(2)}) %all-to-all-start) | async-done | bytes 262176 | tf_op jit(solution)/shard_map/all_to_all | solution.py:355
  25.1 0.0 copy-done.2
  25.1 0.0 copy-start
  25.1 2.2 %copy-done = bf16[256,4,16,128]{3,2,1,0:T(8,128)(2,1)S(1)} copy-done((bf16[256,4,16,128]{3,2,1,0:T(8,128)(2,1)S(1)}, bf16[256,4,16,128]{3,2,1,0:T(8,128)(2,1)}, u32[]{:S(2)}) %copy-start) | copy-done | bytes 4194328
  27.3 5.2 %layer.1 = (f32[1,32,4,16,128]{4,3,2,1,0:T(8,128)}, bf16[4,32,8,128]{3,2,1,0:T(8,128)(2,1)S(1)}) custom-call(bf16[32,32,128]{2,1,0:T(8,128)(2,1)S(1)} %all-to-all-done.parts_ref, bf16[4,4,16,128]{3,2,1,0:T(8,128)(2,1)S(1)} %bitcast.10, bf16[4,16,128]{2,1,0:T(8,128)(2,1)S(1)} %collective-permute-done.xlow_ref, ...), custom_call_target="tpu_custom_call" | custom-call | tf_op jit(solution)/shard_map/layer/pallas_call | solution.py:357
  32.5 19.9 %all_to_all.10.recv_ref = bf16[128,8,128]{2,1,0:T(8,128)(2,1)S(1)} all-to-all(bf16[128,8,128]{2,1,0:T(8,128)(2,1)S(1)} %bitcast.11), channel_id=1, replica_groups=mesh['rep'=4,'gx'=8,'gy'=4] {'rep','gx','gy'}, dimensions={0} | all-to-all | bytes 524288 | tf_op jit(solution)/shard_map/all_to_all | solution.py:376
  52.4 1.7 %finish.1 = (f32[1,8,864]{2,1,0:T(8,128)}, f32[1,8,32]{2,1,0:T(8,128)}, f32[4,8]{1,0:T(4,128)}) custom-call(bf16[128,8,128]{2,1,0:T(8,128)(2,1)S(1)} %all_to_all.10.recv_ref, bf16[4,32]{1,0:T(4,128)(2,1)S(1)} %copy-done.6), custom_call_target="tpu_custom_call" | custom-call | tf_op jit(solution)/shard_map/finish/pallas_call | solution.py:378
  (2 shorter events, 0.0 us)
Async XLA Ops:
  0.6 21.2 %copy-start.4 = (s32[8,768]{1,0:T(8,128)S(1)}, s32[8,768]{1,0:T(8,128)}, u32[]{:S(2)}) copy-start(s32[8,768]{1,0:T(8,128)} %constant.2.clone.codes_ref) | copy-start | bytes 73732
  0.6 15.6 %copy-start.1 = (bf16[1,4,4,16,128]{4,3,2,1,0:T(8,128)(2,1)S(1)}, bf16[1,4,4,16,128]{4,3,2,1,0:T(8,128)(2,1)}, u32[]{:S(2)}) copy-start(bf16[1,4,4,16,128]{4,3,2,1,0:T(8,128)(2,1)} %param.8) | copy-start | bytes 196612
  0.7 21.2 %copy-start.6 = (bf16[4,32]{1,0:T(4,128)(2,1)S(1)}, bf16[4,32]{1,0:T(4,128)(2,1)}, u32[]{:S(2)}) copy-start(bf16[4,32]{1,0:T(4,128)(2,1)} %lift_ref.5) | copy-start | bytes 772
  0.7 21.2 %copy-start.5 = (bf16[1,32,32]{2,1,0:T(8,128)(2,1)S(1)}, bf16[1,32,32]{2,1,0:T(8,128)(2,1)}, u32[]{:S(2)}) copy-start(bf16[1,32,32]{2,1,0:T(8,128)(2,1)} %mix_ref.3) | copy-start | bytes 6148
  0.7 21.2 %copy-start.3 = (bf16[1,32,864]{2,1,0:T(8,128)(2,1)S(1)}, bf16[1,32,864]{2,1,0:T(8,128)(2,1)}, u32[]{:S(2)}) copy-start(bf16[1,32,864]{2,1,0:T(8,128)(2,1)} %conv_ref.3) | copy-start | bytes 165892
  0.7 24.4 %copy-start.2 = (bf16[1,32,4,16,128]{4,3,2,1,0:T(8,128)(2,1)S(1)}, bf16[1,32,4,16,128]{4,3,2,1,0:T(8,128)(2,1)}, u32[]{:S(2)}) copy-start(bf16[1,32,4,16,128]{4,3,2,1,0:T(8,128)(2,1)} %cot_ref.1) | copy-start | bytes 1572868
  7.6 17.5 %all-to-all-start = ((bf16[32,32,128]{2,1,0:T(8,128)(2,1)}), bf16[32,32,128]{2,1,0:T(8,128)(2,1)S(1)}, u32[]{:S(2)}, u32[]{:S(2)}) async-start(bf16[32,32,128]{2,1,0:T(8,128)(2,1)} %project.1), calls=%async_computation | async-start | bytes 524288 | tf_op jit(solution)/shard_map/all_to_all | solution.py:355
  16.3 6.6 %collective-permute-start.1 = (bf16[4,16,128]{2,1,0:T(8,128)(2,1)S(1)}, bf16[4,16,128]{2,1,0:T(8,128)(2,1)S(1)}, u32[]{:S(2)}, u32[]{:S(2)}) collective-permute-start(bf16[4,16,128]{2,1,0:T(8,128)(2,1)S(1)} %get-tuple-element.14), channel_id=1, source_target_pairs={{4,0},{8,4},{12,8},{16,12},{20,16},{24,20},{28,24},{5,1},{9,5},{13... | collective-permute-start | bytes 49160 | tf_op jit(solution)/shard_map/ppermute | solution.py:330
  18.4 4.5 %collective-permute-start = (bf16[4,16,128]{2,1,0:T(8,128)(2,1)S(1)}, bf16[4,16,128]{2,1,0:T(8,128)(2,1)S(1)}, u32[]{:S(2)}, u32[]{:S(2)}) collective-permute-start(bf16[4,16,128]{2,1,0:T(8,128)(2,1)S(1)} %get-tuple-element.15), channel_id=1, source_target_pairs={{0,4},{4,8},{8,12},{12,16},{16,20},{20,24},{24,28},{1,5},{5,9},{9,... | collective-permute-start | bytes 49160 | tf_op jit(solution)/shard_map/ppermute | solution.py:329
  25.1 2.2 %copy-start = (bf16[256,4,16,128]{3,2,1,0:T(8,128)(2,1)S(1)}, bf16[256,4,16,128]{3,2,1,0:T(8,128)(2,1)}, u32[]{:S(2)}) copy-start(bf16[256,4,16,128]{3,2,1,0:T(8,128)(2,1)} %psi_ref.1) | copy-start | bytes 12582916

commit v3 on v2

--- a/solution.py
+++ b/solution.py
@@ -18,6 +18,8 @@
 STACK = 768
 HALO_AT = 576
 U_AT = 704
+PIECES = 8
+EARLY = 3
 TAPROWS = 112
 
 
@@ -91,61 +93,80 @@
     return jnp.where(own, columns[None], 0.0).reshape(864, 128).astype(BF16)
 
 
-def weights_kernel(inv, lift_ref, conv_ref, mix_ref, codes_ref, table_ref):
-    lift = lift_ref[...]
-    codes = codes_ref[...]
-    taps = dot(conv_ref[0], lift_blocks(lift))
-    mixed = dot(mix_ref[0], lift_columns(lift, 108).astype(BF16), TN) * inv
+def weight_table(inv, lift, conv, mix, codes):
+    taps = dot(conv, lift_blocks(lift))
+    mixed = dot(mix, lift_columns(lift, 108).astype(BF16), TN) * inv
     weights = (taps + mixed).astype(BF16)[:, :TAPROWS]
     table = jnp.zeros((32, 16, STACK), F32)
     for dy in range(3):
         spread = dot(weights, selector(codes, dy))
         table = jnp.where(band(codes, dy)[None], spread[:, None, :], table)
-    table_ref[...] = table.reshape(512, STACK).astype(BF16)
-
-
-def project_kernel(steps, micro_ref, phi_ref, out_ref, sums):
-    step = pl.program_id(0)
-    rows = phi_ref.shape[0]
-    wide = rows * 16
-    fields = jnp.concatenate([micro_ref[:, x].reshape(64, 128) for x in range(4)], axis=1)
-    basis = jnp.concatenate([phi_ref[:, x].reshape(wide, 128) for x in range(4)], axis=1)
-    product = dot(fields, basis, NT)
-    same = iota((16, wide), 0) == (iota((16, wide), 1) & 15)
-    chunks = rows // 8
-    for j in range(4):
-        line = jnp.sum(jnp.where(same, product[16 * j : 16 * j + 16], 0.0), axis=0, keepdims=True)
-        for chunk in range(chunks):
-            sums[j, pl.ds(step * chunks + chunk, 1), :] = line[:, 128 * chunk : 128 * chunk + 128]
-
-    @pl.when(step == steps - 1)
-    def _():
-        groups = jnp.where(iota((8, 128), 0) == (iota((8, 128), 1) >> 4), 1.0, 0.0)
-        total = lax.dot_general(
-            groups,
-            sums[...].reshape(128, 128),
-            NT,
-            preferred_element_type=F32,
-            precision=lax.Precision.HIGHEST,
+    return table.reshape(512, STACK).astype(BF16)
+
+
+def stage_kernel(inv, lift_ref, conv_ref, mix_ref, codes_ref, psi_ref, table_ref, *rest):
+    pieces, sems = rest[:-1], rest[-1]
+    count = psi_ref.shape[0] // PIECES
+    copies = [
+        pltpu.make_async_copy(psi_ref.at[pl.ds(k * count, count)], piece, sems.at[k])
+        for k, piece in enumerate(pieces)
+    ]
+    for item in copies:
+        item.start()
+    table_ref[...] = weight_table(inv, lift_ref[...], conv_ref[0], mix_ref[0], codes_ref[...])
+    for item in copies:
+        item.wait()
+
+
+def project_kernel(parts, micro_ref, phi_ref, out_ref, fields_ref, basis_ref, sums, field_sem, sems):
+    def copy(at, count, sem):
+        rows = pl.ds(at, count)
+        return pltpu.make_async_copy(phi_ref.at[rows], basis_ref.at[rows], sem)
+
+    starts = [sum(parts[:k]) for k in range(len(parts))]
+    copies = [copy(at, count, sems.at[k]) for k, (at, count) in enumerate(zip(starts, parts))]
+    own = pltpu.make_async_copy(micro_ref, fields_ref, field_sem)
+    own.start()
+    for item in copies:
+        item.start()
+    own.wait()
+    fields = jnp.concatenate([fields_ref[:, x].reshape(64, 128) for x in range(4)], axis=1)
+    for item, at, count in zip(copies, starts, parts):
+        item.wait()
+        wide = count * 16
+        basis = jnp.concatenate(
+            [basis_ref[at : at + count, x].reshape(wide, 128) for x in range(4)], axis=1
         )
-        high = total.astype(BF16).astype(F32)
-        me = lax.axis_index("gy")
-        edges = []
-        for row in (0, 15):
-            pick = ones_where(iota((8, 64), 1) == (iota((8, 64), 0) & 3) * 16 + row)
-            edge = dot(pick, fields)
-            upper = iota((8, 128), 0) < 4
-            edges.append(
-                [
-                    jnp.where(upper, edge[:, at : at + 128], edge[:, at + 128 : at + 256])
-                    for at in (0, 256)
-                ]
+        product = dot(fields, basis, NT)
+        same = iota((16, wide), 0) == (iota((16, wide), 1) & 15)
+        for j in range(4):
+            line = jnp.sum(
+                jnp.where(same, product[16 * j : 16 * j + 16], 0.0), axis=0, keepdims=True
             )
-        for target in range(4):
-            rim = [jnp.where(target > me, last, first) for first, last in zip(*edges)]
-            message = jnp.concatenate([high, total - high] + rim, axis=0).astype(BF16)
-            for plane in range(out_ref.shape[0] // 4):
-                out_ref[4 * plane + target] = message
+            for chunk in range(count // 8):
+                row = at // 8 + chunk
+                sums[j, row : row + 1, :] = line[:, 128 * chunk : 128 * chunk + 128]
+    groups = ones_where(iota((8, 128), 0) == (iota((8, 128), 1) >> 4))
+    first_part, rest = split(sums[...].reshape(128, 128))
+    total = dot(groups, first_part, NT) + dot(groups, rest, NT)
+    high = total.astype(BF16).astype(F32)
+    me = lax.axis_index("gy")
+    edges = []
+    for row in (0, 15):
+        pick = ones_where(iota((8, 64), 1) == (iota((8, 64), 0) & 3) * 16 + row)
+        edge = dot(pick, fields)
+        upper = iota((8, 128), 0) < 4
+        edges.append(
+            [
+                jnp.where(upper, edge[:, at : at + 128], edge[:, at + 128 : at + 256])
+                for at in (0, 256)
+            ]
+        )
+    for target in range(4):
+        rim = [jnp.where(target > me, last, first) for first, last in zip(*edges)]
+        message = jnp.concatenate([high, total - high] + rim, axis=0).astype(BF16)
+        for plane in range(out_ref.shape[0] // 4):
+            out_ref[4 * plane + target] = message
 
 
 def shift_z(values, dz):
@@ -188,15 +209,19 @@
     inv,
     parts_ref,
     micro_ref,
-    xlow_ref,
-    xhigh_ref,
-    table_ref,
-    psi_ref,
+    near_ref,
+    far_ref,
+    table,
     cot_ref,
     lift_ref,
     conv_ref,
     mix_ref,
     codes_ref,
+    *rest,
+):
+    psi_refs = list(rest[:EARLY])
+    psi_ref = rest[EARLY]
+    (
     out_ref,
     send_ref,
     stack,
@@ -204,9 +229,23 @@
     pre,
     grad,
     corr,
-):
+    late_ref,
+    sems,
+    ) = rest[EARLY + 1 :]
+    count = psi_ref.shape[0] // PIECES
+    copies = []
+    for k in range(EARLY, PIECES):
+        piece = late_ref.at[pl.ds((k - EARLY) * count, count)]
+        copies.append(
+            pltpu.make_async_copy(psi_ref.at[pl.ds(k * count, count)], piece, sems.at[k - EARLY])
+        )
+        copies[-1].start()
+        psi_refs.append(piece)
     codes = codes_ref[...]
-    planes = [xlow_ref[...]] + [micro_ref[:, x] for x in range(4)] + [xhigh_ref[...]]
+    even = lax.axis_index("gx") % 2 == 0
+    near, far = near_ref[...], far_ref[...]
+    ends = jnp.where(even, far, near), jnp.where(even, near, far)
+    planes = [ends[0]] + [micro_ref[:, x] for x in range(4)] + [ends[1]]
     fields = jnp.concatenate([plane.reshape(64, 128) for plane in planes], axis=1).astype(F32)
     rims = received_rims(parts_ref)
     rim_rows = {}
@@ -234,15 +273,21 @@
                 spread[at : at + 16, 128 * chunk : 128 * chunk + 128] = jnp.where(
                     same, row, 0.0
                 ).astype(BF16)
-    for x in range(0, 4, 2):
-        field = jnp.zeros((128, 256), F32)
-        for at in range(0, 256, 16):
-            basis = jnp.concatenate(
-                [psi_ref[at : at + 16, x + k].reshape(256, 128) for k in range(2)], axis=1
-            )
-            field = field + dot(spread[:, 16 * at : 16 * at + 256], basis)
-        stack[U_AT:STACK, 128 * x : 128 * x + 256] = (field[:64] + field[64:]).astype(BF16)
-    pre[...] = dot(table_ref[...], stack[...])
+    fields = [jnp.zeros((128, 256), F32) for _ in range(2)]
+    for k, piece in enumerate(psi_refs):
+        if k == EARLY:
+            for item in copies:
+                item.wait()
+        for pair in range(2):
+            for row in range(0, count, 16):
+                at = k * count + row
+                basis = jnp.concatenate(
+                    [piece[row : row + 16, 2 * pair + n].reshape(256, 128) for n in range(2)], axis=1
+                )
+                fields[pair] = fields[pair] + dot(spread[:, 16 * at : 16 * at + 256], basis)
+    for pair, field in enumerate(fields):
+        stack[U_AT:STACK, 256 * pair : 256 * pair + 256] = (field[:64] + field[64:]).astype(BF16)
+    pre[...] = dot(table[...], stack[...])
 
     def activate(o, carry):
         rows = pl.ds(pl.multiple_of(o * 16, 16), 16)
@@ -311,6 +356,13 @@
 
 
 VMEM = pl.BlockSpec(memory_space=pltpu.VMEM)
+HBM = pl.BlockSpec(memory_space=pltpu.HBM)
+
+
+def in_hbm(array):
+    return pltpu.with_memory_space_constraint(array, pltpu.HBM)
+
+
 LIMIT = pltpu.CompilerParams(vmem_limit_bytes=20 * 1024 * 1024)
 
 
@@ -324,39 +376,47 @@
     scale = 1.0 / math.sqrt(total_cells * reps)
     codes = jnp.asarray(stack_codes())
 
-    up = lambda count: [(i, i + 1) for i in range(count - 1)]
-    down = lambda count: [(i + 1, i) for i in range(count - 1)]
-    xlow = lax.ppermute(micro[:, -1], "gx", up(gx))
-    xhigh = lax.ppermute(micro[:, 0], "gx", down(gx))
-
-    steps = 8
+    even = lax.axis_index("gx") % 2 == 0
+    first, last = micro[:, 0], micro[:, -1]
+    on_chip = [(i, i ^ 1) for i in range(gx)]
+    off_chip = [(i, ((i + 1) ^ 1) - 1) for i in range(1, gx - 1)]
+    near = lax.ppermute(jnp.where(even, last, first), "gx", on_chip)
+    far = lax.ppermute(jnp.where(even, first, last), "gx", off_chip)
+
+    rows = (rank // 2, rank // 4, rank // 4)
     parts = pl.pallas_call(
-        functools.partial(project_kernel, steps),
-        grid=(steps,),
-        in_specs=[
-            pl.BlockSpec((4, 4, 16, 128), lambda s: (0, 0, 0, 0)),
-            pl.BlockSpec((rank // steps, 4, 16, 128), lambda s: (s, 0, 0, 0)),
+        functools.partial(project_kernel, rows),
+        in_specs=[HBM] * 2,
+        out_specs=VMEM,
+        out_shape=jax.ShapeDtypeStruct((gx * gy, 32, 128), BF16),
+        scratch_shapes=[
+            pltpu.VMEM(micro.shape, BF16),
+            pltpu.VMEM(phi.shape, BF16),
+            pltpu.VMEM((4, 32, 128), F32),
+            pltpu.SemaphoreType.DMA,
+            pltpu.SemaphoreType.DMA((len(rows),)),
         ],
-        out_specs=pl.BlockSpec((gx * gy, 32, 128), lambda s: (0, 0, 0)),
-        out_shape=jax.ShapeDtypeStruct((gx * gy, 32, 128), BF16),
-        scratch_shapes=[pltpu.VMEM((4, 32, 128), F32)],
+        compiler_params=pltpu.CompilerParams(vmem_limit_bytes=16 * 1024 * 1024),
         name="project",
-    )(micro, phi)
-
-    table = pl.pallas_call(
-        functools.partial(weights_kernel, inv),
-        in_specs=[VMEM] * 4,
-        out_specs=VMEM,
-        out_shape=jax.ShapeDtypeStruct((512, STACK), BF16),
-        compiler_params=LIMIT,
-        name="weights",
-    )(lift_w, conv_w, mix_w, codes)
+    )(in_hbm(micro), in_hbm(phi))
 
     gathered = lax.all_to_all(parts, ("gx", "gy"), 0, 0)
+
+    table, *pieces = pl.pallas_call(
+        functools.partial(stage_kernel, inv),
+        in_specs=[VMEM] * 4 + [HBM],
+        out_specs=[VMEM] * (1 + EARLY),
+        out_shape=[jax.ShapeDtypeStruct((512, STACK), BF16)]
+        + [jax.ShapeDtypeStruct((rank // PIECES,) + psi.shape[1:], BF16)] * EARLY,
+        scratch_shapes=[pltpu.SemaphoreType.DMA((EARLY,))],
+        compiler_params=pltpu.CompilerParams(vmem_limit_bytes=8 * 1024 * 1024),
+        cost_estimate=pl.CostEstimate(flops=2_000_000_000, bytes_accessed=4_000_000, transcendentals=0),
+        name="stage",
+    )(lift_w, conv_w, mix_w, codes, in_hbm(psi))
 
     out_field, send = pl.pallas_call(
         functools.partial(main_kernel, inv),
-        in_specs=[VMEM] * 11,
+        in_specs=[VMEM] * (10 + EARLY) + [HBM],
         out_specs=[VMEM] * 2,
         out_shape=[
             jax.ShapeDtypeStruct((1, 32, 4, 16, 128), F32),
@@ -368,10 +428,13 @@
             pltpu.VMEM((512, 512), F32),
             pltpu.VMEM((512, 512), BF16),
             pltpu.VMEM((512, STACK), F32),
+            pltpu.VMEM((rank // PIECES * (PIECES - EARLY),) + psi.shape[1:], BF16),
+            pltpu.SemaphoreType.DMA((PIECES - EARLY,)),
         ],
         compiler_params=LIMIT,
+        cost_estimate=pl.CostEstimate(flops=4_000_000_000, bytes_accessed=6_000_000, transcendentals=500_000),
         name="layer",
-    )(gathered, micro, xlow, xhigh, table, psi, cotangent, lift_w, conv_w, mix_w, codes)
+    )(gathered, micro, near, far, table, cotangent, lift_w, conv_w, mix_w, codes, *pieces, in_hbm(psi))
 
     received = lax.all_to_all(send.reshape(reps * gx * gy, 8, 128), ("rep", "gx", "gy"), 0, 0)
 

time: 54.4 us -> 49.9 us (0.917)
  local copies, waits for them, and re-layouts: 2.23 us -> 0.04 us
  starting transfers between devices: 14.2 us -> 12.4 us
  blocking collectives: 19.9 us -> 18.2 us
  waiting for transfers between devices: 2.23 us -> 3.42 us
    unnamed x15 -> x13, local copies, waits for them, and re-layouts: 2.22 us -> 0.04 us
    ppermute x2, starting transfers between devices: 5.56 us -> 3.63 us  [the longest x1 3.54 us: on_device(): far = lax.ppermute(jnp.where(even, first, last), 'gx', off_chip)]
    all_to_all x1, blocking collectives: 19.9 us -> 18.2 us  [on_device(): lax.all_to_all(send.reshape(reps * gx * gy, 8, 128), ('rep', 'gx', 'gy'),...]
    all_to_all x1, waiting for transfers between devices: 2.22 us -> 3.35 us  [on_device(): gathered = lax.all_to_all(parts, ('gx', 'gy'), 0, 0)]
  transfers between devices with their start and end apart: 3 -> 3, of which waited for: 1 -> 2; matrix products, arithmetic and copies ran while one was open for 0% -> 0% of each run, Pallas kernels for 2% -> 3%
where the time goes in v3:
time: 49.9 us; the launch traced here: 49.6 us
  blocking collectives  18.2 us (36%)
  Pallas kernels  14.8 us (30%)
  starting transfers between devices  12.4 us (25%)
  waiting for transfers between devices  3.42 us (7%)
  between operations  0.8 us (2%)
    all_to_all x1, blocking collectives, on_device(): lax.all_to_all(send.reshape(reps * gx * gy, 8, 128), ('rep', 'gx', 'gy'),...  18.2 us
    all_to_all x1, starting transfers between devices, on_device(): gathered = lax.all_to_all(parts, ('gx', 'gy'), 0, 0)  8.74 us
    pallas_call x1, Pallas kernels, on_device(): pl.pallas_call(functools.partial(main_kernel, inv), in_specs=[VMEM] * (10...  6.83 us
    pallas_call x1, Pallas kernels, on_device(): pl.pallas_call(functools.partial(project_kernel, rows), in_specs=[HBM] *...  4.59 us
    ppermute x1, starting transfers between devices, on_device(): far = lax.ppermute(jnp.where(even, first, last), 'gx', off_chip)  3.54 us
    all_to_all x1, waiting for transfers between devices, on_device(): gathered = lax.all_to_all(parts, ('gx', 'gy'), 0, 0)  3.35 us
    pallas_call x1, Pallas kernels, on_device(): pl.pallas_call(functools.partial(stage_kernel, inv), in_specs=[VMEM] * 4...  1.72 us
    pallas_call x1, Pallas kernels, on_device(): pl.pallas_call(functools.partial(finish_kernel, scale, inv), in_specs=[VM...  1.68 us
  transfers between devices with their start and end apart: 3, of which 2 were waited for; matrix products, arithmetic and copies ran while one was open for 0% of the time, Pallas kernels for 3%

profile of v3, /device:TPU:1, one launch (start us, length us, event | category | flops | bytes accessed | tf_op | source)
XLA Modules:
  0.0 49.6 jit_solution(5734401943740525051)
XLA Ops:
  0.6 0.0 copy-start.5
  0.6 0.0 copy-start
  0.7 0.0 copy-start.1
  0.7 0.0 copy-start.4
  0.7 0.0 copy-start.3
  0.7 4.6 %project.1 = bf16[32,32,128]{2,1,0:T(8,128)(2,1)} custom-call(bf16[4,4,16,128]{3,2,1,0:T(8,128)(2,1)} %bitcast.9, bf16[256,4,16,128]{3,2,1,0:T(8,128)(2,1)} %phi_ref.1), custom_call_target="tpu_custom_call" | custom-call | tf_op jit(solution)/shard_map/project/pallas_call | solution.py:387
  5.3 0.0 copy-start.2
  5.3 8.7 %all-to-all-start = ((bf16[32,32,128]{2,1,0:T(8,128)(2,1)}), bf16[32,32,128]{2,1,0:T(8,128)(2,1)S(1)}, u32[]{:S(2)}, u32[]{:S(2)}) async-start(bf16[32,32,128]{2,1,0:T(8,128)(2,1)} %project.1), calls=%async_computation | async-start | bytes 524288 | tf_op jit(solution)/shard_map/all_to_all | solution.py:403
  14.0 0.0 copy-done
  14.1 3.5 %collective-permute-start.1 = (bf16[4,16,128]{2,1,0:T(8,128)(2,1)S(1)}, bf16[4,16,128]{2,1,0:T(8,128)(2,1)S(1)}, u32[]{:S(2)}, u32[]{:S(2)}) collective-permute-start(bf16[4,16,128]{2,1,0:T(8,128)(2,1)S(1)} %get-tuple-element.22), channel_id=1, source_target_pairs={{4,8},{8,4},{12,16},{16,12},{20,24},{24,20},{5,9},{9,5},{13,17},{1... | collective-permute-start | bytes 49160 | tf_op jit(solution)/shard_map/ppermute | solution.py:384
  17.6 0.1 collective-permute-start
  17.7 0.0 copy-done.5
  17.7 0.0 copy-done.1
  17.8 0.0 copy-done.4
  17.8 0.0 copy-done.3
  17.8 1.7 %stage.1 = (bf16[512,768]{1,0:T(8,128)(2,1)S(1)}, bf16[32,4,16,128]{3,2,1,0:T(8,128)(2,1)S(1)}, bf16[32,4,16,128]{3,2,1,0:T(8,128)(2,1)S(1)}, bf16[32,4,16,128]{3,2,1,0:T(8,128)(2,1)S(1)}) custom-call(bf16[4,32]{1,0:T(4,128)(2,1)S(1)} %copy-done.1, bf16[1,32,864]{2,1,0:T(8,128)(2,1)S(1)} %copy-done.3, bf16[1,32,32]{2,1,0:T(8,128)(2,1)S(1)} %copy-done.4, ...), custom_call_target="tpu_custom_call" | custom-call | flops 2000000000 | bytes 4000000 | tf_op jit(solution)/shard_map/stage/pallas_call | solution.py:405
  19.5 0.1 collective-permute-done.1.far_ref
  19.6 0.0 collective-permute-done.near_ref
  19.6 3.3 %all-to-all-done.parts_ref = bf16[32,32,128]{2,1,0:T(8,128)(2,1)S(1)} async-done(((bf16[32,32,128]{2,1,0:T(8,128)(2,1)}), bf16[32,32,128]{2,1,0:T(8,128)(2,1)S(1)}, u32[]{:S(2)}, u32[]{:S(2)}) %all-to-all-start) | async-done | bytes 262176 | tf_op jit(solution)/shard_map/all_to_all | solution.py:403
  22.9 0.0 copy-done.2
  22.9 6.8 %layer.1 = (f32[1,32,4,16,128]{4,3,2,1,0:T(8,128)}, bf16[4,32,8,128]{3,2,1,0:T(8,128)(2,1)S(1)}) custom-call(bf16[32,32,128]{2,1,0:T(8,128)(2,1)S(1)} %all-to-all-done.parts_ref, bf16[4,4,16,128]{3,2,1,0:T(8,128)(2,1)S(1)} %bitcast.10, bf16[4,16,128]{2,1,0:T(8,128)(2,1)S(1)} %collective-permute-done.near_ref, ...), custom_call_target="tpu_custom_call" | custom-call | flops 4000000000 | bytes 6000000 | tf_op jit(solution)/shard_map/layer/pallas_call | solution.py:417
  29.8 18.2 %all_to_all.10.recv_ref = bf16[128,8,128]{2,1,0:T(8,128)(2,1)S(1)} all-to-all(bf16[128,8,128]{2,1,0:T(8,128)(2,1)S(1)} %bitcast.11), channel_id=1, replica_groups=mesh['rep'=4,'gx'=8,'gy'=4] {'rep','gx','gy'}, dimensions={0} | all-to-all | bytes 524288 | tf_op jit(solution)/shard_map/all_to_all | solution.py:439
  48.0 1.7 %finish.1 = (f32[1,8,864]{2,1,0:T(8,128)}, f32[1,8,32]{2,1,0:T(8,128)}, f32[4,8]{1,0:T(4,128)}) custom-call(bf16[128,8,128]{2,1,0:T(8,128)(2,1)S(1)} %all_to_all.10.recv_ref, bf16[4,32]{1,0:T(4,128)(2,1)S(1)} %copy-done.1), custom_call_target="tpu_custom_call" | custom-call | tf_op jit(solution)/shard_map/finish/pallas_call | solution.py:441
  (2 shorter events, 0.0 us)
Async XLA Ops:
  0.6 17.1 %copy-start.5 = (s32[8,768]{1,0:T(8,128)S(1)}, s32[8,768]{1,0:T(8,128)}, u32[]{:S(2)}) copy-start(s32[8,768]{1,0:T(8,128)} %constant.22.clone.codes_ref) | copy-start | bytes 73732
  0.6 13.4 %copy-start = (bf16[1,4,4,16,128]{4,3,2,1,0:T(8,128)(2,1)S(1)}, bf16[1,4,4,16,128]{4,3,2,1,0:T(8,128)(2,1)}, u32[]{:S(2)}) copy-start(bf16[1,4,4,16,128]{4,3,2,1,0:T(8,128)(2,1)} %param.8) | copy-start | bytes 196612
  0.7 17.1 %copy-start.1 = (bf16[4,32]{1,0:T(4,128)(2,1)S(1)}, bf16[4,32]{1,0:T(4,128)(2,1)}, u32[]{:S(2)}) copy-start(bf16[4,32]{1,0:T(4,128)(2,1)} %lift_ref.5) | copy-start | bytes 772
  0.7 17.1 %copy-start.4 = (bf16[1,32,32]{2,1,0:T(8,128)(2,1)S(1)}, bf16[1,32,32]{2,1,0:T(8,128)(2,1)}, u32[]{:S(2)}) copy-start(bf16[1,32,32]{2,1,0:T(8,128)(2,1)} %mix_ref.3) | copy-start | bytes 6148
  0.7 17.1 %copy-start.3 = (bf16[1,32,864]{2,1,0:T(8,128)(2,1)S(1)}, bf16[1,32,864]{2,1,0:T(8,128)(2,1)}, u32[]{:S(2)}) copy-start(bf16[1,32,864]{2,1,0:T(8,128)(2,1)} %conv_ref.3) | copy-start | bytes 165892
  5.3 17.7 %copy-start.2 = (bf16[1,32,4,16,128]{4,3,2,1,0:T(8,128)(2,1)S(1)}, bf16[1,32,4,16,128]{4,3,2,1,0:T(8,128)(2,1)}, u32[]{:S(2)}) copy-start(bf16[1,32,4,16,128]{4,3,2,1,0:T(8,128)(2,1)} %cot_ref.1) | copy-start | bytes 1572868
  5.3 17.6 %all-to-all-start = ((bf16[32,32,128]{2,1,0:T(8,128)(2,1)}), bf16[32,32,128]{2,1,0:T(8,128)(2,1)S(1)}, u32[]{:S(2)}, u32[]{:S(2)}) async-start(bf16[32,32,128]{2,1,0:T(8,128)(2,1)} %project.1), calls=%async_computation | async-start | bytes 524288 | tf_op jit(solution)/shard_map/all_to_all | solution.py:403
  14.1 5.5 %collective-permute-start.1 = (bf16[4,16,128]{2,1,0:T(8,128)(2,1)S(1)}, bf16[4,16,128]{2,1,0:T(8,128)(2,1)S(1)}, u32[]{:S(2)}, u32[]{:S(2)}) collective-permute-start(bf16[4,16,128]{2,1,0:T(8,128)(2,1)S(1)} %get-tuple-element.22), channel_id=1, source_target_pairs={{4,8},{8,4},{12,16},{16,12},{20,24},{24,20},{5,9},{9,5},{13,17},{1... | collective-permute-start | bytes 49160 | tf_op jit(solution)/shard_map/ppermute | solution.py:384
  17.6 1.9 %collective-permute-start = (bf16[4,16,128]{2,1,0:T(8,128)(2,1)S(1)}, bf16[4,16,128]{2,1,0:T(8,128)(2,1)S(1)}, u32[]{:S(2)}, u32[]{:S(2)}) collective-permute-start(bf16[4,16,128]{2,1,0:T(8,128)(2,1)S(1)} %get-tuple-element.23), channel_id=1, source_target_pairs={{0,4},{4,0},{8,12},{12,8},{16,20},{20,16},{24,28},{28,24},{1,5},{5... | collective-permute-start | bytes 49160 | tf_op jit(solution)/shard_map/ppermute | solution.py:383

commit v4 on v3

--- a/solution.py
+++ b/solution.py
@@ -19,8 +19,8 @@
 HALO_AT = 576
 U_AT = 704
 PIECES = 8
-EARLY = 3
-TAPROWS = 112
+EARLY = 5
+TAPROWS = 128
 
 
 def stack_codes():
@@ -93,10 +93,7 @@
     return jnp.where(own, columns[None], 0.0).reshape(864, 128).astype(BF16)
 
 
-def weight_table(inv, lift, conv, mix, codes):
-    taps = dot(conv, lift_blocks(lift))
-    mixed = dot(mix, lift_columns(lift, 108).astype(BF16), TN) * inv
-    weights = (taps + mixed).astype(BF16)[:, :TAPROWS]
+def weight_table(weights, codes):
     table = jnp.zeros((32, 16, STACK), F32)
     for dy in range(3):
         spread = dot(weights, selector(codes, dy))
@@ -104,35 +101,63 @@
     return table.reshape(512, STACK).astype(BF16)
 
 
-def stage_kernel(inv, lift_ref, conv_ref, mix_ref, codes_ref, psi_ref, table_ref, *rest):
-    pieces, sems = rest[:-1], rest[-1]
-    count = psi_ref.shape[0] // PIECES
-    copies = [
-        pltpu.make_async_copy(psi_ref.at[pl.ds(k * count, count)], piece, sems.at[k])
-        for k, piece in enumerate(pieces)
-    ]
-    for item in copies:
-        item.start()
-    table_ref[...] = weight_table(inv, lift_ref[...], conv_ref[0], mix_ref[0], codes_ref[...])
-    for item in copies:
-        item.wait()
-
-
-def project_kernel(parts, micro_ref, phi_ref, out_ref, fields_ref, basis_ref, sums, field_sem, sems):
+def stage_kernel(inv, lift_ref, conv_ref, mix_ref, weights_ref, pairs_ref, taps_ref, owned_ref):
+    lift, conv, mix = lift_ref[...], conv_ref[0], mix_ref[0]
+    blocks = lift_blocks(lift)
+    taps_ref[...] = blocks
+    own_lift = lift_columns(lift, 108)
+    mixed = dot(mix, own_lift.astype(BF16), TN) * inv
+    weights_ref[...] = (dot(conv, blocks) + mixed).astype(BF16)
+    eye = ones_where(iota((32, 32), 0) == iota((32, 32), 1))
+    turned = (dot(eye, mix, NT) * inv).astype(BF16)
+    pairs = jnp.concatenate([conv, turned], axis=1)
+    pairs_ref[...] = jnp.concatenate([pairs, pairs], axis=0)
+    rep = lax.axis_index("rep")
+    pick = ones_where(iota((8, 32), 1) == iota((8, 32), 0) + 8 * rep)
+    mine = dot(pick, own_lift.astype(BF16))
+    owned_ref[...] = jnp.concatenate(
+        [mine if b == 0 else pltpu.roll(mine, 4 * b, 1) for b in range(4)], axis=0
+    ).astype(BF16)
+
+
+def project_kernel(parts, micro_ref, phi_ref, psi_ref, out_ref, *rest):
+    pieces, (fields_ref, basis_ref, sums, message, sems) = rest[:EARLY], rest[EARLY:]
+
     def copy(at, count, sem):
         rows = pl.ds(at, count)
         return pltpu.make_async_copy(phi_ref.at[rows], basis_ref.at[rows], sem)
 
     starts = [sum(parts[:k]) for k in range(len(parts))]
     copies = [copy(at, count, sems.at[k]) for k, (at, count) in enumerate(zip(starts, parts))]
-    own = pltpu.make_async_copy(micro_ref, fields_ref, field_sem)
+    own = pltpu.make_async_copy(micro_ref, fields_ref, sems.at[len(parts)])
     own.start()
     for item in copies:
         item.start()
+    count = psi_ref.shape[0] // PIECES
+    others = [
+        pltpu.make_async_copy(
+            psi_ref.at[pl.ds(k * count, count)], piece, sems.at[len(parts) + 2 + k]
+        )
+        for k, piece in enumerate(pieces)
+    ]
     own.wait()
     fields = jnp.concatenate([fields_ref[:, x].reshape(64, 128) for x in range(4)], axis=1)
+    me = lax.axis_index("gy")
+    upper = iota((8, 128), 0) < 4
+    edges = []
+    for row in (0, 15):
+        pick = ones_where(iota((8, 64), 1) == (iota((8, 64), 0) & 3) * 16 + row)
+        edge = dot(pick, fields)
+        halves = [
+            jnp.where(upper, edge[:, at : at + 128], edge[:, at + 128 : at + 256]) for at in (0, 256)
+        ]
+        edges.append(jnp.concatenate(halves, axis=0))
+    rims = [jnp.where(target > me, edges[1], edges[0]) for target in range(4)]
     for item, at, count in zip(copies, starts, parts):
         item.wait()
+        if at == starts[1]:
+            for other in others:
+                other.start()
         wide = count * 16
         basis = jnp.concatenate(
             [basis_ref[at : at + count, x].reshape(wide, 128) for x in range(4)], axis=1
@@ -150,23 +175,15 @@
     first_part, rest = split(sums[...].reshape(128, 128))
     total = dot(groups, first_part, NT) + dot(groups, rest, NT)
     high = total.astype(BF16).astype(F32)
-    me = lax.axis_index("gy")
-    edges = []
-    for row in (0, 15):
-        pick = ones_where(iota((8, 64), 1) == (iota((8, 64), 0) & 3) * 16 + row)
-        edge = dot(pick, fields)
-        upper = iota((8, 128), 0) < 4
-        edges.append(
-            [
-                jnp.where(upper, edge[:, at : at + 128], edge[:, at + 128 : at + 256])
-                for at in (0, 256)
-            ]
-        )
     for target in range(4):
-        rim = [jnp.where(target > me, last, first) for first, last in zip(*edges)]
-        message = jnp.concatenate([high, total - high] + rim, axis=0).astype(BF16)
-        for plane in range(out_ref.shape[0] // 4):
-            out_ref[4 * plane + target] = message
+        whole = jnp.concatenate([high, total - high, rims[target]], axis=0).astype(BF16)
+        for plane in range(message.shape[0] // 4):
+            message[4 * plane + target] = whole
+    send = pltpu.make_async_copy(message, out_ref, sems.at[len(parts) + 1])
+    send.start()
+    for other in others:
+        other.wait()
+    send.wait()
 
 
 def shift_z(values, dz):
@@ -205,43 +222,24 @@
     return jnp.concatenate(pieces, axis=1)
 
 
-def main_kernel(
-    inv,
-    parts_ref,
-    micro_ref,
-    near_ref,
-    far_ref,
-    table,
-    cot_ref,
-    lift_ref,
-    conv_ref,
-    mix_ref,
-    codes_ref,
-    *rest,
-):
+def main_kernel(parts_ref, micro_ref, near_ref, far_ref, weights_ref, pairs_ref, codes_ref, *rest):
     psi_refs = list(rest[:EARLY])
-    psi_ref = rest[EARLY]
-    (
-    out_ref,
-    send_ref,
-    stack,
-    spread,
-    pre,
-    grad,
-    corr,
-    late_ref,
-    sems,
-    ) = rest[EARLY + 1 :]
+    psi_ref, cot_ref, out_ref, send_ref = rest[EARLY : EARLY + 4]
+    table, stack, spread, pre, grad, corr, late_ref, cot, out, sems = rest[EARLY + 4 :]
     count = psi_ref.shape[0] // PIECES
+    late = PIECES - EARLY
     copies = []
-    for k in range(EARLY, PIECES):
-        piece = late_ref.at[pl.ds((k - EARLY) * count, count)]
+    for k in range(late):
+        piece = late_ref.at[pl.ds(k * count, count)]
         copies.append(
-            pltpu.make_async_copy(psi_ref.at[pl.ds(k * count, count)], piece, sems.at[k - EARLY])
+            pltpu.make_async_copy(psi_ref.at[pl.ds((EARLY + k) * count, count)], piece, sems.at[k])
         )
-        copies[-1].start()
         psi_refs.append(piece)
+    cot_copy = pltpu.make_async_copy(cot_ref, cot, sems.at[late])
+    for item in copies + [cot_copy]:
+        item.start()
     codes = codes_ref[...]
+    table[...] = weight_table(weights_ref[...], codes)
     even = lax.axis_index("gx") % 2 == 0
     near, far = near_ref[...], far_ref[...]
     ends = jnp.where(even, far, near), jnp.where(even, near, far)
@@ -289,6 +287,8 @@
         stack[U_AT:STACK, 256 * pair : 256 * pair + 256] = (field[:64] + field[64:]).astype(BF16)
     pre[...] = dot(table[...], stack[...])
 
+    cot_copy.wait()
+
     def activate(o, carry):
         rows = pl.ds(pl.multiple_of(o * 16, 16), 16)
         for x in range(4):
@@ -296,12 +296,14 @@
             values = pre[rows, lanes]
             cumulative = 0.5 * (1.0 + lax.erf(values * (1.0 / math.sqrt(2.0))))
             density = jnp.exp(-0.5 * values * values) * (1.0 / math.sqrt(2.0 * math.pi))
-            out_ref[0, o, x] = values * cumulative
+            out[0, o, x] = values * cumulative
             slope = cumulative + values * density
-            grad[rows, lanes] = (cot_ref[0, o, x].astype(F32) * slope).astype(BF16)
+            grad[rows, lanes] = (cot[0, o, x].astype(F32) * slope).astype(BF16)
         return carry
 
     lax.fori_loop(0, 32, activate, 0, unroll=2)
+    out_copy = pltpu.make_async_copy(out, out_ref, sems.at[late + 1])
+    out_copy.start()
     corr[...] = dot(grad[...], stack[...], NT)
     bands = [band(codes, dy) for dy in range(3)]
     moments = jnp.zeros((32, TAPROWS), F32)
@@ -312,47 +314,47 @@
             reduced[dy].append(jnp.sum(jnp.where(bands[dy], block, 0.0), axis=0, keepdims=True))
     for dy in range(3):
         moments = moments + dot_split(jnp.concatenate(reduced[dy], axis=0), selector(codes, dy), NT)
-    lift = lift_ref[...]
-    high, low = split(moments)
-    lanes112 = iota((112, 128), 1)
-    rows112 = iota((112, 128), 0)
-    conv = conv_ref[0]
-    products = dot(conv, high, TN) + dot(conv, low, TN)
-    products = products.reshape(27, 32, TAPROWS)
-    own = iota((27, 1, TAPROWS), 0) == (iota((27, 1, TAPROWS), 2) >> 2)
-    summed = jnp.sum(jnp.where(own, products, 0.0), axis=0)
-    to_lane = ones_where(((rows112 & 3) == lanes112 - 124) & (rows112 < 108))
-    lift_term = dot_split(summed, to_lane)
-    last = ones_where((rows112 - 108 == lanes112 - 124) & (rows112 >= 108))
-    coupled = dot_split(moments, last)
-    chigh, clow = split(coupled)
-    lift_term = lift_term + inv * (dot(mix_ref[0], chigh) + dot(mix_ref[0], clow))
-    keep = ones_where((rows112 == lanes112) & (rows112 < 108))
-    kept = dot_split(moments, keep)
-    block = kept + lift_term
+    turned_high, turned_low = split(moments.T)
+    turned = jnp.concatenate([turned_high, turned_low], axis=1)
+    products = dot(turned, pairs_ref[...])
+    own = (iota((TAPROWS, 896), 0) >> 2) == (iota((TAPROWS, 896), 1) >> 5)
+    folded = jnp.sum(jnp.where(own, products, 0.0).reshape(TAPROWS // 8, 8, 896), axis=0)
+    lifted = folded[:, 0:128]
+    for at in range(128, 896, 128):
+        lifted = lifted + folded[:, at : at + 128]
+    lifted = lifted + pltpu.roll(lifted, 64, 1)
+    lifted = lifted + pltpu.roll(lifted, 32, 1)
+    lifted = lifted + pltpu.roll(lifted, 4, 0)
+    lanes = iota((8, 128), 1)
     shared = jnp.zeros((8, 128), F32)
     for b in range(4):
-        pick = ones_where((rows112 - 108 == lanes112 - 108 - 4 * b) & (rows112 >= 108))
-        shared = shared + dot_split(moments[8 * b : 8 * b + 8], pick)
+        rows = moments[8 * b : 8 * b + 8]
+        rows = rows if b == 0 else pltpu.roll(rows, 4 * b, 1)
+        shared = jnp.where((lanes >= 108 + 4 * b) & (lanes < 112 + 4 * b), rows, shared)
+    upper = iota((8, 128), 0) < 4
     for k in range(4):
-        message = (block[8 * k : 8 * k + 8] + shared).astype(send_ref.dtype)
+        first = pltpu.roll(lifted, 124 - 8 * k, 1)
+        second = pltpu.roll(lifted, 120 - 8 * k, 1)
+        columns = jnp.where(upper, first, second)
+        message = jnp.where(lanes < 108, moments[8 * k : 8 * k + 8], shared)
+        message = jnp.where(lanes >= 124, columns, message).astype(send_ref.dtype)
         send_ref[k] = jnp.broadcast_to(message[None], send_ref.shape[1:])
-
-
-def finish_kernel(scale, inv, recv_ref, lift_ref, conv_out, mix_out, lift_out):
-    lift = lift_ref[...]
-    rep = lax.axis_index("rep")
+    out_copy.wait()
+
+
+def finish_kernel(scale, inv, recv_ref, taps_ref, owned_ref, conv_out, mix_out, lift_out):
     flat = recv_ref[...].reshape(1024, 128)
     total = dot(ones_where(iota((8, 1024), 0) == (iota((8, 1024), 1) & 7)), flat)
-    conv_out[0] = dot_split(total, lift_blocks(lift), NT) * scale
-    owned = ones_where(iota((8, 32), 1) == iota((8, 32), 0) + 8 * rep)
+    high, low = split(total)
+    both = jnp.concatenate([high.astype(F32), low.astype(F32)], axis=0).astype(BF16)
+    conv = dot(both, taps_ref[...], NT)
+    conv_out[0] = (conv[:8] + conv[8:]) * scale
+    mixed = dot(owned_ref[...], both, NT) * (scale * inv)
     for b in range(4):
-        left = dot(owned, lift_columns(lift, 108 + 4 * b).astype(BF16)).astype(BF16)
-        high, low = split(total)
-        mix_out[0, :, 8 * b : 8 * b + 8] = (dot(left, high, NT) + dot(left, low, NT)) * (scale * inv)
-    pick = ones_where(iota((4, 128), 1) - 124 == iota((4, 128), 0))
-    high, low = split(total)
-    lift_out[...] = (dot(pick, high, NT) + dot(pick, low, NT)) * scale
+        rows = mixed[8 * b : 8 * b + 8]
+        mix_out[0, :, 8 * b : 8 * b + 8] = rows[:, :8] + rows[:, 8:]
+    lift_out[:, 0:4] = total[0:4, 124:128] * scale
+    lift_out[:, 4:8] = total[4:8, 124:128] * scale
 
 
 VMEM = pl.BlockSpec(memory_space=pltpu.VMEM)
@@ -383,64 +385,69 @@
     near = lax.ppermute(jnp.where(even, last, first), "gx", on_chip)
     far = lax.ppermute(jnp.where(even, first, last), "gx", off_chip)
 
-    rows = (rank // 2, rank // 4, rank // 4)
-    parts = pl.pallas_call(
+    rows = (rank // 4, 3 * rank // 8, 3 * rank // 8)
+    parts, *pieces = pl.pallas_call(
         functools.partial(project_kernel, rows),
-        in_specs=[HBM] * 2,
-        out_specs=VMEM,
-        out_shape=jax.ShapeDtypeStruct((gx * gy, 32, 128), BF16),
+        in_specs=[HBM] * 3,
+        out_specs=[HBM] + [VMEM] * EARLY,
+        out_shape=[jax.ShapeDtypeStruct((gx * gy, 32, 128), BF16)]
+        + [jax.ShapeDtypeStruct((rank // PIECES,) + psi.shape[1:], BF16)] * EARLY,
         scratch_shapes=[
             pltpu.VMEM(micro.shape, BF16),
             pltpu.VMEM(phi.shape, BF16),
             pltpu.VMEM((4, 32, 128), F32),
-            pltpu.SemaphoreType.DMA,
-            pltpu.SemaphoreType.DMA((len(rows),)),
+            pltpu.VMEM((gx * gy, 32, 128), BF16),
+            pltpu.SemaphoreType.DMA((len(rows) + 2 + EARLY,)),
         ],
         compiler_params=pltpu.CompilerParams(vmem_limit_bytes=16 * 1024 * 1024),
         name="project",
-    )(in_hbm(micro), in_hbm(phi))
+    )(in_hbm(micro), in_hbm(phi), in_hbm(psi))
 
     gathered = lax.all_to_all(parts, ("gx", "gy"), 0, 0)
 
-    table, *pieces = pl.pallas_call(
+    weights, pairs, taps, owned = pl.pallas_call(
         functools.partial(stage_kernel, inv),
-        in_specs=[VMEM] * 4 + [HBM],
-        out_specs=[VMEM] * (1 + EARLY),
-        out_shape=[jax.ShapeDtypeStruct((512, STACK), BF16)]
-        + [jax.ShapeDtypeStruct((rank // PIECES,) + psi.shape[1:], BF16)] * EARLY,
-        scratch_shapes=[pltpu.SemaphoreType.DMA((EARLY,))],
+        in_specs=[VMEM] * 3,
+        out_specs=[VMEM] * 4,
+        out_shape=[
+            jax.ShapeDtypeStruct((32, TAPROWS), BF16),
+            jax.ShapeDtypeStruct((64, 896), BF16),
+            jax.ShapeDtypeStruct((864, 128), BF16),
+            jax.ShapeDtypeStruct((32, 128), BF16),
+        ],
         compiler_params=pltpu.CompilerParams(vmem_limit_bytes=8 * 1024 * 1024),
         cost_estimate=pl.CostEstimate(flops=2_000_000_000, bytes_accessed=4_000_000, transcendentals=0),
         name="stage",
-    )(lift_w, conv_w, mix_w, codes, in_hbm(psi))
-
+    )(lift_w, conv_w, mix_w)
+
+    out_shape = jax.ShapeDtypeStruct((1, 32, 4, 16, 128), F32)
     out_field, send = pl.pallas_call(
-        functools.partial(main_kernel, inv),
-        in_specs=[VMEM] * (10 + EARLY) + [HBM],
-        out_specs=[VMEM] * 2,
-        out_shape=[
-            jax.ShapeDtypeStruct((1, 32, 4, 16, 128), F32),
-            jax.ShapeDtypeStruct((reps, gx * gy, 8, 128), BF16),
-        ],
+        main_kernel,
+        in_specs=[VMEM] * (7 + EARLY) + [HBM] * 2,
+        out_specs=[HBM, VMEM],
+        out_shape=[out_shape, jax.ShapeDtypeStruct((reps, gx * gy, 8, 128), BF16)],
         scratch_shapes=[
+            pltpu.VMEM((512, STACK), BF16),
             pltpu.VMEM((STACK, 512), BF16),
             pltpu.VMEM((128, 4096), BF16),
             pltpu.VMEM((512, 512), F32),
             pltpu.VMEM((512, 512), BF16),
             pltpu.VMEM((512, STACK), F32),
             pltpu.VMEM((rank // PIECES * (PIECES - EARLY),) + psi.shape[1:], BF16),
-            pltpu.SemaphoreType.DMA((PIECES - EARLY,)),
+            pltpu.VMEM(cotangent.shape, BF16),
+            pltpu.VMEM(out_shape.shape, F32),
+            pltpu.SemaphoreType.DMA((PIECES - EARLY + 2,)),
         ],
         compiler_params=LIMIT,
         cost_estimate=pl.CostEstimate(flops=4_000_000_000, bytes_accessed=6_000_000, transcendentals=500_000),
         name="layer",
-    )(gathered, micro, near, far, table, cotangent, lift_w, conv_w, mix_w, codes, *pieces, in_hbm(psi))
+    )(gathered, micro, near, far, weights, pairs, codes, *pieces, in_hbm(psi), in_hbm(cotangent))
 
     received = lax.all_to_all(send.reshape(reps * gx * gy, 8, 128), ("rep", "gx", "gy"), 0, 0)
 
     grads = pl.pallas_call(
         functools.partial(finish_kernel, scale, inv),
-        in_specs=[VMEM] * 2,
+        in_specs=[VMEM] * 3,
         out_specs=[VMEM] * 3,
         out_shape=[
             jax.ShapeDtypeStruct((1, 8, 864), F32),
@@ -449,7 +456,7 @@
         ],
         compiler_params=LIMIT,
         name="finish",
-    )(received, lift_w)
+    )(received, taps, owned)
     return (out_field, *grads)
 
 

time: 49.9 us -> 48.2 us (0.966)
  Pallas kernels: 14.8 us -> 11.9 us
  waiting for transfers between devices: 3.42 us -> 4.75 us
    pallas_call x2, Pallas kernels: 8.55 us -> 6.88 us  [the longest x1 6.47 us: on_device(): pl.pallas_call(main_kernel, in_specs=[VMEM] * (7 + EARLY) + [HBM] * 2, ou...]
    ppermute x1, waiting for transfers between devices: 0.07 us -> 1.4 us  [on_device(): far = lax.ppermute(jnp.where(even, first, last), 'gx', off_chip)]
    pallas_call x1, Pallas kernels: 1.68 us -> 1.03 us  [on_device(): pl.pallas_call(functools.partial(finish_kernel, scale, inv), in_specs=[VM...]
    pallas_call x1, Pallas kernels: 4.59 us -> 3.98 us  [on_device(): pl.pallas_call(functools.partial(project_kernel, rows), in_specs=[HBM] *...]
  transfers between devices with their start and end apart: 3 -> 3, of which waited for: 2 -> 2; matrix products, arithmetic and copies ran while one was open for 0% -> 0% of each run, Pallas kernels for 3% -> 1%
where the time goes in v4:
time: 48.2 us; the launch traced here: 47.9 us
  blocking collectives  18.2 us (38%)
  starting transfers between devices  12.2 us (25%)
  Pallas kernels  11.9 us (25%)
  waiting for transfers between devices  4.75 us (10%)
  between operations  0.78 us (2%)
    all_to_all x1, blocking collectives, on_device(): lax.all_to_all(send.reshape(reps * gx * gy, 8, 128), ('rep', 'gx', 'gy'),...  18.2 us
    all_to_all x1, starting transfers between devices, on_device(): gathered = lax.all_to_all(parts, ('gx', 'gy'), 0, 0)  8.6 us
    pallas_call x1, Pallas kernels, on_device(): pl.pallas_call(main_kernel, in_specs=[VMEM] * (7 + EARLY) + [HBM] * 2, ou...  6.47 us
    pallas_call x1, Pallas kernels, on_device(): pl.pallas_call(functools.partial(project_kernel, rows), in_specs=[HBM] *...  3.98 us
    ppermute x1, starting transfers between devices, on_device(): far = lax.ppermute(jnp.where(even, first, last), 'gx', off_chip)  3.54 us
    all_to_all x1, waiting for transfers between devices, on_device(): gathered = lax.all_to_all(parts, ('gx', 'gy'), 0, 0)  3.35 us
    ppermute x1, waiting for transfers between devices, on_device(): far = lax.ppermute(jnp.where(even, first, last), 'gx', off_chip)  1.4 us
    pallas_call x1, Pallas kernels, on_device(): pl.pallas_call(functools.partial(finish_kernel, scale, inv), in_specs=[VM...  1.03 us
  transfers between devices with their start and end apart: 3, of which 2 were waited for; matrix products, arithmetic and copies ran while one was open for 0% of the time, Pallas kernels for 1%

profile of v4, /device:TPU:1, one launch (start us, length us, event | category | flops | bytes accessed | tf_op | source)
XLA Modules:
  0.0 47.9 jit_solution(5786761513742359267)
XLA Ops:
  0.6 0.0 copy-start
  0.6 0.0 copy-start.1
  0.7 0.0 copy-start.2
  0.7 0.0 copy-start.3
  0.7 4.0 %project.1 = (bf16[32,32,128]{2,1,0:T(8,128)(2,1)}, bf16[32,4,16,128]{3,2,1,0:T(8,128)(2,1)S(1)}, bf16[32,4,16,128]{3,2,1,0:T(8,128)(2,1)S(1)}, bf16[32,4,16,128...) custom-call(bf16[4,4,16,128]{3,2,1,0:T(8,128)(2,1)} %bitcast.9, ...), custom_call_target="tpu_custom_call" | custom-call | tf_op jit(solution)/shard_map/project/pallas_call | solution.py:389
  4.7 0.0 copy-start.4
  4.7 8.6 %all-to-all-start = ((bf16[32,32,128]{2,1,0:T(8,128)(2,1)}), bf16[32,32,128]{2,1,0:T(8,128)(2,1)S(1)}, u32[]{:S(2)}, u32[]{:S(2)}) async-start(bf16[32,32,128]{2,1,0:T(8,128)(2,1)} %get-tuple-element.19), calls=%async_computation | async-start | bytes 524288 | tf_op jit(solution)/shard_map/all_to_all | solution.py:406
  13.3 0.0 copy-done
  13.3 3.5 %collective-permute-start.1 = (bf16[4,16,128]{2,1,0:T(8,128)(2,1)S(1)}, bf16[4,16,128]{2,1,0:T(8,128)(2,1)S(1)}, u32[]{:S(2)}, u32[]{:S(2)}) collective-permute-start(bf16[4,16,128]{2,1,0:T(8,128)(2,1)S(1)} %get-tuple-element.34), channel_id=1, source_target_pairs={{4,8},{8,4},{12,16},{16,12},{20,24},{24,20},{5,9},{9,5},{13,17},{1... | collective-permute-start | bytes 49160 | tf_op jit(solution)/shard_map/ppermute | solution.py:386
  16.9 0.1 collective-permute-start
  17.0 0.0 copy-done.1
  17.0 0.0 copy-done.2
  17.0 0.0 copy-done.3
  17.0 0.4 stage.1
  17.4 1.4 %collective-permute-done.1.far_ref = bf16[4,16,128]{2,1,0:T(8,128)(2,1)S(1)} collective-permute-done((bf16[4,16,128]{2,1,0:T(8,128)(2,1)S(1)}, bf16[4,16,128]{2,1,0:T(8,128)(2,1)S(1)}, u32[]{:S(2)}, u32[]{:S(2)}) %collective-permute-start.1) | collective-permute-done | bytes 16416 | tf_op jit(solution)/shard_map/ppermute | solution.py:386
  18.8 0.0 collective-permute-done.near_ref
  18.8 3.3 %all-to-all-done.parts_ref = bf16[32,32,128]{2,1,0:T(8,128)(2,1)S(1)} async-done(((bf16[32,32,128]{2,1,0:T(8,128)(2,1)}), bf16[32,32,128]{2,1,0:T(8,128)(2,1)S(1)}, u32[]{:S(2)}, u32[]{:S(2)}) %all-to-all-start) | async-done | bytes 262176 | tf_op jit(solution)/shard_map/all_to_all | solution.py:406
  22.2 0.0 copy-done.4
  22.2 6.5 %layer.1 = (f32[1,32,4,16,128]{4,3,2,1,0:T(8,128)}, bf16[4,32,8,128]{3,2,1,0:T(8,128)(2,1)S(1)}) custom-call(bf16[32,32,128]{2,1,0:T(8,128)(2,1)S(1)} %all-to-all-done.parts_ref, bf16[4,4,16,128]{3,2,1,0:T(8,128)(2,1)S(1)} %bitcast.10, bf16[4,16,128]{2,1,0:T(8,128)(2,1)S(1)} %collective-permute-done.near_ref, ...), custom_call_target="tpu_custom_call" | custom-call | flops 4000000000 | bytes 6000000 | tf_op jit(solution)/shard_map/layer/pallas_call | solution.py:424
  28.7 18.2 %all_to_all.10.recv_ref = bf16[128,8,128]{2,1,0:T(8,128)(2,1)S(1)} all-to-all(bf16[128,8,128]{2,1,0:T(8,128)(2,1)S(1)} %bitcast.11), channel_id=1, replica_groups=mesh['rep'=4,'gx'=8,'gy'=4] {'rep','gx','gy'}, dimensions={0} | all-to-all | bytes 524288 | tf_op jit(solution)/shard_map/all_to_all | solution.py:446
  46.8 1.0 %finish.1 = (f32[1,8,864]{2,1,0:T(8,128)}, f32[1,8,32]{2,1,0:T(8,128)}, f32[4,8]{1,0:T(4,128)}) custom-call(bf16[128,8,128]{2,1,0:T(8,128)(2,1)S(1)} %all_to_all.10.recv_ref, bf16[864,128]{1,0:T(8,128)(2,1)S(1)} %get-tuple-element.29.taps_ref, bf16[32,128]{1,0:T(8,128)(2,1)S(1)} %get-tuple-element.30.owned_ref), custom_call_target="tpu_custom_call" | custom-call | tf_op jit(solution)/shard_map/finish/pallas_call | solution.py:448
  (2 shorter events, 0.0 us)
Async XLA Ops:
  0.6 12.7 %copy-start = (bf16[1,4,4,16,128]{4,3,2,1,0:T(8,128)(2,1)S(1)}, bf16[1,4,4,16,128]{4,3,2,1,0:T(8,128)(2,1)}, u32[]{:S(2)}) copy-start(bf16[1,4,4,16,128]{4,3,2,1,0:T(8,128)(2,1)} %param.8) | copy-start | bytes 196612
  0.6 16.3 %copy-start.1 = (bf16[1,32,864]{2,1,0:T(8,128)(2,1)S(1)}, bf16[1,32,864]{2,1,0:T(8,128)(2,1)}, u32[]{:S(2)}) copy-start(bf16[1,32,864]{2,1,0:T(8,128)(2,1)} %conv_ref.1) | copy-start | bytes 165892
  0.7 16.3 %copy-start.2 = (bf16[1,32,32]{2,1,0:T(8,128)(2,1)S(1)}, bf16[1,32,32]{2,1,0:T(8,128)(2,1)}, u32[]{:S(2)}) copy-start(bf16[1,32,32]{2,1,0:T(8,128)(2,1)} %mix_ref.1) | copy-start | bytes 6148
  0.7 16.3 %copy-start.3 = (bf16[4,32]{1,0:T(4,128)(2,1)S(1)}, bf16[4,32]{1,0:T(4,128)(2,1)}, u32[]{:S(2)}) copy-start(bf16[4,32]{1,0:T(4,128)(2,1)} %lift_ref.1) | copy-start | bytes 772
  4.7 17.5 %copy-start.4 = (s32[8,768]{1,0:T(8,128)S(1)}, s32[8,768]{1,0:T(8,128)}, u32[]{:S(2)}) copy-start(s32[8,768]{1,0:T(8,128)} %constant.22.clone.codes_ref) | copy-start | bytes 73732
  4.7 17.5 %all-to-all-start = ((bf16[32,32,128]{2,1,0:T(8,128)(2,1)}), bf16[32,32,128]{2,1,0:T(8,128)(2,1)S(1)}, u32[]{:S(2)}, u32[]{:S(2)}) async-start(bf16[32,32,128]{2,1,0:T(8,128)(2,1)} %get-tuple-element.19), calls=%async_computation | async-start | bytes 524288 | tf_op jit(solution)/shard_map/all_to_all | solution.py:406
  13.3 5.5 %collective-permute-start.1 = (bf16[4,16,128]{2,1,0:T(8,128)(2,1)S(1)}, bf16[4,16,128]{2,1,0:T(8,128)(2,1)S(1)}, u32[]{:S(2)}, u32[]{:S(2)}) collective-permute-start(bf16[4,16,128]{2,1,0:T(8,128)(2,1)S(1)} %get-tuple-element.34), channel_id=1, source_target_pairs={{4,8},{8,4},{12,16},{16,12},{20,24},{24,20},{5,9},{9,5},{13,17},{1... | collective-permute-start | bytes 49160 | tf_op jit(solution)/shard_map/ppermute | solution.py:386
  16.9 1.9 %collective-permute-start = (bf16[4,16,128]{2,1,0:T(8,128)(2,1)S(1)}, bf16[4,16,128]{2,1,0:T(8,128)(2,1)S(1)}, u32[]{:S(2)}, u32[]{:S(2)}) collective-permute-start(bf16[4,16,128]{2,1,0:T(8,128)(2,1)S(1)} %get-tuple-element.35), channel_id=1, source_target_pairs={{0,4},{4,0},{8,12},{12,8},{16,20},{20,16},{24,28},{28,24},{1,5},{5... | collective-permute-start | bytes 49160 | tf_op jit(solution)/shard_map/ppermute | solution.py:385

commit v5 on v4

--- a/solution.py
+++ b/solution.py
@@ -21,6 +21,9 @@
 PIECES = 8
 EARLY = 5
 TAPROWS = 128
+
+
+ROLLED = HALO_AT
 
 
 def stack_codes():
@@ -36,14 +39,18 @@
             row = 16 if side else -1
         elif lane >= U_AT:
             j, row = divmod(lane - U_AT, 16)
-            codes[1, lane] = 108 + j
-            codes[3, lane] = row
+            codes[1, lane] = codes[4, lane] = 108 + j
+            codes[3, lane], codes[5, lane] = row, 0
             continue
         else:
             continue
         for dy in range(3):
             codes[dy, lane] = (9 * dx + 3 * dy + dz) * 4 + j
-        codes[3, lane] = row
+        codes[3, lane], codes[5, lane] = row, 1
+        if lane >= HALO_AT:
+            codes[4, lane] = codes[2 if side else 0, lane]
+        elif 7 <= row < 10:
+            codes[4, lane] = codes[row - 7, lane]
     return codes
 
 
@@ -93,12 +100,19 @@
     return jnp.where(own, columns[None], 0.0).reshape(864, 128).astype(BF16)
 
 
-def weight_table(weights, codes):
-    table = jnp.zeros((32, 16, STACK), F32)
-    for dy in range(3):
-        spread = dot(weights, selector(codes, dy))
-        table = jnp.where(band(codes, dy)[None], spread[:, None, :], table)
-    return table.reshape(512, STACK).astype(BF16)
+def weight_table(weights, codes, table):
+    spread = dot(weights, selector(codes, 4))
+    valid = jnp.abs(codes[3:4, :] - iota((16, STACK), 0)) <= codes[5:6, :]
+    for o in range(32):
+        for at in range(0, STACK, 128):
+            lanes = slice(at, at + 128)
+            whole = jnp.broadcast_to(spread[o : o + 1, lanes], (16, 128))
+            if at < ROLLED:
+                rolled = pltpu.roll(whole, 120, 1, stride=1, stride_axis=0)
+                if at + 128 > ROLLED:
+                    rolled = jnp.where(iota((16, 128), 1) < ROLLED - at, rolled, whole)
+                whole = rolled
+            table[16 * o : 16 * o + 16, lanes] = jnp.where(valid[:, lanes], whole, 0.0).astype(BF16)
 
 
 def stage_kernel(inv, lift_ref, conv_ref, mix_ref, weights_ref, pairs_ref, taps_ref, owned_ref):
@@ -239,7 +253,7 @@
     for item in copies + [cot_copy]:
         item.start()
     codes = codes_ref[...]
-    table[...] = weight_table(weights_ref[...], codes)
+    weight_table(weights_ref[...], codes, table)
     even = lax.axis_index("gx") % 2 == 0
     near, far = near_ref[...], far_ref[...]
     ends = jnp.where(even, far, near), jnp.where(even, near, far)
@@ -285,26 +299,32 @@
                 fields[pair] = fields[pair] + dot(spread[:, 16 * at : 16 * at + 256], basis)
     for pair, field in enumerate(fields):
         stack[U_AT:STACK, 256 * pair : 256 * pair + 256] = (field[:64] + field[64:]).astype(BF16)
-    pre[...] = dot(table[...], stack[...])
-
     cot_copy.wait()
-
-    def activate(o, carry):
-        rows = pl.ds(pl.multiple_of(o * 16, 16), 16)
-        for x in range(4):
-            lanes = slice(128 * x, 128 * x + 128)
-            values = pre[rows, lanes]
-            cumulative = 0.5 * (1.0 + lax.erf(values * (1.0 / math.sqrt(2.0))))
-            density = jnp.exp(-0.5 * values * values) * (1.0 / math.sqrt(2.0 * math.pi))
-            out[0, o, x] = values * cumulative
-            slope = cumulative + values * density
-            grad[rows, lanes] = (cot[0, o, x].astype(F32) * slope).astype(BF16)
-        return carry
-
-    lax.fori_loop(0, 32, activate, 0, unroll=2)
-    out_copy = pltpu.make_async_copy(out, out_ref, sems.at[late + 1])
-    out_copy.start()
-    corr[...] = dot(grad[...], stack[...], NT)
+    out_copies = []
+    for pair in range(2):
+        half = slice(256 * pair, 256 * pair + 256)
+        pre[:, half] = dot(table[...], stack[:, half])
+        for o in range(32):
+            rows = slice(16 * o, 16 * o + 16)
+            for x in (2 * pair, 2 * pair + 1):
+                lanes = slice(128 * x, 128 * x + 128)
+                values = pre[rows, lanes]
+                cumulative = 0.5 * (1.0 + lax.erf(values * (1.0 / math.sqrt(2.0))))
+                density = jnp.exp(-0.5 * values * values) * (1.0 / math.sqrt(2.0 * math.pi))
+                out[0, o, x] = values * cumulative
+                slope = cumulative + values * density
+                grad[rows, lanes] = (cot[0, o, x].astype(F32) * slope).astype(BF16)
+        out_copies.append(
+            pltpu.make_async_copy(
+                out.at[:, :, pl.ds(2 * pair, 2)], out_ref.at[:, :, pl.ds(2 * pair, 2)], sems.at[late + 1 + pair]
+            )
+        )
+        out_copies[-1].start()
+        product = dot(grad[:, half], stack[:, half], NT)
+        if pair == 0:
+            corr[...] = product
+        else:
+            corr[...] += product
     bands = [band(codes, dy) for dy in range(3)]
     moments = jnp.zeros((32, TAPROWS), F32)
     reduced = [[], [], []]
@@ -339,7 +359,8 @@
         message = jnp.where(lanes < 108, moments[8 * k : 8 * k + 8], shared)
         message = jnp.where(lanes >= 124, columns, message).astype(send_ref.dtype)
         send_ref[k] = jnp.broadcast_to(message[None], send_ref.shape[1:])
-    out_copy.wait()
+    for item in out_copies:
+        item.wait()
 
 
 def finish_kernel(scale, inv, recv_ref, taps_ref, owned_ref, conv_out, mix_out, lift_out):
@@ -436,7 +457,7 @@
             pltpu.VMEM((rank // PIECES * (PIECES - EARLY),) + psi.shape[1:], BF16),
             pltpu.VMEM(cotangent.shape, BF16),
             pltpu.VMEM(out_shape.shape, F32),
-            pltpu.SemaphoreType.DMA((PIECES - EARLY + 2,)),
+            pltpu.SemaphoreType.DMA((PIECES - EARLY + 3,)),
         ],
         compiler_params=LIMIT,
         cost_estimate=pl.CostEstimate(flops=4_000_000_000, bytes_accessed=6_000_000, transcendentals=500_000),

time: 48.2 us -> 47.5 us (0.985)
  Pallas kernels: 11.9 us -> 11.2 us
    pallas_call x1, Pallas kernels: 6.47 us -> 5.74 us  [on_device(): pl.pallas_call(main_kernel, in_specs=[VMEM] * (7 + EARLY) + [HBM] * 2, ou...]
where the time goes in v5:
time: 47.5 us; the launch traced here: 47.1 us
  blocking collectives  18.2 us (38%)
  starting transfers between devices  12.2 us (26%)
  Pallas kernels  11.2 us (24%)
  waiting for transfers between devices  4.75 us (10%)
  between operations  0.78 us (2%)
    all_to_all x1, blocking collectives, on_device(): lax.all_to_all(send.reshape(reps * gx * gy, 8, 128), ('rep', 'gx', 'gy'),...  18.2 us
    all_to_all x1, starting transfers between devices, on_device(): gathered = lax.all_to_all(parts, ('gx', 'gy'), 0, 0)  8.6 us
    pallas_call x1, Pallas kernels, on_device(): pl.pallas_call(main_kernel, in_specs=[VMEM] * (7 + EARLY) + [HBM] * 2, ou...  5.74 us
    pallas_call x1, Pallas kernels, on_device(): pl.pallas_call(functools.partial(project_kernel, rows), in_specs=[HBM] *...  3.98 us
    ppermute x1, starting transfers between devices, on_device(): far = lax.ppermute(jnp.where(even, first, last), 'gx', off_chip)  3.54 us
    all_to_all x1, waiting for transfers between devices, on_device(): gathered = lax.all_to_all(parts, ('gx', 'gy'), 0, 0)  3.35 us
    ppermute x1, waiting for transfers between devices, on_device(): far = lax.ppermute(jnp.where(even, first, last), 'gx', off_chip)  1.4 us
    pallas_call x1, Pallas kernels, on_device(): pl.pallas_call(functools.partial(finish_kernel, scale, inv), in_specs=[VM...  1.03 us
  transfers between devices with their start and end apart: 3, of which 2 were waited for; matrix products, arithmetic and copies ran while one was open for 0% of the time, Pallas kernels for 1%

profile of v5, /device:TPU:1, one launch (start us, length us, event | category | flops | bytes accessed | tf_op | source)
XLA Modules:
  0.0 47.1 jit_solution(2612107238541742395)
XLA Ops:
  0.6 0.0 copy-start
  0.6 0.0 copy-start.1
  0.7 0.0 copy-start.2
  0.7 0.0 copy-start.3
  0.7 4.0 %project.1 = (bf16[32,32,128]{2,1,0:T(8,128)(2,1)}, bf16[32,4,16,128]{3,2,1,0:T(8,128)(2,1)S(1)}, bf16[32,4,16,128]{3,2,1,0:T(8,128)(2,1)S(1)}, bf16[32,4,16,128...) custom-call(bf16[4,4,16,128]{3,2,1,0:T(8,128)(2,1)} %bitcast.9, ...), custom_call_target="tpu_custom_call" | custom-call | tf_op jit(solution)/shard_map/project/pallas_call | solution.py:410
  4.7 0.0 copy-start.4
  4.7 8.6 %all-to-all-start = ((bf16[32,32,128]{2,1,0:T(8,128)(2,1)}), bf16[32,32,128]{2,1,0:T(8,128)(2,1)S(1)}, u32[]{:S(2)}, u32[]{:S(2)}) async-start(bf16[32,32,128]{2,1,0:T(8,128)(2,1)} %get-tuple-element.19), calls=%async_computation | async-start | bytes 524288 | tf_op jit(solution)/shard_map/all_to_all | solution.py:427
  13.3 0.0 copy-done
  13.3 3.5 %collective-permute-start.1 = (bf16[4,16,128]{2,1,0:T(8,128)(2,1)S(1)}, bf16[4,16,128]{2,1,0:T(8,128)(2,1)S(1)}, u32[]{:S(2)}, u32[]{:S(2)}) collective-permute-start(bf16[4,16,128]{2,1,0:T(8,128)(2,1)S(1)} %get-tuple-element.34), channel_id=1, source_target_pairs={{4,8},{8,4},{12,16},{16,12},{20,24},{24,20},{5,9},{9,5},{13,17},{1... | collective-permute-start | bytes 49160 | tf_op jit(solution)/shard_map/ppermute | solution.py:407
  16.9 0.1 collective-permute-start
  17.0 0.0 copy-done.1
  17.0 0.0 copy-done.2
  17.0 0.0 copy-done.3
  17.0 0.4 stage.1
  17.4 1.4 %collective-permute-done.1.far_ref = bf16[4,16,128]{2,1,0:T(8,128)(2,1)S(1)} collective-permute-done((bf16[4,16,128]{2,1,0:T(8,128)(2,1)S(1)}, bf16[4,16,128]{2,1,0:T(8,128)(2,1)S(1)}, u32[]{:S(2)}, u32[]{:S(2)}) %collective-permute-start.1) | collective-permute-done | bytes 16416 | tf_op jit(solution)/shard_map/ppermute | solution.py:407
  18.8 0.0 collective-permute-done.near_ref
  18.8 3.3 %all-to-all-done.parts_ref = bf16[32,32,128]{2,1,0:T(8,128)(2,1)S(1)} async-done(((bf16[32,32,128]{2,1,0:T(8,128)(2,1)}), bf16[32,32,128]{2,1,0:T(8,128)(2,1)S(1)}, u32[]{:S(2)}, u32[]{:S(2)}) %all-to-all-start) | async-done | bytes 262176 | tf_op jit(solution)/shard_map/all_to_all | solution.py:427
  22.2 0.0 copy-done.4
  22.2 5.7 %layer.1 = (f32[1,32,4,16,128]{4,3,2,1,0:T(8,128)}, bf16[4,32,8,128]{3,2,1,0:T(8,128)(2,1)S(1)}) custom-call(bf16[32,32,128]{2,1,0:T(8,128)(2,1)S(1)} %all-to-all-done.parts_ref, bf16[4,4,16,128]{3,2,1,0:T(8,128)(2,1)S(1)} %bitcast.10, bf16[4,16,128]{2,1,0:T(8,128)(2,1)S(1)} %collective-permute-done.near_ref, ...), custom_call_target="tpu_custom_call" | custom-call | flops 4000000000 | bytes 6000000 | tf_op jit(solution)/shard_map/layer/pallas_call | solution.py:445
  27.9 18.2 %all_to_all.10.recv_ref = bf16[128,8,128]{2,1,0:T(8,128)(2,1)S(1)} all-to-all(bf16[128,8,128]{2,1,0:T(8,128)(2,1)S(1)} %bitcast.11), channel_id=1, replica_groups=mesh['rep'=4,'gx'=8,'gy'=4] {'rep','gx','gy'}, dimensions={0} | all-to-all | bytes 524288 | tf_op jit(solution)/shard_map/all_to_all | solution.py:467
  46.1 1.0 %finish.1 = (f32[1,8,864]{2,1,0:T(8,128)}, f32[1,8,32]{2,1,0:T(8,128)}, f32[4,8]{1,0:T(4,128)}) custom-call(bf16[128,8,128]{2,1,0:T(8,128)(2,1)S(1)} %all_to_all.10.recv_ref, bf16[864,128]{1,0:T(8,128)(2,1)S(1)} %get-tuple-element.29.taps_ref, bf16[32,128]{1,0:T(8,128)(2,1)S(1)} %get-tuple-element.30.owned_ref), custom_call_target="tpu_custom_call" | custom-call | tf_op jit(solution)/shard_map/finish/pallas_call | solution.py:469
  (2 shorter events, 0.0 us)
Async XLA Ops:
  0.6 12.7 %copy-start = (bf16[1,4,4,16,128]{4,3,2,1,0:T(8,128)(2,1)S(1)}, bf16[1,4,4,16,128]{4,3,2,1,0:T(8,128)(2,1)}, u32[]{:S(2)}) copy-start(bf16[1,4,4,16,128]{4,3,2,1,0:T(8,128)(2,1)} %param.8) | copy-start | bytes 196612
  0.6 16.3 %copy-start.1 = (bf16[1,32,864]{2,1,0:T(8,128)(2,1)S(1)}, bf16[1,32,864]{2,1,0:T(8,128)(2,1)}, u32[]{:S(2)}) copy-start(bf16[1,32,864]{2,1,0:T(8,128)(2,1)} %conv_ref.1) | copy-start | bytes 165892
  0.7 16.3 %copy-start.2 = (bf16[1,32,32]{2,1,0:T(8,128)(2,1)S(1)}, bf16[1,32,32]{2,1,0:T(8,128)(2,1)}, u32[]{:S(2)}) copy-start(bf16[1,32,32]{2,1,0:T(8,128)(2,1)} %mix_ref.1) | copy-start | bytes 6148
  0.7 16.3 %copy-start.3 = (bf16[4,32]{1,0:T(4,128)(2,1)S(1)}, bf16[4,32]{1,0:T(4,128)(2,1)}, u32[]{:S(2)}) copy-start(bf16[4,32]{1,0:T(4,128)(2,1)} %lift_ref.1) | copy-start | bytes 772
  4.7 17.5 %copy-start.4 = (s32[8,768]{1,0:T(8,128)S(1)}, s32[8,768]{1,0:T(8,128)}, u32[]{:S(2)}) copy-start(s32[8,768]{1,0:T(8,128)} %constant.22.clone.codes_ref) | copy-start | bytes 73732
  4.7 17.5 %all-to-all-start = ((bf16[32,32,128]{2,1,0:T(8,128)(2,1)}), bf16[32,32,128]{2,1,0:T(8,128)(2,1)S(1)}, u32[]{:S(2)}, u32[]{:S(2)}) async-start(bf16[32,32,128]{2,1,0:T(8,128)(2,1)} %get-tuple-element.19), calls=%async_computation | async-start | bytes 524288 | tf_op jit(solution)/shard_map/all_to_all | solution.py:427
  13.3 5.5 %collective-permute-start.1 = (bf16[4,16,128]{2,1,0:T(8,128)(2,1)S(1)}, bf16[4,16,128]{2,1,0:T(8,128)(2,1)S(1)}, u32[]{:S(2)}, u32[]{:S(2)}) collective-permute-start(bf16[4,16,128]{2,1,0:T(8,128)(2,1)S(1)} %get-tuple-element.34), channel_id=1, source_target_pairs={{4,8},{8,4},{12,16},{16,12},{20,24},{24,20},{5,9},{9,5},{13,17},{1... | collective-permute-start | bytes 49160 | tf_op jit(solution)/shard_map/ppermute | solution.py:407
  16.9 1.9 %collective-permute-start = (bf16[4,16,128]{2,1,0:T(8,128)(2,1)S(1)}, bf16[4,16,128]{2,1,0:T(8,128)(2,1)S(1)}, u32[]{:S(2)}, u32[]{:S(2)}) collective-permute-start(bf16[4,16,128]{2,1,0:T(8,128)(2,1)S(1)} %get-tuple-element.35), channel_id=1, source_target_pairs={{0,4},{4,0},{8,12},{12,8},{16,20},{20,16},{24,28},{28,24},{1,5},{5... | collective-permute-start | bytes 49160 | tf_op jit(solution)/shard_map/ppermute | solution.py:406

commit v6 on v5

--- a/solution.py
+++ b/solution.py
@@ -74,6 +74,17 @@
 
 def ones_where(condition):
     return jnp.where(condition, 1.0, 0.0).astype(BF16)
+
+
+def row_sums(tiles):
+    rows = iota((8, 128), 0)
+    for step in (1, 2, 4):
+        first = (rows & step) == 0
+        tiles = [
+            jnp.where(first, a, b) + pltpu.roll(jnp.where(first, b, a), 8 - step, 0)
+            for a, b in zip(tiles[0::2], tiles[1::2])
+        ]
+    return tiles[0]
 
 
 def selector(codes, dy):
@@ -177,14 +188,19 @@
             [basis_ref[at : at + count, x].reshape(wide, 128) for x in range(4)], axis=1
         )
         product = dot(fields, basis, NT)
-        same = iota((16, wide), 0) == (iota((16, wide), 1) & 15)
-        for j in range(4):
-            line = jnp.sum(
-                jnp.where(same, product[16 * j : 16 * j + 16], 0.0), axis=0, keepdims=True
-            )
-            for chunk in range(count // 8):
-                row = at // 8 + chunk
-                sums[j, row : row + 1, :] = line[:, 128 * chunk : 128 * chunk + 128]
+        same = iota((16, 128), 0) == (iota((16, 128), 1) & 15)
+        for chunk in range(0, count // 8, 4):
+            row = at // 8 + chunk
+            for pair in (0, 2):
+                tiles = []
+                for j in (pair, pair + 1):
+                    for one in range(chunk, chunk + 4):
+                        block = product[16 * j : 16 * j + 16, 128 * one : 128 * one + 128]
+                        block = jnp.where(same, block, 0.0)
+                        tiles.append(block[:8] + block[8:])
+                packed = row_sums(tiles)
+                sums[pair, row : row + 4, :] = packed[:4]
+                sums[pair + 1, row : row + 4, :] = packed[4:]
     groups = ones_where(iota((8, 128), 0) == (iota((8, 128), 1) >> 4))
     first_part, rest = split(sums[...].reshape(128, 128))
     total = dot(groups, first_part, NT) + dot(groups, rest, NT)
@@ -325,15 +341,21 @@
             corr[...] = product
         else:
             corr[...] += product
-    bands = [band(codes, dy) for dy in range(3)]
     moments = jnp.zeros((32, TAPROWS), F32)
-    reduced = [[], [], []]
-    for o in range(32):
-        block = corr[16 * o : 16 * o + 16, :]
-        for dy in range(3):
-            reduced[dy].append(jnp.sum(jnp.where(bands[dy], block, 0.0), axis=0, keepdims=True))
     for dy in range(3):
-        moments = moments + dot_split(jnp.concatenate(reduced[dy], axis=0), selector(codes, dy), NT)
+        valid = band(codes, dy)
+        reduced = []
+        for first in range(0, 32, 8):
+            pieces = []
+            for at in range(0, STACK, 128):
+                lanes = slice(at, at + 128)
+                tiles = []
+                for o in range(first, first + 8):
+                    block = jnp.where(valid[:, lanes], corr[16 * o : 16 * o + 16, lanes], 0.0)
+                    tiles.append(block[:8] + block[8:])
+                pieces.append(row_sums(tiles))
+            reduced.append(jnp.concatenate(pieces, axis=1))
+        moments = moments + dot_split(jnp.concatenate(reduced, axis=0), selector(codes, dy), NT)
     turned_high, turned_low = split(moments.T)
     turned = jnp.concatenate([turned_high, turned_low], axis=1)
     products = dot(turned, pairs_ref[...])

time: 47.5 us -> 47.3 us (level)
  no operation moved by 1% of the time
where the time goes in v6:
time: 47.3 us; the launch traced here: 46.9 us
  blocking collectives  18.2 us (38%)
  starting transfers between devices  12.2 us (26%)
  Pallas kernels  10.9 us (23%)
  waiting for transfers between devices  4.75 us (10%)
  between operations  0.78 us (2%)
    all_to_all x1, blocking collectives, on_device(): lax.all_to_all(send.reshape(reps * gx * gy, 8, 128), ('rep', 'gx', 'gy'),...  18.2 us
    all_to_all x1, starting transfers between devices, on_device(): gathered = lax.all_to_all(parts, ('gx', 'gy'), 0, 0)  8.6 us
    pallas_call x1, Pallas kernels, on_device(): pl.pallas_call(main_kernel, in_specs=[VMEM] * (7 + EARLY) + [HBM] * 2, ou...  5.53 us
    pallas_call x1, Pallas kernels, on_device(): pl.pallas_call(functools.partial(project_kernel, rows), in_specs=[HBM] *...  3.98 us
    ppermute x1, starting transfers between devices, on_device(): far = lax.ppermute(jnp.where(even, first, last), 'gx', off_chip)  3.54 us
    all_to_all x1, waiting for transfers between devices, on_device(): gathered = lax.all_to_all(parts, ('gx', 'gy'), 0, 0)  3.35 us
    ppermute x1, waiting for transfers between devices, on_device(): far = lax.ppermute(jnp.where(even, first, last), 'gx', off_chip)  1.4 us
    pallas_call x1, Pallas kernels, on_device(): pl.pallas_call(functools.partial(finish_kernel, scale, inv), in_specs=[VM...  1.03 us
  transfers between devices with their start and end apart: 3, of which 2 were waited for; matrix products, arithmetic and copies ran while one was open for 0% of the time, Pallas kernels for 1%

profile of v6, /device:TPU:1, one launch (start us, length us, event | category | flops | bytes accessed | tf_op | source)
XLA Modules:
  0.0 46.9 jit_solution(16936385865529513656)
XLA Ops:
  0.6 0.0 copy-start
  0.6 0.0 copy-start.1
  0.7 0.0 copy-start.2
  0.7 0.0 copy-start.3
  0.7 4.0 %project.1 = (bf16[32,32,128]{2,1,0:T(8,128)(2,1)}, bf16[32,4,16,128]{3,2,1,0:T(8,128)(2,1)S(1)}, bf16[32,4,16,128]{3,2,1,0:T(8,128)(2,1)S(1)}, bf16[32,4,16,128...) custom-call(bf16[4,4,16,128]{3,2,1,0:T(8,128)(2,1)} %bitcast.9, ...), custom_call_target="tpu_custom_call" | custom-call | tf_op jit(solution)/shard_map/project/pallas_call | solution.py:432
  4.7 0.0 copy-start.4
  4.7 8.6 %all-to-all-start = ((bf16[32,32,128]{2,1,0:T(8,128)(2,1)}), bf16[32,32,128]{2,1,0:T(8,128)(2,1)S(1)}, u32[]{:S(2)}, u32[]{:S(2)}) async-start(bf16[32,32,128]{2,1,0:T(8,128)(2,1)} %get-tuple-element.19), calls=%async_computation | async-start | bytes 524288 | tf_op jit(solution)/shard_map/all_to_all | solution.py:449
  13.3 0.0 copy-done
  13.3 3.5 %collective-permute-start.1 = (bf16[4,16,128]{2,1,0:T(8,128)(2,1)S(1)}, bf16[4,16,128]{2,1,0:T(8,128)(2,1)S(1)}, u32[]{:S(2)}, u32[]{:S(2)}) collective-permute-start(bf16[4,16,128]{2,1,0:T(8,128)(2,1)S(1)} %get-tuple-element.34), channel_id=1, source_target_pairs={{4,8},{8,4},{12,16},{16,12},{20,24},{24,20},{5,9},{9,5},{13,17},{1... | collective-permute-start | bytes 49160 | tf_op jit(solution)/shard_map/ppermute | solution.py:429
  16.9 0.1 collective-permute-start
  17.0 0.0 copy-done.1
  17.0 0.0 copy-done.2
  17.0 0.0 copy-done.3
  17.0 0.4 stage.1
  17.4 1.4 %collective-permute-done.1.far_ref = bf16[4,16,128]{2,1,0:T(8,128)(2,1)S(1)} collective-permute-done((bf16[4,16,128]{2,1,0:T(8,128)(2,1)S(1)}, bf16[4,16,128]{2,1,0:T(8,128)(2,1)S(1)}, u32[]{:S(2)}, u32[]{:S(2)}) %collective-permute-start.1) | collective-permute-done | bytes 16416 | tf_op jit(solution)/shard_map/ppermute | solution.py:429
  18.8 0.0 collective-permute-done.near_ref
  18.8 3.3 %all-to-all-done.parts_ref = bf16[32,32,128]{2,1,0:T(8,128)(2,1)S(1)} async-done(((bf16[32,32,128]{2,1,0:T(8,128)(2,1)}), bf16[32,32,128]{2,1,0:T(8,128)(2,1)S(1)}, u32[]{:S(2)}, u32[]{:S(2)}) %all-to-all-start) | async-done | bytes 262176 | tf_op jit(solution)/shard_map/all_to_all | solution.py:449
  22.2 0.0 copy-done.4
  22.2 5.5 %layer.1 = (f32[1,32,4,16,128]{4,3,2,1,0:T(8,128)}, bf16[4,32,8,128]{3,2,1,0:T(8,128)(2,1)S(1)}) custom-call(bf16[32,32,128]{2,1,0:T(8,128)(2,1)S(1)} %all-to-all-done.parts_ref, bf16[4,4,16,128]{3,2,1,0:T(8,128)(2,1)S(1)} %bitcast.10, bf16[4,16,128]{2,1,0:T(8,128)(2,1)S(1)} %collective-permute-done.near_ref, ...), custom_call_target="tpu_custom_call" | custom-call | flops 4000000000 | bytes 6000000 | tf_op jit(solution)/shard_map/layer/pallas_call | solution.py:467
  27.7 18.2 %all_to_all.10.recv_ref = bf16[128,8,128]{2,1,0:T(8,128)(2,1)S(1)} all-to-all(bf16[128,8,128]{2,1,0:T(8,128)(2,1)S(1)} %bitcast.11), channel_id=1, replica_groups=mesh['rep'=4,'gx'=8,'gy'=4] {'rep','gx','gy'}, dimensions={0} | all-to-all | bytes 524288 | tf_op jit(solution)/shard_map/all_to_all | solution.py:489
  45.9 1.0 %finish.1 = (f32[1,8,864]{2,1,0:T(8,128)}, f32[1,8,32]{2,1,0:T(8,128)}, f32[4,8]{1,0:T(4,128)}) custom-call(bf16[128,8,128]{2,1,0:T(8,128)(2,1)S(1)} %all_to_all.10.recv_ref, bf16[864,128]{1,0:T(8,128)(2,1)S(1)} %get-tuple-element.29.taps_ref, bf16[32,128]{1,0:T(8,128)(2,1)S(1)} %get-tuple-element.30.owned_ref), custom_call_target="tpu_custom_call" | custom-call | tf_op jit(solution)/shard_map/finish/pallas_call | solution.py:491
  (2 shorter events, 0.0 us)
Async XLA Ops:
  0.6 12.7 %copy-start = (bf16[1,4,4,16,128]{4,3,2,1,0:T(8,128)(2,1)S(1)}, bf16[1,4,4,16,128]{4,3,2,1,0:T(8,128)(2,1)}, u32[]{:S(2)}) copy-start(bf16[1,4,4,16,128]{4,3,2,1,0:T(8,128)(2,1)} %param.8) | copy-start | bytes 196612
  0.6 16.3 %copy-start.1 = (bf16[1,32,864]{2,1,0:T(8,128)(2,1)S(1)}, bf16[1,32,864]{2,1,0:T(8,128)(2,1)}, u32[]{:S(2)}) copy-start(bf16[1,32,864]{2,1,0:T(8,128)(2,1)} %conv_ref.1) | copy-start | bytes 165892
  0.7 16.3 %copy-start.2 = (bf16[1,32,32]{2,1,0:T(8,128)(2,1)S(1)}, bf16[1,32,32]{2,1,0:T(8,128)(2,1)}, u32[]{:S(2)}) copy-start(bf16[1,32,32]{2,1,0:T(8,128)(2,1)} %mix_ref.1) | copy-start | bytes 6148
  0.7 16.3 %copy-start.3 = (bf16[4,32]{1,0:T(4,128)(2,1)S(1)}, bf16[4,32]{1,0:T(4,128)(2,1)}, u32[]{:S(2)}) copy-start(bf16[4,32]{1,0:T(4,128)(2,1)} %lift_ref.1) | copy-start | bytes 772
  4.7 17.5 %copy-start.4 = (s32[8,768]{1,0:T(8,128)S(1)}, s32[8,768]{1,0:T(8,128)}, u32[]{:S(2)}) copy-start(s32[8,768]{1,0:T(8,128)} %constant.22.clone.codes_ref) | copy-start | bytes 73732
  4.7 17.5 %all-to-all-start = ((bf16[32,32,128]{2,1,0:T(8,128)(2,1)}), bf16[32,32,128]{2,1,0:T(8,128)(2,1)S(1)}, u32[]{:S(2)}, u32[]{:S(2)}) async-start(bf16[32,32,128]{2,1,0:T(8,128)(2,1)} %get-tuple-element.19), calls=%async_computation | async-start | bytes 524288 | tf_op jit(solution)/shard_map/all_to_all | solution.py:449
  13.3 5.5 %collective-permute-start.1 = (bf16[4,16,128]{2,1,0:T(8,128)(2,1)S(1)}, bf16[4,16,128]{2,1,0:T(8,128)(2,1)S(1)}, u32[]{:S(2)}, u32[]{:S(2)}) collective-permute-start(bf16[4,16,128]{2,1,0:T(8,128)(2,1)S(1)} %get-tuple-element.34), channel_id=1, source_target_pairs={{4,8},{8,4},{12,16},{16,12},{20,24},{24,20},{5,9},{9,5},{13,17},{1... | collective-permute-start | bytes 49160 | tf_op jit(solution)/shard_map/ppermute | solution.py:429
  16.9 1.9 %collective-permute-start = (bf16[4,16,128]{2,1,0:T(8,128)(2,1)S(1)}, bf16[4,16,128]{2,1,0:T(8,128)(2,1)S(1)}, u32[]{:S(2)}, u32[]{:S(2)}) collective-permute-start(bf16[4,16,128]{2,1,0:T(8,128)(2,1)S(1)} %get-tuple-element.35), channel_id=1, source_target_pairs={{0,4},{4,0},{8,12},{12,8},{16,20},{20,16},{24,28},{28,24},{1,5},{5... | collective-permute-start | bytes 49160 | tf_op jit(solution)/shard_map/ppermute | solution.py:428

commit v7 on v6

--- a/solution.py
+++ b/solution.py
@@ -266,7 +266,7 @@
         )
         psi_refs.append(piece)
     cot_copy = pltpu.make_async_copy(cot_ref, cot, sems.at[late])
-    for item in copies + [cot_copy]:
+    for item in copies:
         item.start()
     codes = codes_ref[...]
     weight_table(weights_ref[...], codes, table)
@@ -288,6 +288,7 @@
     stack[HALO_AT:U_AT, :] = jnp.concatenate(
         [rim_block, jnp.zeros((U_AT - HALO_AT - 72, 512), F32)], axis=0
     ).astype(BF16)
+    cot_copy.start()
     both = jnp.sum(parts_ref[:, 0:16, :].astype(F32), axis=0)
     high, low = split(both[:8] + both[8:])
     groups = ones_where(iota((8, 128), 0) == (iota((8, 128), 1) >> 4))
@@ -341,7 +342,7 @@
             corr[...] = product
         else:
             corr[...] += product
-    moments = jnp.zeros((32, TAPROWS), F32)
+    bands = []
     for dy in range(3):
         valid = band(codes, dy)
         reduced = []
@@ -355,7 +356,12 @@
                     tiles.append(block[:8] + block[8:])
                 pieces.append(row_sums(tiles))
             reduced.append(jnp.concatenate(pieces, axis=1))
-        moments = moments + dot_split(jnp.concatenate(reduced, axis=0), selector(codes, dy), NT)
+        bands.append(jnp.concatenate(reduced, axis=0))
+    banded = jnp.concatenate(bands, axis=1)
+    picks = jnp.concatenate([selector(codes, dy) for dy in range(3)], axis=1)
+    high, low = split(banded)
+    both = dot(jnp.concatenate([high, low], axis=0), picks, NT)
+    moments = both[:32] + both[32:]
     turned_high, turned_low = split(moments.T)
     turned = jnp.concatenate([turned_high, turned_low], axis=1)
     products = dot(turned, pairs_ref[...])

time: 47.3 us -> 47 us (level)
  no operation moved by 1% of the time
where the time goes in v7:
time: 47 us; the launch traced here: 46.7 us
  blocking collectives  18.2 us (39%)
  starting transfers between devices  12.2 us (26%)
  Pallas kernels  10.7 us (23%)
  waiting for transfers between devices  4.75 us (10%)
  between operations  0.78 us (2%)
    all_to_all x1, blocking collectives, on_device(): lax.all_to_all(send.reshape(reps * gx * gy, 8, 128), ('rep', 'gx', 'gy'),...  18.2 us
    all_to_all x1, starting transfers between devices, on_device(): gathered = lax.all_to_all(parts, ('gx', 'gy'), 0, 0)  8.6 us
    pallas_call x1, Pallas kernels, on_device(): pl.pallas_call(main_kernel, in_specs=[VMEM] * (7 + EARLY) + [HBM] * 2, ou...  5.25 us
    pallas_call x1, Pallas kernels, on_device(): pl.pallas_call(functools.partial(project_kernel, rows), in_specs=[HBM] *...  3.98 us
    ppermute x1, starting transfers between devices, on_device(): far = lax.ppermute(jnp.where(even, first, last), 'gx', off_chip)  3.54 us
    all_to_all x1, waiting for transfers between devices, on_device(): gathered = lax.all_to_all(parts, ('gx', 'gy'), 0, 0)  3.35 us
    ppermute x1, waiting for transfers between devices, on_device(): far = lax.ppermute(jnp.where(even, first, last), 'gx', off_chip)  1.4 us
    pallas_call x1, Pallas kernels, on_device(): pl.pallas_call(functools.partial(finish_kernel, scale, inv), in_specs=[VM...  1.03 us
  transfers between devices with their start and end apart: 3, of which 2 were waited for; matrix products, arithmetic and copies ran while one was open for 0% of the time, Pallas kernels for 1%

profile of v7, /device:TPU:1, one launch (start us, length us, event | category | flops | bytes accessed | tf_op | source)
XLA Modules:
  0.0 46.7 jit_solution(14201041192851870602)
XLA Ops:
  0.6 0.0 copy-start
  0.6 0.0 copy-start.1
  0.7 0.0 copy-start.2
  0.7 0.0 copy-start.3
  0.7 4.0 %project.1 = (bf16[32,32,128]{2,1,0:T(8,128)(2,1)}, bf16[32,4,16,128]{3,2,1,0:T(8,128)(2,1)S(1)}, bf16[32,4,16,128]{3,2,1,0:T(8,128)(2,1)S(1)}, bf16[32,4,16,128...) custom-call(bf16[4,4,16,128]{3,2,1,0:T(8,128)(2,1)} %bitcast.9, ...), custom_call_target="tpu_custom_call" | custom-call | tf_op jit(solution)/shard_map/project/pallas_call | solution.py:438
  4.7 0.0 copy-start.4
  4.7 8.6 %all-to-all-start = ((bf16[32,32,128]{2,1,0:T(8,128)(2,1)}), bf16[32,32,128]{2,1,0:T(8,128)(2,1)S(1)}, u32[]{:S(2)}, u32[]{:S(2)}) async-start(bf16[32,32,128]{2,1,0:T(8,128)(2,1)} %get-tuple-element.19), calls=%async_computation | async-start | bytes 524288 | tf_op jit(solution)/shard_map/all_to_all | solution.py:455
  13.3 0.0 copy-done
  13.3 3.5 %collective-permute-start.1 = (bf16[4,16,128]{2,1,0:T(8,128)(2,1)S(1)}, bf16[4,16,128]{2,1,0:T(8,128)(2,1)S(1)}, u32[]{:S(2)}, u32[]{:S(2)}) collective-permute-start(bf16[4,16,128]{2,1,0:T(8,128)(2,1)S(1)} %get-tuple-element.34), channel_id=1, source_target_pairs={{4,8},{8,4},{12,16},{16,12},{20,24},{24,20},{5,9},{9,5},{13,17},{1... | collective-permute-start | bytes 49160 | tf_op jit(solution)/shard_map/ppermute | solution.py:435
  16.9 0.1 collective-permute-start
  17.0 0.0 copy-done.1
  17.0 0.0 copy-done.2
  17.0 0.0 copy-done.3
  17.0 0.4 stage.1
  17.4 1.4 %collective-permute-done.1.far_ref = bf16[4,16,128]{2,1,0:T(8,128)(2,1)S(1)} collective-permute-done((bf16[4,16,128]{2,1,0:T(8,128)(2,1)S(1)}, bf16[4,16,128]{2,1,0:T(8,128)(2,1)S(1)}, u32[]{:S(2)}, u32[]{:S(2)}) %collective-permute-start.1) | collective-permute-done | bytes 16416 | tf_op jit(solution)/shard_map/ppermute | solution.py:435
  18.8 0.0 collective-permute-done.near_ref
  18.8 3.3 %all-to-all-done.parts_ref = bf16[32,32,128]{2,1,0:T(8,128)(2,1)S(1)} async-done(((bf16[32,32,128]{2,1,0:T(8,128)(2,1)}), bf16[32,32,128]{2,1,0:T(8,128)(2,1)S(1)}, u32[]{:S(2)}, u32[]{:S(2)}) %all-to-all-start) | async-done | bytes 262176 | tf_op jit(solution)/shard_map/all_to_all | solution.py:455
  22.2 0.0 copy-done.4
  22.2 5.2 %layer.1 = (f32[1,32,4,16,128]{4,3,2,1,0:T(8,128)}, bf16[4,32,8,128]{3,2,1,0:T(8,128)(2,1)S(1)}) custom-call(bf16[32,32,128]{2,1,0:T(8,128)(2,1)S(1)} %all-to-all-done.parts_ref, bf16[4,4,16,128]{3,2,1,0:T(8,128)(2,1)S(1)} %bitcast.10, bf16[4,16,128]{2,1,0:T(8,128)(2,1)S(1)} %collective-permute-done.near_ref, ...), custom_call_target="tpu_custom_call" | custom-call | flops 4000000000 | bytes 6000000 | tf_op jit(solution)/shard_map/layer/pallas_call | solution.py:473
  27.4 18.2 %all_to_all.10.recv_ref = bf16[128,8,128]{2,1,0:T(8,128)(2,1)S(1)} all-to-all(bf16[128,8,128]{2,1,0:T(8,128)(2,1)S(1)} %bitcast.11), channel_id=1, replica_groups=mesh['rep'=4,'gx'=8,'gy'=4] {'rep','gx','gy'}, dimensions={0} | all-to-all | bytes 524288 | tf_op jit(solution)/shard_map/all_to_all | solution.py:495
  45.6 1.0 %finish.1 = (f32[1,8,864]{2,1,0:T(8,128)}, f32[1,8,32]{2,1,0:T(8,128)}, f32[4,8]{1,0:T(4,128)}) custom-call(bf16[128,8,128]{2,1,0:T(8,128)(2,1)S(1)} %all_to_all.10.recv_ref, bf16[864,128]{1,0:T(8,128)(2,1)S(1)} %get-tuple-element.29.taps_ref, bf16[32,128]{1,0:T(8,128)(2,1)S(1)} %get-tuple-element.30.owned_ref), custom_call_target="tpu_custom_call" | custom-call | tf_op jit(solution)/shard_map/finish/pallas_call | solution.py:497
  (2 shorter events, 0.0 us)
Async XLA Ops:
  0.6 12.7 %copy-start = (bf16[1,4,4,16,128]{4,3,2,1,0:T(8,128)(2,1)S(1)}, bf16[1,4,4,16,128]{4,3,2,1,0:T(8,128)(2,1)}, u32[]{:S(2)}) copy-start(bf16[1,4,4,16,128]{4,3,2,1,0:T(8,128)(2,1)} %param.8) | copy-start | bytes 196612
  0.6 16.3 %copy-start.1 = (bf16[1,32,864]{2,1,0:T(8,128)(2,1)S(1)}, bf16[1,32,864]{2,1,0:T(8,128)(2,1)}, u32[]{:S(2)}) copy-start(bf16[1,32,864]{2,1,0:T(8,128)(2,1)} %conv_ref.1) | copy-start | bytes 165892
  0.7 16.3 %copy-start.2 = (bf16[1,32,32]{2,1,0:T(8,128)(2,1)S(1)}, bf16[1,32,32]{2,1,0:T(8,128)(2,1)}, u32[]{:S(2)}) copy-start(bf16[1,32,32]{2,1,0:T(8,128)(2,1)} %mix_ref.1) | copy-start | bytes 6148
  0.7 16.3 %copy-start.3 = (bf16[4,32]{1,0:T(4,128)(2,1)S(1)}, bf16[4,32]{1,0:T(4,128)(2,1)}, u32[]{:S(2)}) copy-start(bf16[4,32]{1,0:T(4,128)(2,1)} %lift_ref.1) | copy-start | bytes 772
  4.7 17.5 %copy-start.4 = (s32[8,768]{1,0:T(8,128)S(1)}, s32[8,768]{1,0:T(8,128)}, u32[]{:S(2)}) copy-start(s32[8,768]{1,0:T(8,128)} %constant.22.clone.codes_ref) | copy-start | bytes 73732
  4.7 17.5 %all-to-all-start = ((bf16[32,32,128]{2,1,0:T(8,128)(2,1)}), bf16[32,32,128]{2,1,0:T(8,128)(2,1)S(1)}, u32[]{:S(2)}, u32[]{:S(2)}) async-start(bf16[32,32,128]{2,1,0:T(8,128)(2,1)} %get-tuple-element.19), calls=%async_computation | async-start | bytes 524288 | tf_op jit(solution)/shard_map/all_to_all | solution.py:455
  13.3 5.5 %collective-permute-start.1 = (bf16[4,16,128]{2,1,0:T(8,128)(2,1)S(1)}, bf16[4,16,128]{2,1,0:T(8,128)(2,1)S(1)}, u32[]{:S(2)}, u32[]{:S(2)}) collective-permute-start(bf16[4,16,128]{2,1,0:T(8,128)(2,1)S(1)} %get-tuple-element.34), channel_id=1, source_target_pairs={{4,8},{8,4},{12,16},{16,12},{20,24},{24,20},{5,9},{9,5},{13,17},{1... | collective-permute-start | bytes 49160 | tf_op jit(solution)/shard_map/ppermute | solution.py:435
  16.9 1.9 %collective-permute-start = (bf16[4,16,128]{2,1,0:T(8,128)(2,1)S(1)}, bf16[4,16,128]{2,1,0:T(8,128)(2,1)S(1)}, u32[]{:S(2)}, u32[]{:S(2)}) collective-permute-start(bf16[4,16,128]{2,1,0:T(8,128)(2,1)S(1)} %get-tuple-element.35), channel_id=1, source_target_pairs={{0,4},{4,0},{8,12},{12,8},{16,20},{20,16},{24,28},{28,24},{1,5},{5... | collective-permute-start | bytes 49160 | tf_op jit(solution)/shard_map/ppermute | solution.py:434

commit v8 on v7

--- a/solution.py
+++ b/solution.py
@@ -292,16 +292,16 @@
     both = jnp.sum(parts_ref[:, 0:16, :].astype(F32), axis=0)
     high, low = split(both[:8] + both[8:])
     groups = ones_where(iota((8, 128), 0) == (iota((8, 128), 1) >> 4))
-    same = iota((16, 128), 0) == (iota((16, 128), 1) & 15)
+    same = ones_where(iota((16, 128), 0) == (iota((16, 128), 1) & 15))
     for part, values in enumerate((high, low)):
         expanded = dot(values, groups, TN)
         for j in range(4):
             for chunk in range(32):
                 row = expanded[32 * j + chunk : 32 * j + chunk + 1, :]
                 at = 64 * part + 16 * j
-                spread[at : at + 16, 128 * chunk : 128 * chunk + 128] = jnp.where(
-                    same, row, 0.0
-                ).astype(BF16)
+                spread[at : at + 16, 128 * chunk : 128 * chunk + 128] = (
+                    jnp.broadcast_to(row, (16, 128)).astype(BF16) * same
+                )
     fields = [jnp.zeros((128, 256), F32) for _ in range(2)]
     for k, piece in enumerate(psi_refs):
         if k == EARLY:
@@ -434,7 +434,7 @@
     near = lax.ppermute(jnp.where(even, last, first), "gx", on_chip)
     far = lax.ppermute(jnp.where(even, first, last), "gx", off_chip)
 
-    rows = (rank // 4, 3 * rank // 8, 3 * rank // 8)
+    rows = (rank // 4,) * 4
     parts, *pieces = pl.pallas_call(
         functools.partial(project_kernel, rows),
         in_specs=[HBM] * 3,

time: 47 us -> 47 us (level)
  no operation moved by 1% of the time
where the time goes in v8:
time: 47 us; the launch traced here: 46.7 us
  blocking collectives  18.2 us (39%)
  starting transfers between devices  12.2 us (26%)
  Pallas kernels  10.7 us (23%)
  waiting for transfers between devices  4.75 us (10%)
  between operations  0.78 us (2%)
    all_to_all x1, blocking collectives, on_device(): lax.all_to_all(send.reshape(reps * gx * gy, 8, 128), ('rep', 'gx', 'gy'),...  18.2 us
    all_to_all x1, starting transfers between devices, on_device(): gathered = lax.all_to_all(parts, ('gx', 'gy'), 0, 0)  8.6 us
    pallas_call x1, Pallas kernels, on_device(): pl.pallas_call(main_kernel, in_specs=[VMEM] * (7 + EARLY) + [HBM] * 2, ou...  5.17 us
    pallas_call x1, Pallas kernels, on_device(): pl.pallas_call(functools.partial(project_kernel, rows), in_specs=[HBM] *...  4.08 us
    ppermute x1, starting transfers between devices, on_device(): far = lax.ppermute(jnp.where(even, first, last), 'gx', off_chip)  3.54 us
    all_to_all x1, waiting for transfers between devices, on_device(): gathered = lax.all_to_all(parts, ('gx', 'gy'), 0, 0)  3.35 us
    ppermute x1, waiting for transfers between devices, on_device(): far = lax.ppermute(jnp.where(even, first, last), 'gx', off_chip)  1.4 us
    pallas_call x1, Pallas kernels, on_device(): pl.pallas_call(functools.partial(finish_kernel, scale, inv), in_specs=[VM...  1.03 us
  transfers between devices with their start and end apart: 3, of which 2 were waited for; matrix products, arithmetic and copies ran while one was open for 0% of the time, Pallas kernels for 1%

profile of v8, /device:TPU:1, one launch (start us, length us, event | category | flops | bytes accessed | tf_op | source)
XLA Modules:
  0.0 46.7 jit_solution(7741767453250548391)
XLA Ops:
  0.6 0.0 copy-start
  0.6 0.0 copy-start.1
  0.7 0.0 copy-start.2
  0.7 0.0 copy-start.3
  0.7 4.1 %project.1 = (bf16[32,32,128]{2,1,0:T(8,128)(2,1)}, bf16[32,4,16,128]{3,2,1,0:T(8,128)(2,1)S(1)}, bf16[32,4,16,128]{3,2,1,0:T(8,128)(2,1)S(1)}, bf16[32,4,16,128...) custom-call(bf16[4,4,16,128]{3,2,1,0:T(8,128)(2,1)} %bitcast.9, ...), custom_call_target="tpu_custom_call" | custom-call | tf_op jit(solution)/shard_map/project/pallas_call | solution.py:438
  4.8 0.0 copy-start.4
  4.8 8.6 %all-to-all-start = ((bf16[32,32,128]{2,1,0:T(8,128)(2,1)}), bf16[32,32,128]{2,1,0:T(8,128)(2,1)S(1)}, u32[]{:S(2)}, u32[]{:S(2)}) async-start(bf16[32,32,128]{2,1,0:T(8,128)(2,1)} %get-tuple-element.19), calls=%async_computation | async-start | bytes 524288 | tf_op jit(solution)/shard_map/all_to_all | solution.py:455
  13.4 0.0 copy-done
  13.4 3.5 %collective-permute-start.1 = (bf16[4,16,128]{2,1,0:T(8,128)(2,1)S(1)}, bf16[4,16,128]{2,1,0:T(8,128)(2,1)S(1)}, u32[]{:S(2)}, u32[]{:S(2)}) collective-permute-start(bf16[4,16,128]{2,1,0:T(8,128)(2,1)S(1)} %get-tuple-element.34), channel_id=1, source_target_pairs={{4,8},{8,4},{12,16},{16,12},{20,24},{24,20},{5,9},{9,5},{13,17},{1... | collective-permute-start | bytes 49160 | tf_op jit(solution)/shard_map/ppermute | solution.py:435
  17.0 0.1 collective-permute-start
  17.1 0.0 copy-done.1
  17.1 0.0 copy-done.2
  17.1 0.0 copy-done.3
  17.1 0.4 stage.1
  17.5 1.4 %collective-permute-done.1.far_ref = bf16[4,16,128]{2,1,0:T(8,128)(2,1)S(1)} collective-permute-done((bf16[4,16,128]{2,1,0:T(8,128)(2,1)S(1)}, bf16[4,16,128]{2,1,0:T(8,128)(2,1)S(1)}, u32[]{:S(2)}, u32[]{:S(2)}) %collective-permute-start.1) | collective-permute-done | bytes 16416 | tf_op jit(solution)/shard_map/ppermute | solution.py:435
  18.9 0.0 collective-permute-done.near_ref
  18.9 3.3 %all-to-all-done.parts_ref = bf16[32,32,128]{2,1,0:T(8,128)(2,1)S(1)} async-done(((bf16[32,32,128]{2,1,0:T(8,128)(2,1)}), bf16[32,32,128]{2,1,0:T(8,128)(2,1)S(1)}, u32[]{:S(2)}, u32[]{:S(2)}) %all-to-all-start) | async-done | bytes 262176 | tf_op jit(solution)/shard_map/all_to_all | solution.py:455
  22.3 0.0 copy-done.4
  22.3 5.2 %layer.1 = (f32[1,32,4,16,128]{4,3,2,1,0:T(8,128)}, bf16[4,32,8,128]{3,2,1,0:T(8,128)(2,1)S(1)}) custom-call(bf16[32,32,128]{2,1,0:T(8,128)(2,1)S(1)} %all-to-all-done.parts_ref, bf16[4,4,16,128]{3,2,1,0:T(8,128)(2,1)S(1)} %bitcast.10, bf16[4,16,128]{2,1,0:T(8,128)(2,1)S(1)} %collective-permute-done.near_ref, ...), custom_call_target="tpu_custom_call" | custom-call | flops 4000000000 | bytes 6000000 | tf_op jit(solution)/shard_map/layer/pallas_call | solution.py:473
  27.5 18.2 %all_to_all.10.recv_ref = bf16[128,8,128]{2,1,0:T(8,128)(2,1)S(1)} all-to-all(bf16[128,8,128]{2,1,0:T(8,128)(2,1)S(1)} %bitcast.11), channel_id=1, replica_groups=mesh['rep'=4,'gx'=8,'gy'=4] {'rep','gx','gy'}, dimensions={0} | all-to-all | bytes 524288 | tf_op jit(solution)/shard_map/all_to_all | solution.py:495
  45.6 1.0 %finish.1 = (f32[1,8,864]{2,1,0:T(8,128)}, f32[1,8,32]{2,1,0:T(8,128)}, f32[4,8]{1,0:T(4,128)}) custom-call(bf16[128,8,128]{2,1,0:T(8,128)(2,1)S(1)} %all_to_all.10.recv_ref, bf16[864,128]{1,0:T(8,128)(2,1)S(1)} %get-tuple-element.29.taps_ref, bf16[32,128]{1,0:T(8,128)(2,1)S(1)} %get-tuple-element.30.owned_ref), custom_call_target="tpu_custom_call" | custom-call | tf_op jit(solution)/shard_map/finish/pallas_call | solution.py:497
  (2 shorter events, 0.0 us)
Async XLA Ops:
  0.6 12.8 %copy-start = (bf16[1,4,4,16,128]{4,3,2,1,0:T(8,128)(2,1)S(1)}, bf16[1,4,4,16,128]{4,3,2,1,0:T(8,128)(2,1)}, u32[]{:S(2)}) copy-start(bf16[1,4,4,16,128]{4,3,2,1,0:T(8,128)(2,1)} %param.8) | copy-start | bytes 196612
  0.6 16.4 %copy-start.1 = (bf16[1,32,864]{2,1,0:T(8,128)(2,1)S(1)}, bf16[1,32,864]{2,1,0:T(8,128)(2,1)}, u32[]{:S(2)}) copy-start(bf16[1,32,864]{2,1,0:T(8,128)(2,1)} %conv_ref.1) | copy-start | bytes 165892
  0.7 16.4 %copy-start.2 = (bf16[1,32,32]{2,1,0:T(8,128)(2,1)S(1)}, bf16[1,32,32]{2,1,0:T(8,128)(2,1)}, u32[]{:S(2)}) copy-start(bf16[1,32,32]{2,1,0:T(8,128)(2,1)} %mix_ref.1) | copy-start | bytes 6148
  0.7 16.4 %copy-start.3 = (bf16[4,32]{1,0:T(4,128)(2,1)S(1)}, bf16[4,32]{1,0:T(4,128)(2,1)}, u32[]{:S(2)}) copy-start(bf16[4,32]{1,0:T(4,128)(2,1)} %lift_ref.1) | copy-start | bytes 772
  4.8 17.5 %copy-start.4 = (s32[8,768]{1,0:T(8,128)S(1)}, s32[8,768]{1,0:T(8,128)}, u32[]{:S(2)}) copy-start(s32[8,768]{1,0:T(8,128)} %constant.22.clone.codes_ref) | copy-start | bytes 73732
  4.8 17.5 %all-to-all-start = ((bf16[32,32,128]{2,1,0:T(8,128)(2,1)}), bf16[32,32,128]{2,1,0:T(8,128)(2,1)S(1)}, u32[]{:S(2)}, u32[]{:S(2)}) async-start(bf16[32,32,128]{2,1,0:T(8,128)(2,1)} %get-tuple-element.19), calls=%async_computation | async-start | bytes 524288 | tf_op jit(solution)/shard_map/all_to_all | solution.py:455
  13.4 5.5 %collective-permute-start.1 = (bf16[4,16,128]{2,1,0:T(8,128)(2,1)S(1)}, bf16[4,16,128]{2,1,0:T(8,128)(2,1)S(1)}, u32[]{:S(2)}, u32[]{:S(2)}) collective-permute-start(bf16[4,16,128]{2,1,0:T(8,128)(2,1)S(1)} %get-tuple-element.34), channel_id=1, source_target_pairs={{4,8},{8,4},{12,16},{16,12},{20,24},{24,20},{5,9},{9,5},{13,17},{1... | collective-permute-start | bytes 49160 | tf_op jit(solution)/shard_map/ppermute | solution.py:435
  17.0 1.9 %collective-permute-start = (bf16[4,16,128]{2,1,0:T(8,128)(2,1)S(1)}, bf16[4,16,128]{2,1,0:T(8,128)(2,1)S(1)}, u32[]{:S(2)}, u32[]{:S(2)}) collective-permute-start(bf16[4,16,128]{2,1,0:T(8,128)(2,1)S(1)} %get-tuple-element.35), channel_id=1, source_target_pairs={{0,4},{4,0},{8,12},{12,8},{16,20},{20,16},{24,28},{28,24},{1,5},{5... | collective-permute-start | bytes 49160 | tf_op jit(solution)/shard_map/ppermute | solution.py:434

commit v9 on v7

--- a/solution.py
+++ b/solution.py
@@ -304,9 +304,8 @@
                 ).astype(BF16)
     fields = [jnp.zeros((128, 256), F32) for _ in range(2)]
     for k, piece in enumerate(psi_refs):
-        if k == EARLY:
-            for item in copies:
-                item.wait()
+        if k >= EARLY:
+            copies[k - EARLY].wait()
         for pair in range(2):
             for row in range(0, count, 16):
                 at = k * count + row
@@ -316,11 +315,12 @@
                 fields[pair] = fields[pair] + dot(spread[:, 16 * at : 16 * at + 256], basis)
     for pair, field in enumerate(fields):
         stack[U_AT:STACK, 256 * pair : 256 * pair + 256] = (field[:64] + field[64:]).astype(BF16)
-    cot_copy.wait()
     out_copies = []
     for pair in range(2):
         half = slice(256 * pair, 256 * pair + 256)
         pre[:, half] = dot(table[...], stack[:, half])
+        if pair == 0:
+            cot_copy.wait()
         for o in range(32):
             rows = slice(16 * o, 16 * o + 16)
             for x in (2 * pair, 2 * pair + 1):

time: 47 us -> 46.7 us (level)
  no operation moved by 1% of the time
where the time goes in v9:
time: 46.7 us; the launch traced here: 46.4 us
  blocking collectives  18.2 us (39%)
  starting transfers between devices  12.2 us (26%)
  Pallas kernels  10.4 us (22%)
  waiting for transfers between devices  4.75 us (10%)
  between operations  0.78 us (2%)
    all_to_all x1, blocking collectives, on_device(): lax.all_to_all(send.reshape(reps * gx * gy, 8, 128), ('rep', 'gx', 'gy'),...  18.2 us
    all_to_all x1, starting transfers between devices, on_device(): gathered = lax.all_to_all(parts, ('gx', 'gy'), 0, 0)  8.6 us
    pallas_call x1, Pallas kernels, on_device(): pl.pallas_call(main_kernel, in_specs=[VMEM] * (7 + EARLY) + [HBM] * 2, ou...  4.98 us
    pallas_call x1, Pallas kernels, on_device(): pl.pallas_call(functools.partial(project_kernel, rows), in_specs=[HBM] *...  3.98 us
    ppermute x1, starting transfers between devices, on_device(): far = lax.ppermute(jnp.where(even, first, last), 'gx', off_chip)  3.54 us
    all_to_all x1, waiting for transfers between devices, on_device(): gathered = lax.all_to_all(parts, ('gx', 'gy'), 0, 0)  3.35 us
    ppermute x1, waiting for transfers between devices, on_device(): far = lax.ppermute(jnp.where(even, first, last), 'gx', off_chip)  1.4 us
    pallas_call x1, Pallas kernels, on_device(): pl.pallas_call(functools.partial(finish_kernel, scale, inv), in_specs=[VM...  1.03 us
  transfers between devices with their start and end apart: 3, of which 2 were waited for; matrix products, arithmetic and copies ran while one was open for 0% of the time, Pallas kernels for 1%

profile of v9, /device:TPU:1, one launch (start us, length us, event | category | flops | bytes accessed | tf_op | source)
XLA Modules:
  0.0 46.4 jit_solution(11616984242432800183)
XLA Ops:
  0.6 0.0 copy-start
  0.6 0.0 copy-start.1
  0.7 0.0 copy-start.2
  0.7 0.0 copy-start.3
  0.7 4.0 %project.1 = (bf16[32,32,128]{2,1,0:T(8,128)(2,1)}, bf16[32,4,16,128]{3,2,1,0:T(8,128)(2,1)S(1)}, bf16[32,4,16,128]{3,2,1,0:T(8,128)(2,1)S(1)}, bf16[32,4,16,128...) custom-call(bf16[4,4,16,128]{3,2,1,0:T(8,128)(2,1)} %bitcast.9, ...), custom_call_target="tpu_custom_call" | custom-call | tf_op jit(solution)/shard_map/project/pallas_call | solution.py:438
  4.7 0.0 copy-start.4
  4.7 8.6 %all-to-all-start = ((bf16[32,32,128]{2,1,0:T(8,128)(2,1)}), bf16[32,32,128]{2,1,0:T(8,128)(2,1)S(1)}, u32[]{:S(2)}, u32[]{:S(2)}) async-start(bf16[32,32,128]{2,1,0:T(8,128)(2,1)} %get-tuple-element.19), calls=%async_computation | async-start | bytes 524288 | tf_op jit(solution)/shard_map/all_to_all | solution.py:455
  13.3 0.0 copy-done
  13.3 3.5 %collective-permute-start.1 = (bf16[4,16,128]{2,1,0:T(8,128)(2,1)S(1)}, bf16[4,16,128]{2,1,0:T(8,128)(2,1)S(1)}, u32[]{:S(2)}, u32[]{:S(2)}) collective-permute-start(bf16[4,16,128]{2,1,0:T(8,128)(2,1)S(1)} %get-tuple-element.34), channel_id=1, source_target_pairs={{4,8},{8,4},{12,16},{16,12},{20,24},{24,20},{5,9},{9,5},{13,17},{1... | collective-permute-start | bytes 49160 | tf_op jit(solution)/shard_map/ppermute | solution.py:435
  16.9 0.1 collective-permute-start
  17.0 0.0 copy-done.1
  17.0 0.0 copy-done.2
  17.0 0.0 copy-done.3
  17.0 0.4 stage.1
  17.4 1.4 %collective-permute-done.1.far_ref = bf16[4,16,128]{2,1,0:T(8,128)(2,1)S(1)} collective-permute-done((bf16[4,16,128]{2,1,0:T(8,128)(2,1)S(1)}, bf16[4,16,128]{2,1,0:T(8,128)(2,1)S(1)}, u32[]{:S(2)}, u32[]{:S(2)}) %collective-permute-start.1) | collective-permute-done | bytes 16416 | tf_op jit(solution)/shard_map/ppermute | solution.py:435
  18.8 0.0 collective-permute-done.near_ref
  18.8 3.3 %all-to-all-done.parts_ref = bf16[32,32,128]{2,1,0:T(8,128)(2,1)S(1)} async-done(((bf16[32,32,128]{2,1,0:T(8,128)(2,1)}), bf16[32,32,128]{2,1,0:T(8,128)(2,1)S(1)}, u32[]{:S(2)}, u32[]{:S(2)}) %all-to-all-start) | async-done | bytes 262176 | tf_op jit(solution)/shard_map/all_to_all | solution.py:455
  22.2 0.0 copy-done.4
  22.2 5.0 %layer.1 = (f32[1,32,4,16,128]{4,3,2,1,0:T(8,128)}, bf16[4,32,8,128]{3,2,1,0:T(8,128)(2,1)S(1)}) custom-call(bf16[32,32,128]{2,1,0:T(8,128)(2,1)S(1)} %all-to-all-done.parts_ref, bf16[4,4,16,128]{3,2,1,0:T(8,128)(2,1)S(1)} %bitcast.10, bf16[4,16,128]{2,1,0:T(8,128)(2,1)S(1)} %collective-permute-done.near_ref, ...), custom_call_target="tpu_custom_call" | custom-call | flops 4000000000 | bytes 6000000 | tf_op jit(solution)/shard_map/layer/pallas_call | solution.py:473
  27.2 18.2 %all_to_all.10.recv_ref = bf16[128,8,128]{2,1,0:T(8,128)(2,1)S(1)} all-to-all(bf16[128,8,128]{2,1,0:T(8,128)(2,1)S(1)} %bitcast.11), channel_id=1, replica_groups=mesh['rep'=4,'gx'=8,'gy'=4] {'rep','gx','gy'}, dimensions={0} | all-to-all | bytes 524288 | tf_op jit(solution)/shard_map/all_to_all | solution.py:495
  45.4 1.0 %finish.1 = (f32[1,8,864]{2,1,0:T(8,128)}, f32[1,8,32]{2,1,0:T(8,128)}, f32[4,8]{1,0:T(4,128)}) custom-call(bf16[128,8,128]{2,1,0:T(8,128)(2,1)S(1)} %all_to_all.10.recv_ref, bf16[864,128]{1,0:T(8,128)(2,1)S(1)} %get-tuple-element.29.taps_ref, bf16[32,128]{1,0:T(8,128)(2,1)S(1)} %get-tuple-element.30.owned_ref), custom_call_target="tpu_custom_call" | custom-call | tf_op jit(solution)/shard_map/finish/pallas_call | solution.py:497
  (2 shorter events, 0.0 us)
Async XLA Ops:
  0.6 12.7 %copy-start = (bf16[1,4,4,16,128]{4,3,2,1,0:T(8,128)(2,1)S(1)}, bf16[1,4,4,16,128]{4,3,2,1,0:T(8,128)(2,1)}, u32[]{:S(2)}) copy-start(bf16[1,4,4,16,128]{4,3,2,1,0:T(8,128)(2,1)} %param.8) | copy-start | bytes 196612
  0.6 16.3 %copy-start.1 = (bf16[1,32,864]{2,1,0:T(8,128)(2,1)S(1)}, bf16[1,32,864]{2,1,0:T(8,128)(2,1)}, u32[]{:S(2)}) copy-start(bf16[1,32,864]{2,1,0:T(8,128)(2,1)} %conv_ref.1) | copy-start | bytes 165892
  0.7 16.3 %copy-start.2 = (bf16[1,32,32]{2,1,0:T(8,128)(2,1)S(1)}, bf16[1,32,32]{2,1,0:T(8,128)(2,1)}, u32[]{:S(2)}) copy-start(bf16[1,32,32]{2,1,0:T(8,128)(2,1)} %mix_ref.1) | copy-start | bytes 6148
  0.7 16.3 %copy-start.3 = (bf16[4,32]{1,0:T(4,128)(2,1)S(1)}, bf16[4,32]{1,0:T(4,128)(2,1)}, u32[]{:S(2)}) copy-start(bf16[4,32]{1,0:T(4,128)(2,1)} %lift_ref.1) | copy-start | bytes 772
  4.7 17.5 %copy-start.4 = (s32[8,768]{1,0:T(8,128)S(1)}, s32[8,768]{1,0:T(8,128)}, u32[]{:S(2)}) copy-start(s32[8,768]{1,0:T(8,128)} %constant.22.clone.codes_ref) | copy-start | bytes 73732
  4.7 17.5 %all-to-all-start = ((bf16[32,32,128]{2,1,0:T(8,128)(2,1)}), bf16[32,32,128]{2,1,0:T(8,128)(2,1)S(1)}, u32[]{:S(2)}, u32[]{:S(2)}) async-start(bf16[32,32,128]{2,1,0:T(8,128)(2,1)} %get-tuple-element.19), calls=%async_computation | async-start | bytes 524288 | tf_op jit(solution)/shard_map/all_to_all | solution.py:455
  13.3 5.5 %collective-permute-start.1 = (bf16[4,16,128]{2,1,0:T(8,128)(2,1)S(1)}, bf16[4,16,128]{2,1,0:T(8,128)(2,1)S(1)}, u32[]{:S(2)}, u32[]{:S(2)}) collective-permute-start(bf16[4,16,128]{2,1,0:T(8,128)(2,1)S(1)} %get-tuple-element.34), channel_id=1, source_target_pairs={{4,8},{8,4},{12,16},{16,12},{20,24},{24,20},{5,9},{9,5},{13,17},{1... | collective-permute-start | bytes 49160 | tf_op jit(solution)/shard_map/ppermute | solution.py:435
  16.9 1.9 %collective-permute-start = (bf16[4,16,128]{2,1,0:T(8,128)(2,1)S(1)}, bf16[4,16,128]{2,1,0:T(8,128)(2,1)S(1)}, u32[]{:S(2)}, u32[]{:S(2)}) collective-permute-start(bf16[4,16,128]{2,1,0:T(8,128)(2,1)S(1)} %get-tuple-element.35), channel_id=1, source_target_pairs={{0,4},{4,0},{8,12},{12,8},{16,20},{20,16},{24,28},{28,24},{1,5},{5... | collective-permute-start | bytes 49160 | tf_op jit(solution)/shard_map/ppermute | solution.py:434
